TPU v7x, 32 devices: a whole 2x2x4 slice. The times are simulated.
32 devices in a mesh: river: 4 (over y, core), coast: 8 (over z, x).
Axes of the slice: x: 2, y: 2, z: 4, core: 2. Of those that a mesh axis runs over, the one named last changes fastest.
Arguments:
- reach_depth: float32 [2048, 128], P(('river', 'coast')), may hold values from 0.02 to 4
- reach_flow: float32 [2048, 128], P(('river', 'coast')), may hold values from -3 to 3
- reach_bed: float32 [2048, 128], P(('river', 'coast')), may hold values from 0 to 1
- reach_width: float32 [2048, 128], P(('river', 'coast')), may hold values from 200 to 800
- reach_length: float32 [2048, 128], P(('river', 'coast')), may hold values from 4000 to 12000
- runoff: float32 [2048, 128], P(('river', 'coast')), may hold values from 1 to 100
- flows_into: int32 [2048, 128], P(('river', 'coast')), may hold values from 1 to 128, as said below
- mouth_prev: float32 [2048, 32], P(('river', 'coast')), may hold values from -1.5 to 1.5
- mouth_tile: int32 [2048, 32, 1], P(('river', 'coast')), may hold values from 0 to 31; in each aligned block of 2048 rows (0 to 2047, 2048 to 4095, ..., all dimensions but the last counted through in order) at most 128 rows name the same one
- mouth_cell: int32 [2048, 32], P(('river', 'coast')), may hold values from 0 to 4095
- sea_level: float32 [128, 1024], P('river', 'coast'), may hold values from -1.2 to 1.2
- sea_bed: float32 [128, 1024], P('river', 'coast'), may hold values from -4 to 0.5
- wet_mask: int32 [128, 1024], P('river', 'coast'), may hold values 0 or 1
- flux_east: float32 [128, 1024], P('river', 'coast'), may hold values from -3 to 3
- flux_north: float32 [128, 1024], P('river', 'coast'), may hold values from -3 to 3
Outputs:
- depth_after: float32 [2048, 128], P(('river', 'coast'))
- level_after: float32 [128, 1024], P('river', 'coast')
- mouth_level: float32 [2048, 384], P(('river', 'coast'))
Inputs may be any that keep to these rules, and one draw needn't show every extreme that they name: `flows_into`: in every block the last 32 reaches have the value 128 (they flow to the sea); every other reach i names a reach of the same block with index i + 1 to i + 16. `mouth_tile`: among the mouths of one device (the rows of one device, in order), no tile is named more than 128 times, a bound that some block reaches; every tile is named by some mouth.
All inputs are finite; a program needn't handle non-finite values. No bound on the sum of `wet_mask` on one device may be relied on, other than what follows from the above.
Results may differ from a plain program's by a relative error of at most 0.0002.
Values sent between devices are 32-bit elements; how exact they have to be, the bound alone decides.
No kernel may reach another device: no remote copies, remote signals or barrier semaphores. Data moves between devices by JAX's collectives and lax.ppermute only.
A program may use at most 64 MiB of HBM per device.

v0:
```python
import jax
import jax.numpy as jnp
from jax import lax
from jax.sharding import PartitionSpec as P

RB = 128
MPB = 32
STEPS = 12


gravity = 9.81
step_seconds = 300.0
cell_metres = 3000.0
river_manning = 0.035
ocean_manning = 0.025
depth_floor = 0.05
reach_offsets = 16


def padded_2(shard, sides, width):
    for axis, dim in sides:
        size, length = (lax.axis_size(axis), shard.shape[dim])
        up = [(i, (i + 1) % size) for i in range(size - 1)]
        down = [(j, i) for i, j in up]
        last = lax.slice_in_dim(shard, length - width, length, axis=dim)
        leading = lax.slice_in_dim(shard, 0, width, axis=dim)
        before = lax.ppermute(last, axis, up)
        after = lax.ppermute(leading, axis, down)
        shard = jnp.concatenate([before, shard, after], axis=dim)
    return shard


def from_behind(block, axis, distance):
    devices = range(lax.axis_size(axis))
    route = [(i - distance, i) for i in devices if i - distance in devices]
    return lax.ppermute(block, axis, route)


def inertial(unit_flow, upper_level, lower_level, bed_upper, bed_lower, distance, manning):
    face_depth = jnp.maximum(upper_level, lower_level) - jnp.maximum(bed_upper, bed_lower)
    driving = (
        gravity
        * step_seconds
        * jnp.maximum(face_depth, 0.0)
        * (upper_level - lower_level)
        / distance
    )
    friction = (
        gravity
        * step_seconds
        * manning
        * manning
        * jnp.abs(unit_flow)
        / jnp.power(jnp.maximum(face_depth, depth_floor), 7.0 / 3.0)
    )
    return (unit_flow + driving) / (1.0 + friction)


def look_down(values, offset_masks):
    blocks = values.shape[0]
    inland = offset_masks[0].shape[1]
    padded = jnp.concatenate([values, jnp.zeros((blocks, reach_offsets), jnp.float32)], axis=1)
    found = jnp.zeros((blocks, inland), jnp.float32)
    for offset in range(1, reach_offsets + 1):
        found = found + jnp.where(
            offset_masks[offset - 1], padded[:, offset : offset + inland], 0.0
        )
    return found


def gather_inflow(discharge_inland, offset_masks):
    blocks, inland = discharge_inland.shape
    total = jnp.zeros((blocks, RB + reach_offsets), jnp.float32)
    for offset in range(1, reach_offsets + 1):
        moved = jnp.where(offset_masks[offset - 1], discharge_inland, 0.0)
        placed = jnp.concatenate(
            [
                jnp.zeros((blocks, offset), jnp.float32),
                moved,
                jnp.zeros((blocks, RB + reach_offsets - offset - inland), jnp.float32),
            ],
            axis=1,
        )
        total = total + placed
    return total[:, :RB]


def river_step(
    water_depth,
    unit_flow,
    reach_bed,
    reach_width,
    reach_length,
    runoff,
    offset_masks,
    bed_down,
    mouth_prev,
):
    inland = RB - MPB
    surface = reach_bed + water_depth
    below = jnp.concatenate([look_down(surface, offset_masks), mouth_prev], axis=1)
    unit_flow = inertial(
        unit_flow, surface, below, reach_bed, bed_down, reach_length, river_manning
    )
    discharge = unit_flow * reach_width
    inflow = gather_inflow(discharge[:, :inland], offset_masks)
    water_depth = water_depth + step_seconds * (inflow + runoff - discharge) / (
        reach_width * reach_length
    )
    return (water_depth, unit_flow, discharge[:, inland:])


def per_device(
    reach_depth,
    reach_flow,
    reach_bed,
    reach_width,
    reach_length,
    runoff,
    flows_into,
    mouth_prev,
    mouth_tile,
    mouth_cell,
    sea_level,
    sea_bed,
    wet_mask,
    flux_east,
    flux_north,
):
    river_count = lax.axis_size("river")
    coast_count = lax.axis_size("coast")
    devices = river_count * coast_count
    blocks = reach_depth.shape[0]
    tile_rows, tile_cols = sea_level.shape
    mouths = blocks * MPB
    capacity = max(2, 2 * blocks * MPB // devices)
    inland = RB - MPB
    down_index = flows_into[:, :inland]
    position = jnp.arange(inland, dtype=jnp.int32)[None, :]
    offset_masks = [down_index == position + offset for offset in range(1, reach_offsets + 1)]
    bed_down = jnp.concatenate([look_down(reach_bed, offset_masks), reach_bed[:, inland:]], axis=1)
    target = mouth_tile.reshape(mouths)
    sorter = jnp.argsort(target, stable=True)
    sorted_tiles = target[sorter]
    first_index = jnp.searchsorted(sorted_tiles, sorted_tiles, side="left")
    ranked = jnp.arange(mouths, dtype=jnp.int32) - first_index
    slot_index = jnp.zeros((mouths,), jnp.int32).at[sorter].set(ranked)
    cell_index = mouth_cell.reshape(mouths)
    water_level = jnp.where(wet_mask == 1, jnp.maximum(sea_level, sea_bed), sea_bed)
    bed_padded = padded_2(sea_bed, (("river", 0), ("coast", 1)), 1)
    west_row = from_behind(flux_east[tile_rows - 1 :, :], "river", 1)
    south_edge = from_behind(flux_north[:, tile_cols - 1 :], "coast", 1)
    east_faces = jnp.concatenate([west_row, flux_east], axis=0)

    def river_turn(substep, carry):
        water_depth, unit_flow, series = carry
        water_depth, unit_flow, mouth_flow = river_step(
            water_depth,
            unit_flow,
            reach_bed,
            reach_width,
            reach_length,
            runoff,
            offset_masks,
            bed_down,
            mouth_prev,
        )
        series = lax.dynamic_update_slice_in_dim(series, mouth_flow.reshape(1, mouths), substep, 0)
        return (water_depth, unit_flow, series)

    start_series = jnp.zeros((STEPS, mouths), jnp.float32)
    water_depth, unit_flow, series = lax.fori_loop(
        0, STEPS, river_turn, (reach_depth, reach_flow, start_series)
    )
    sending = (
        jnp.zeros((devices, STEPS, capacity), jnp.float32).at[target, :, slot_index].set(series.T)
    )
    labels = jnp.zeros((devices, capacity), jnp.int32).at[target, slot_index].set(cell_index)
    arrived, arrived_cells = (
        lax.all_to_all(
            sending.reshape(devices, STEPS * capacity),
            ("river", "coast"),
            split_axis=0,
            concat_axis=0,
            tiled=True,
        ),
        lax.all_to_all(labels, ("river", "coast"), split_axis=0, concat_axis=0, tiled=True),
    )
    arrived = arrived.reshape(devices, STEPS, capacity)
    flat_cells = arrived_cells.reshape(devices * capacity)
    cell_rows = flat_cells // tile_cols
    cell_cols = flat_cells % tile_cols
    row_hits = (cell_rows[:, None] == jnp.arange(tile_rows, dtype=jnp.int32)[None, :]).astype(
        jnp.float32
    )
    col_hits = (cell_cols[:, None] == jnp.arange(tile_cols, dtype=jnp.int32)[None, :]).astype(
        jnp.float32
    )
    incoming_all = jnp.transpose(arrived, (1, 0, 2)).reshape(STEPS, devices * capacity)
    weighted = incoming_all[:, :, None] * col_hits[None, :, :]
    sources = jnp.einsum("mr,kmc->krc", row_hits, weighted, precision=lax.Precision.HIGHEST)

    def ocean_turn(substep, carry):
        level_now, east_now, north_now, edge_now, replies = carry
        source = lax.dynamic_index_in_dim(sources, substep, 0, keepdims=False)
        padded = padded_2(level_now, (("river", 0), ("coast", 1)), 1)
        east_now = inertial(
            east_now,
            padded[:-1, 1:-1],
            padded[1:, 1:-1],
            bed_padded[:-1, 1:-1],
            bed_padded[1:, 1:-1],
            cell_metres,
            ocean_manning,
        )
        north_now = inertial(
            north_now,
            padded[1:-1, 1:-1],
            padded[1:-1, 2:],
            bed_padded[1:-1, 1:-1],
            bed_padded[1:-1, 2:],
            cell_metres,
            ocean_manning,
        )
        edge_now = inertial(
            edge_now,
            padded[1:-1, 0:1],
            padded[1:-1, 1:2],
            bed_padded[1:-1, 0:1],
            bed_padded[1:-1, 1:2],
            cell_metres,
            ocean_manning,
        )
        north_lower = jnp.concatenate([edge_now, north_now[:, :-1]], axis=1)
        spread = east_now[1:] - east_now[:-1] + north_now - north_lower
        level_now = (
            level_now
            - step_seconds / cell_metres * spread
            + step_seconds / (cell_metres * cell_metres) * source
        )
        picked = level_now.reshape(tile_rows * tile_cols)[flat_cells].reshape(devices, 1, capacity)
        replies = lax.dynamic_update_slice_in_dim(replies, picked, substep, 1)
        return (level_now, east_now, north_now, edge_now, replies)

    start_replies = jnp.zeros((devices, STEPS, capacity), jnp.float32)
    water_level, east_faces, north_faces, south_edge, replies = lax.fori_loop(
        0, STEPS, ocean_turn, (water_level, east_faces, flux_north, south_edge, start_replies)
    )
    returned = lax.all_to_all(
        replies.reshape(devices, STEPS * capacity),
        ("river", "coast"),
        split_axis=0,
        concat_axis=0,
        tiled=True,
    )
    returned = returned.reshape(devices, STEPS, capacity)
    tile_grid = target.reshape(blocks, 1, MPB)
    slot_grid = slot_index.reshape(blocks, 1, MPB)
    step_grid = jnp.arange(STEPS, dtype=jnp.int32).reshape(1, STEPS, 1)
    mouth_level = returned[tile_grid, step_grid, slot_grid].reshape(blocks, STEPS * MPB)
    return (water_depth, water_level, mouth_level)


def solution(mesh):
    placed = (
        P(("river", "coast"), None),
        P(("river", "coast"), None),
        P(("river", "coast"), None),
        P(("river", "coast"), None),
        P(("river", "coast"), None),
        P(("river", "coast"), None),
        P(("river", "coast"), None),
        P(("river", "coast"), None),
        P(("river", "coast"), None, None),
        P(("river", "coast"), None),
        P("river", "coast"),
        P("river", "coast"),
        P("river", "coast"),
        P("river", "coast"),
        P("river", "coast"),
    )
    return jax.shard_map(
        per_device,
        mesh=mesh,
        in_specs=placed,
        out_specs=(P(("river", "coast"), None), P("river", "coast"), P(("river", "coast"), None)),
        check_vma=False,
    )
```

profile of v0, /device:TPU:1, one launch (start us, length us, event | category | flops | bytes accessed | tf_op | source)
XLA Modules:
  0.0 959.1 jit_solution(13715357433802049873)
XLA Ops:
  7.4 11.8 %gather_fusion.2 = s32[2048]{0:T(1024)S(1)} fusion(s32[2048]{0:T(1024)S(1)} %reshape.313, s32[2048]{0:T(1024)S(1)} %get-tuple-element.1280), kind=kCustom, calls=%fused_computation.2 | custom fusion | bytes 24576 | tf_op jit(solution)/shard_map/gather | solution.py:144
  19.3 142.4 %while.70 = (s32[]{:T(128)}, u32[2048]{0:T(1024)S(1)}, u32[2048]{0:T(1024)S(1)}, s32[2048]{0:T(1024)S(1)}, s32[]{:T(128)}, /*index=5*/s32[]{:T(128)}, s32[]{}) while((s32[]{:T(128)}, u32[2048]{0:T(1024)S(1)}, u32[2048]{0:T(1024)S(1)}, s32[2048]{0:T(1024)S(1)}, s32[]{:T(128)}, /*index=5*/s32[]{:T(128)}, s32[]{}) %tuple.186), condition=%wide.region_4.5_spmd.clone, body=%wide.region_3.4_spmd.clone.sunk | while | flops 38916 | bytes 135269 | solution.py:145
  19.3 11.8 %gather_fusion.1 = s32[2048]{0:T(1024)S(1)} fusion(s32[2048]{0:T(1024)S(1)} %get-tuple-element.1735, u32[2048]{0:T(1024)S(1)} %broadcast_clamp_fusion.6), kind=kCustom, calls=%fused_computation.clone.clone.1 | custom fusion | bytes 24576 | tf_op jit(solution)/shard_map/jit(searchsorted)/jit(_searchsorted_scan_impl)/vmap(jit(_searchsorted_scan_impl))/while/body/eval_jaxpr/gather | solution.py:145
  31.2 11.8 %gather_fusion.1 = s32[2048]{0:T(1024)S(1)} fusion(s32[2048]{0:T(1024)S(1)} %get-tuple-element.1735, u32[2048]{0:T(1024)S(1)} %broadcast_clamp_fusion.6), kind=kCustom, calls=%fused_computation.clone.clone.1 | custom fusion | bytes 24576 | tf_op jit(solution)/shard_map/jit(searchsorted)/jit(_searchsorted_scan_impl)/vmap(jit(_searchsorted_scan_impl))/while/body/eval_jaxpr/gather | solution.py:145
  43.1 11.8 %gather_fusion.1 = s32[2048]{0:T(1024)S(1)} fusion(s32[2048]{0:T(1024)S(1)} %get-tuple-element.1735, u32[2048]{0:T(1024)S(1)} %broadcast_clamp_fusion.6), kind=kCustom, calls=%fused_computation.clone.clone.1 | custom fusion | bytes 24576 | tf_op jit(solution)/shard_map/jit(searchsorted)/jit(_searchsorted_scan_impl)/vmap(jit(_searchsorted_scan_impl))/while/body/eval_jaxpr/gather | solution.py:145
  54.9 11.8 %gather_fusion.1 = s32[2048]{0:T(1024)S(1)} fusion(s32[2048]{0:T(1024)S(1)} %get-tuple-element.1735, u32[2048]{0:T(1024)S(1)} %broadcast_clamp_fusion.6), kind=kCustom, calls=%fused_computation.clone.clone.1 | custom fusion | bytes 24576 | tf_op jit(solution)/shard_map/jit(searchsorted)/jit(_searchsorted_scan_impl)/vmap(jit(_searchsorted_scan_impl))/while/body/eval_jaxpr/gather | solution.py:145
  66.8 11.8 %gather_fusion.1 = s32[2048]{0:T(1024)S(1)} fusion(s32[2048]{0:T(1024)S(1)} %get-tuple-element.1735, u32[2048]{0:T(1024)S(1)} %broadcast_clamp_fusion.6), kind=kCustom, calls=%fused_computation.clone.clone.1 | custom fusion | bytes 24576 | tf_op jit(solution)/shard_map/jit(searchsorted)/jit(_searchsorted_scan_impl)/vmap(jit(_searchsorted_scan_impl))/while/body/eval_jaxpr/gather | solution.py:145
  78.7 11.8 %gather_fusion.1 = s32[2048]{0:T(1024)S(1)} fusion(s32[2048]{0:T(1024)S(1)} %get-tuple-element.1735, u32[2048]{0:T(1024)S(1)} %broadcast_clamp_fusion.6), kind=kCustom, calls=%fused_computation.clone.clone.1 | custom fusion | bytes 24576 | tf_op jit(solution)/shard_map/jit(searchsorted)/jit(_searchsorted_scan_impl)/vmap(jit(_searchsorted_scan_impl))/while/body/eval_jaxpr/gather | solution.py:145
  90.5 11.8 %gather_fusion.1 = s32[2048]{0:T(1024)S(1)} fusion(s32[2048]{0:T(1024)S(1)} %get-tuple-element.1735, u32[2048]{0:T(1024)S(1)} %broadcast_clamp_fusion.6), kind=kCustom, calls=%fused_computation.clone.clone.1 | custom fusion | bytes 24576 | tf_op jit(solution)/shard_map/jit(searchsorted)/jit(_searchsorted_scan_impl)/vmap(jit(_searchsorted_scan_impl))/while/body/eval_jaxpr/gather | solution.py:145
  102.4 11.8 %gather_fusion.1 = s32[2048]{0:T(1024)S(1)} fusion(s32[2048]{0:T(1024)S(1)} %get-tuple-element.1735, u32[2048]{0:T(1024)S(1)} %broadcast_clamp_fusion.6), kind=kCustom, calls=%fused_computation.clone.clone.1 | custom fusion | bytes 24576 | tf_op jit(solution)/shard_map/jit(searchsorted)/jit(_searchsorted_scan_impl)/vmap(jit(_searchsorted_scan_impl))/while/body/eval_jaxpr/gather | solution.py:145
  114.3 11.8 %gather_fusion.1 = s32[2048]{0:T(1024)S(1)} fusion(s32[2048]{0:T(1024)S(1)} %get-tuple-element.1735, u32[2048]{0:T(1024)S(1)} %broadcast_clamp_fusion.6), kind=kCustom, calls=%fused_computation.clone.clone.1 | custom fusion | bytes 24576 | tf_op jit(solution)/shard_map/jit(searchsorted)/jit(_searchsorted_scan_impl)/vmap(jit(_searchsorted_scan_impl))/while/body/eval_jaxpr/gather | solution.py:145
  126.1 11.8 %gather_fusion.1 = s32[2048]{0:T(1024)S(1)} fusion(s32[2048]{0:T(1024)S(1)} %get-tuple-element.1735, u32[2048]{0:T(1024)S(1)} %broadcast_clamp_fusion.6), kind=kCustom, calls=%fused_computation.clone.clone.1 | custom fusion | bytes 24576 | tf_op jit(solution)/shard_map/jit(searchsorted)/jit(_searchsorted_scan_impl)/vmap(jit(_searchsorted_scan_impl))/while/body/eval_jaxpr/gather | solution.py:145
  138.0 11.8 %gather_fusion.1 = s32[2048]{0:T(1024)S(1)} fusion(s32[2048]{0:T(1024)S(1)} %get-tuple-element.1735, u32[2048]{0:T(1024)S(1)} %broadcast_clamp_fusion.6), kind=kCustom, calls=%fused_computation.clone.clone.1 | custom fusion | bytes 24576 | tf_op jit(solution)/shard_map/jit(searchsorted)/jit(_searchsorted_scan_impl)/vmap(jit(_searchsorted_scan_impl))/while/body/eval_jaxpr/gather | solution.py:145
  149.9 11.8 %gather_fusion.1 = s32[2048]{0:T(1024)S(1)} fusion(s32[2048]{0:T(1024)S(1)} %get-tuple-element.1735, u32[2048]{0:T(1024)S(1)} %broadcast_clamp_fusion.6), kind=kCustom, calls=%fused_computation.clone.clone.1 | custom fusion | bytes 24576 | tf_op jit(solution)/shard_map/jit(searchsorted)/jit(_searchsorted_scan_impl)/vmap(jit(_searchsorted_scan_impl))/while/body/eval_jaxpr/gather | solution.py:145
  170.2 8.6 scatter_custom_fusion.2
  201.7 33.0 %while.68 = (s32[]{:T(128)}, f32[64,128]{1,0:T(8,128)S(1)}, f32[64,128]{1,0:T(8,128)S(1)}, f32[12,2048]{1,0:T(8,128)S(1)}, f32[64,128]{1,0:T(8,128)S(1)}, /*inde...) while((s32[]{:T(128)}, f32[64,128]{1,0:T(8,128)S(1)}, ...), condition=%wide.region_1.2_spmd, body=%wide.region_0.1_spmd.sunk | while | flops 886786 | bytes 2274661 | solution.py:172
  266.8 12.2 %fusion.47 = f32[12,32,128]{2,1,0:T(8,128)S(1)} fusion(f32[4096,128]{1,0:T(8,128)} %fusion.46, f32[12,4096]{1,0:T(8,128)S(1)} %bitcast.55, s32[4096]{0:T(1024)S(1)} %get-tuple-element.1274), kind=kOutput, calls=%fused_computation.123 | convolution fusion | flops 2422341632 | bytes 2506752 | tf_op jit(solution)/shard_map/mr,kmc->krc/dot_general | solution.py:201
  279.0 460.5 %while.69 = (s32[]{:T(128)}, f32[32,128]{1,0:T(8,128)S(1)}, f32[33,128]{1,0:T(8,128)S(1)}, f32[32,128]{1,0:T(8,128)S(1)}, f32[32,1]{1,0:T(8,128)S(1)}, /*index=5...) while((s32[]{:T(128)}, f32[32,128]{1,0:T(8,128)S(1)}, ...), condition=%wide.region_9.10_spmd, body=%wide.region_8.9_spmd.sunk | while | flops 191297 | bytes 474281 | solution.py:246
  291.8 23.0 %gather_fusion = f32[4096]{0:T(1024)S(1)} fusion(f32[4096]{0:T(1024)S(1)} %bitcast.44, s32[4096]{0:T(1024)S(1)} %broadcast_clamp_fusion.5), kind=kCustom, calls=%fused_computation.1.clone.1 | custom fusion | bytes 49152 | tf_op jit(solution)/shard_map/while/body/eval_jaxpr/gather | solution.py:241
  330.0 23.0 %gather_fusion = f32[4096]{0:T(1024)S(1)} fusion(f32[4096]{0:T(1024)S(1)} %bitcast.44, s32[4096]{0:T(1024)S(1)} %broadcast_clamp_fusion.5), kind=kCustom, calls=%fused_computation.1.clone.1 | custom fusion | bytes 49152 | tf_op jit(solution)/shard_map/while/body/eval_jaxpr/gather | solution.py:241
  368.7 23.0 %gather_fusion = f32[4096]{0:T(1024)S(1)} fusion(f32[4096]{0:T(1024)S(1)} %bitcast.44, s32[4096]{0:T(1024)S(1)} %broadcast_clamp_fusion.5), kind=kCustom, calls=%fused_computation.1.clone.1 | custom fusion | bytes 49152 | tf_op jit(solution)/shard_map/while/body/eval_jaxpr/gather | solution.py:241
  407.3 23.0 %gather_fusion = f32[4096]{0:T(1024)S(1)} fusion(f32[4096]{0:T(1024)S(1)} %bitcast.44, s32[4096]{0:T(1024)S(1)} %broadcast_clamp_fusion.5), kind=kCustom, calls=%fused_computation.1.clone.1 | custom fusion | bytes 49152 | tf_op jit(solution)/shard_map/while/body/eval_jaxpr/gather | solution.py:241
  446.0 23.0 %gather_fusion = f32[4096]{0:T(1024)S(1)} fusion(f32[4096]{0:T(1024)S(1)} %bitcast.44, s32[4096]{0:T(1024)S(1)} %broadcast_clamp_fusion.5), kind=kCustom, calls=%fused_computation.1.clone.1 | custom fusion | bytes 49152 | tf_op jit(solution)/shard_map/while/body/eval_jaxpr/gather | solution.py:241
  484.6 23.0 %gather_fusion = f32[4096]{0:T(1024)S(1)} fusion(f32[4096]{0:T(1024)S(1)} %bitcast.44, s32[4096]{0:T(1024)S(1)} %broadcast_clamp_fusion.5), kind=kCustom, calls=%fused_computation.1.clone.1 | custom fusion | bytes 49152 | tf_op jit(solution)/shard_map/while/body/eval_jaxpr/gather | solution.py:241
  523.3 23.0 %gather_fusion = f32[4096]{0:T(1024)S(1)} fusion(f32[4096]{0:T(1024)S(1)} %bitcast.44, s32[4096]{0:T(1024)S(1)} %broadcast_clamp_fusion.5), kind=kCustom, calls=%fused_computation.1.clone.1 | custom fusion | bytes 49152 | tf_op jit(solution)/shard_map/while/body/eval_jaxpr/gather | solution.py:241
  561.9 23.0 %gather_fusion = f32[4096]{0:T(1024)S(1)} fusion(f32[4096]{0:T(1024)S(1)} %bitcast.44, s32[4096]{0:T(1024)S(1)} %broadcast_clamp_fusion.5), kind=kCustom, calls=%fused_computation.1.clone.1 | custom fusion | bytes 49152 | tf_op jit(solution)/shard_map/while/body/eval_jaxpr/gather | solution.py:241
  600.5 23.0 %gather_fusion = f32[4096]{0:T(1024)S(1)} fusion(f32[4096]{0:T(1024)S(1)} %bitcast.44, s32[4096]{0:T(1024)S(1)} %broadcast_clamp_fusion.5), kind=kCustom, calls=%fused_computation.1.clone.1 | custom fusion | bytes 49152 | tf_op jit(solution)/shard_map/while/body/eval_jaxpr/gather | solution.py:241
  639.2 23.0 %gather_fusion = f32[4096]{0:T(1024)S(1)} fusion(f32[4096]{0:T(1024)S(1)} %bitcast.44, s32[4096]{0:T(1024)S(1)} %broadcast_clamp_fusion.5), kind=kCustom, calls=%fused_computation.1.clone.1 | custom fusion | bytes 49152 | tf_op jit(solution)/shard_map/while/body/eval_jaxpr/gather | solution.py:241
  677.8 23.0 %gather_fusion = f32[4096]{0:T(1024)S(1)} fusion(f32[4096]{0:T(1024)S(1)} %bitcast.44, s32[4096]{0:T(1024)S(1)} %broadcast_clamp_fusion.5), kind=kCustom, calls=%fused_computation.1.clone.1 | custom fusion | bytes 49152 | tf_op jit(solution)/shard_map/while/body/eval_jaxpr/gather | solution.py:241
  716.5 23.0 %gather_fusion = f32[4096]{0:T(1024)S(1)} fusion(f32[4096]{0:T(1024)S(1)} %bitcast.44, s32[4096]{0:T(1024)S(1)} %broadcast_clamp_fusion.5), kind=kCustom, calls=%fused_computation.1.clone.1 | custom fusion | bytes 49152 | tf_op jit(solution)/shard_map/while/body/eval_jaxpr/gather | solution.py:241
  740.5 12.5 %all-to-all-start.2 = ((f32[32,1,1536]{2,1,0:T(1,128)}), f32[32,1,1536]{2,1,0:T(1,128)S(1)}, u32[]{:S(2)}, u32[]{:S(2)}) async-start(f32[32,1,1536]{2,1,0:T(1,128)} %all_to_all.25), calls=%async_computation.2 | async-start | bytes 393216 | tf_op jit(solution)/shard_map/all_to_all | solution.py:249
  762.0 196.5 %gather_fusion.3 = f32[24576]{0:T(1024)S(1)} fusion(f32[32,12,128]{2,1,0:T(8,128)S(1)} %reshape.317, s32[24576]{0:T(1024)S(1)} %reshape.353), kind=kCustom, calls=%fused_computation.3 | custom fusion | bytes 491520 | tf_op jit(solution)/shard_map/gather | solution.py:260
  (1234 shorter events, 294.1 us)
Async XLA Ops:
  178.8 72.8 %all-to-all-start.1 = ((s32[32,1,128]{2,1,0:T(1,128)}), s32[32,1,128]{2,1,0:T(1,128)S(1)}, u32[]{:S(2)}, u32[]{:S(2)}) async-start(s32[32,1,128]{2,1,0:T(1,128)} %bitcast.10), calls=%async_computation.1 | async-start | bytes 32768 | tf_op jit(solution)/shard_map/all_to_all | solution.py:187
  186.5 57.0 %collective-permute-start.6 = (f32[1,128]{1,0:T(1,128)}, f32[1,128]{1,0:T(1,128)}, u32[]{:S(2)}, u32[]{:S(2)}) collective-permute-start(f32[1,128]{1,0:T(1,128)} %get-tuple-element.1279), channel_id=1, source_target_pairs={{0,8},{8,16},{16,24},{1,9},{9,17},{17,25},{2,10},{10,18},{18,26},{... | collective-permute-start | bytes 1544 | tf_op jit(solution)/shard_map/ppermute | solution.py:27
  190.0 53.5 %collective-permute-start.7 = (f32[1,128]{1,0:T(1,128)}, f32[1,128]{1,0:T(1,128)}, u32[]{:S(2)}, u32[]{:S(2)}) collective-permute-start(f32[1,128]{1,0:T(1,128)} %get-tuple-element.1278), channel_id=1, source_target_pairs={{8,0},{16,8},{24,16},{9,1},{17,9},{25,17},{10,2},{18,10},{26,18},{... | collective-permute-start | bytes 1544 | tf_op jit(solution)/shard_map/ppermute | solution.py:28
  192.6 86.4 %collective-permute-start.5 = (f32[32,1]{1,0:T(8,128)}, f32[32,1]{1,0:T(8,128)S(1)}, u32[]{:S(2)}, u32[]{:S(2)}) collective-permute-start(f32[32,1]{1,0:T(8,128)} %slice.442), channel_id=1, source_target_pairs={{0,1},{1,2},{2,3},{3,4},{4,5},{5,6},{6,7},{8,9},{9,10},{10,11},{11... | collective-permute-start | bytes 392 | tf_op jit(solution)/shard_map/ppermute | solution.py:36
  197.0 53.3 %collective-permute-start.4 = (f32[1,128]{1,0:T(1,128)}, f32[1,128]{1,0:T(1,128)}, u32[]{:S(2)}, u32[]{:S(2)}) collective-permute-start(f32[1,128]{1,0:T(1,128)} %slice.441), channel_id=1, source_target_pairs={{0,8},{8,16},{16,24},{1,9},{9,17},{17,25},{2,10},{10,18},{18,26},{... | collective-permute-start | bytes 1544 | tf_op jit(solution)/shard_map/ppermute | solution.py:36
  244.3 6.6 collective-permute-start.8
  251.7 14.3 %all-to-all-start = ((f32[32,1,1536]{2,1,0:T(1,128)}), f32[32,1,1536]{2,1,0:T(1,128)S(1)}, u32[]{:S(2)}, u32[]{:S(2)}) async-start(f32[32,1,1536]{2,1,0:T(1,128)} %all_to_all.24), calls=%async_computation | async-start | bytes 393216 | tf_op jit(solution)/shard_map/all_to_all | solution.py:180
  314.9 7.2 collective-permute-start
  353.2 7.0 collective-permute-start
  360.9 6.8 collective-permute-start.2
  362.2 6.4 collective-permute-start.3
  391.8 7.0 collective-permute-start
  399.6 6.8 collective-permute-start.2
  400.9 6.4 collective-permute-start.3
  430.5 7.0 collective-permute-start
  438.2 6.8 collective-permute-start.2
  439.5 6.4 collective-permute-start.3
  469.1 7.0 collective-permute-start
  476.9 6.8 collective-permute-start.2
  507.8 7.0 collective-permute-start
  515.5 6.8 collective-permute-start.2
  546.4 7.0 collective-permute-start
  554.1 6.8 collective-permute-start.2
  585.0 7.0 collective-permute-start
  592.8 6.8 collective-permute-start.2
  623.7 7.0 collective-permute-start
  631.4 6.8 collective-permute-start.2
  662.3 7.0 collective-permute-start
  670.1 6.8 collective-permute-start.2
  701.0 7.0 collective-permute-start
  708.7 6.8 collective-permute-start.2
  740.5 21.0 %all-to-all-start.2 = ((f32[32,1,1536]{2,1,0:T(1,128)}), f32[32,1,1536]{2,1,0:T(1,128)S(1)}, u32[]{:S(2)}, u32[]{:S(2)}) async-start(f32[32,1,1536]{2,1,0:T(1,128)} %all_to_all.25), calls=%async_computation.2 | async-start | bytes 393216 | tf_op jit(solution)/shard_map/all_to_all | solution.py:249
  (44 other events, 2495.9 us)
where the time goes:
time: 962 us; the launch traced here: 959 us
  local copies, waits for them, and re-layouts  681 us (71%)
  starting transfers between devices  204 us (21%)
  waiting for transfers between devices  29.8 us (3%)
  other arithmetic  26.4 us (3%)
  matrix products  12.2 us (1%)
    gather x12, local copies, waits for them, and re-layouts, ocean_turn(): level_now.reshape(tile_rows * tile_cols)[flat_cells]  276 us
    gather x1, local copies, waits for them, and re-layouts, per_device(): returned[tile_grid, step_grid, slot_grid].reshape(blocks, STEPS * MPB)  196 us
    gather x12, local copies, waits for them, and re-layouts, per_device(): first_index = jnp.searchsorted(sorted_tiles, sorted_tiles, side='left')  141 us
    ppermute x26, starting transfers between devices, padded_2(): before = lax.ppermute(last, axis, up)  129 us
    ppermute x26, starting transfers between devices, padded_2(): after = lax.ppermute(leading, axis, down)  42.3 us
  transfers between devices with their start and end apart: 57, of which 26 were waited for; matrix products, arithmetic and copies ran while one was open for 7% of the time, Pallas kernels for 0%

commit v1 on v0

v1 whole, which is shorter than its diff:
```python
import functools
import math

import jax
import jax.numpy as jnp
from jax import lax
from jax.experimental import pallas as pl
from jax.experimental.pallas import tpu as pltpu
from jax.sharding import PartitionSpec as P

RB = 128
MPB = 32
STEPS = 12

gravity = 9.81
step_seconds = 300.0
cell_metres = 3000.0
river_manning = 0.035
ocean_manning = 0.025
depth_floor = 0.05
reach_offsets = 16

LANES = 128
SENT = 13
TALL = 16
WIDE = 256
HALO = 12
STRIP = 16
FIELDS = 16
f32, bf16, i32 = jnp.float32, jnp.bfloat16, jnp.int32

PARAMS = pltpu.CompilerParams(vmem_limit_bytes=40 * 1024 * 1024)


def flow_after(unit_flow, upper, lower, bed_top, drive, manning):
    face_depth = jnp.maximum(upper, lower) - bed_top
    driving = drive * jnp.maximum(face_depth, 0.0) * (upper - lower)
    power = -7.0 / 3.0 * math.log2(math.e)
    thin = jnp.exp2(jnp.log(jnp.maximum(face_depth, depth_floor)) * power)
    friction = (gravity * step_seconds * manning * manning) * jnp.abs(unit_flow) * thin
    divisor = 1.0 + friction
    inverse = pl.reciprocal(divisor, approx=True)
    inverse = inverse * (2.0 - divisor * inverse)
    return (unit_flow + driving) * inverse


def in_two(values):
    high = values.astype(bf16)
    return high, (values - high.astype(f32)).astype(bf16)


def small(labels):
    return jnp.broadcast_to(labels.astype(f32), (TALL, labels.shape[1])).astype(bf16)


def one_hot_columns(columns, rhs, lanes):
    labels = small(columns)
    place = lax.broadcasted_iota(i32, labels.shape, 0).astype(f32).astype(bf16)
    one, none = jnp.ones(labels.shape, bf16), jnp.zeros(labels.shape, bf16)
    for part in range(WIDE // TALL):
        hit = labels - part * TALL == place
        rhs[part * TALL : (part + 1) * TALL, lanes] = jnp.where(hit, one, none)


def lay_out(values, rows, columns, lhs, rhs, lanes):
    high, low = in_two(values)
    labels = small(rows)
    none = jnp.zeros(labels.shape, bf16)
    for row in range(TALL):
        hit = labels == row
        lhs[row * TALL : (row + 1) * TALL, lanes] = jnp.where(hit, high, none)
        lhs[WIDE + row * TALL : WIDE + (row + 1) * TALL, lanes] = jnp.where(hit, low, none)
    one_hot_columns(columns, rhs, lanes)


def add_up(lhs, rhs):
    both = lax.dot_general(
        lhs[...], rhs[...], (((1,), (1,)), ((), ())), preferred_element_type=f32
    )
    return both[:WIDE] + both[WIDE:]


def look_up(table, rows, hot):
    both = jnp.concatenate([hot, hot], axis=0)
    found = jnp.dot(table, both, preferred_element_type=f32)
    total = jnp.zeros((TALL, rows.shape[1]), f32)
    for row in range(TALL):
        hit = jnp.broadcast_to(rows == row, total.shape)
        total = total + jnp.where(hit, found[row * TALL : (row + 1) * TALL], 0.0)
    return total


def cell_labels(cells, tile_cols):
    row, column = cells // tile_cols, cells % tile_cols
    return row % TALL, row // TALL * tile_cols + column


def river_kernel(
    devices,
    capacity,
    *refs,
):
    inputs, (depth_out, send_out, address_out), refs = refs[:10], refs[10:13], refs[13:]
    copies = [
        pltpu.make_async_copy(whole, own, refs[10].at[number])
        for number, (whole, own) in enumerate(zip(inputs, refs[:10]))
    ]
    for copy in copies[::-1]:
        copy.start()
    river_steps(devices, capacity, copies, *refs[:10], depth_out, send_out, address_out, *refs[10:])


def river_steps(
    devices,
    capacity,
    copies,
    depth_in,
    flow_in,
    bed_in,
    width_in,
    length_in,
    runoff_in,
    into_in,
    prev_in,
    tile_in,
    cell_in,
    depth_out,
    send_out,
    address_out,
    arrivals,
    depth_end,
    enters,
    series,
    turned,
    tiles,
    hots,
    lhs,
    rhs,
):
    blocks = depth_in.shape[0]
    groups = LANES // MPB
    rows = blocks // groups
    inland = RB - MPB
    lane = lax.broadcasted_iota(i32, (blocks, RB), 1)

    turned[...] = jnp.zeros_like(turned)
    for copy in copies[7:]:
        copy.wait()
    turned[0:MPB, 0:blocks] = tile_in[...].astype(f32)
    turned[MPB : 2 * MPB, 0:blocks] = cell_in[...].astype(f32)
    turned[inland:RB, 0:blocks] = prev_in[...]
    mouths = jnp.transpose(turned[...])[0:blocks]
    prev = mouths

    def grouped(array, first):
        lanes16 = lax.broadcasted_iota(i32, (rows, LANES), 1)
        result = jnp.zeros((rows, LANES), f32)
        for g in range(groups):
            part = array[g * rows : (g + 1) * rows]
            shift = (g * MPB - first) % LANES
            part = part if shift == 0 else pltpu.roll(part, shift, 1)
            result = jnp.where(lanes16 // MPB == g, part, result)
        return result

    tiles[...] = grouped(mouths, 0).astype(i32)
    series[STEPS * rows : (STEPS + 1) * rows] = grouped(mouths, MPB)
    series[(STEPS + 1) * rows :] = jnp.zeros((series.shape[0] - (STEPS + 1) * rows, LANES), f32)

    for i in range(rows):
        names = jnp.broadcast_to(tiles[i : i + 1], (devices, LANES))
        hit = names == lax.broadcasted_iota(i32, (devices, LANES), 0)
        hots[i * devices : (i + 1) * devices] = jnp.where(hit, 1.0, 0.0).astype(bf16)
    shape = (LANES, 2 * LANES)
    earlier = lax.broadcasted_iota(i32, shape, 0) < lax.broadcasted_iota(i32, shape, 1)
    counted = jnp.dot(
        hots[...], jnp.where(earlier, 1.0, 0.0).astype(bf16), preferred_element_type=f32
    )
    before = jnp.zeros((devices, LANES), f32)
    for i in range(rows):
        part = slice(i * devices, (i + 1) * devices)
        ranks = (counted[part, :LANES] + before) * hots[part].astype(f32)
        rank = jnp.sum(ranks, axis=0, keepdims=True).astype(i32)
        address_out[i : i + 1] = tiles[i : i + 1] * capacity + rank
        before = before + counted[part, LANES:]

    for copy in copies[:7]:
        copy.wait()
    into = into_in[...]
    at_mouth = lane >= inland
    down = jnp.where(at_mouth, 0, into)
    offset = jnp.where(at_mouth, 0, into - lane)
    bed = bed_in[...]
    bed_top = jnp.where(
        at_mouth, bed, jnp.maximum(bed, jnp.take_along_axis(bed, down, axis=1))
    )
    drive = gravity * step_seconds / length_in[...]
    area = step_seconds / (width_in[...] * length_in[...])
    for o in range(1, reach_offsets + 1):
        hit = jnp.where(offset == o, 1.0, 0.0)
        enters[o - 1] = pltpu.roll(hit, o, 1)

    def river_turn(substep, carry):
        depth, flow = carry
        surface = bed + depth
        below = jnp.where(at_mouth, prev, jnp.take_along_axis(surface, down, axis=1))
        flow = flow_after(flow, surface, below, bed_top, drive, river_manning)
        discharge = flow * width_in[...]
        inflow = enters[0] * pltpu.roll(discharge, 1, 1)
        for o in range(2, reach_offsets + 1):
            inflow = inflow + enters[o - 1] * pltpu.roll(discharge, o, 1)
        depth = depth + area * (inflow + runoff_in[...] - discharge)
        series[pl.ds(pl.multiple_of(substep * rows, rows), rows)] = grouped(discharge, inland)
        return depth, flow

    depth, _ = lax.fori_loop(0, STEPS, river_turn, (depth_in[...], flow_in[...]), unroll=2)
    depth_end[...] = depth
    finished = pltpu.make_async_copy(depth_end, depth_out, arrivals.at[len(copies)])
    finished.start()

    for i in range(rows):
        address = address_out[i : i + 1]
        lay_out(
            series[pl.ds(i, TALL, stride=rows)],
            address // WIDE,
            address % WIDE,
            lhs,
            rhs,
            slice(i * LANES, (i + 1) * LANES),
        )
    packed = add_up(lhs, rhs)
    for row in range(TALL):
        part = packed[row * TALL : row * TALL + SENT]
        for half in range(2):
            at = (2 * row + half) * SENT
            send_out[at : at + SENT] = part[:, half * LANES : (half + 1) * LANES]
    finished.wait()


def reach_of(field):
    return STEPS - 1 - field if field < STEPS else HALO


ROW_AT = [sum(reach_of(f) for f in range(field)) for field in range(FIELDS + 1)]
ROWS_SENT = -(-ROW_AT[FIELDS] // 8) * 8


def source_kernel(arrived, *refs):
    inputs, (fields, odd, even, rhs), refs = refs[:5], refs[5:9], refs[9:]
    first_of_pair = lax.axis_index("river") % 2 == 0
    sea_level, sea_bed, wet_mask, flux_east, flux_north, arrivals, lhs, sums = refs
    copies = [
        pltpu.make_async_copy(whole, own, arrivals.at[number])
        for number, (whole, own) in enumerate(zip(inputs, refs[:5]))
    ]
    for copy in copies:
        copy.start()
    groups = arrived.shape[0] // SENT
    tile_rows, tile_cols = sea_level.shape

    def place(s, carry):
        values = arrived[pl.ds(s * SENT, SENT)]
        values = jnp.concatenate([values, jnp.zeros((TALL - SENT, LANES), f32)], axis=0)
        cells = values[STEPS : STEPS + 1].astype(i32)
        rows, columns = cell_labels(cells, tile_cols)
        lay_out(values, rows, columns, lhs, rhs, pl.ds(pl.multiple_of(s * LANES, LANES), LANES))
        return carry

    lax.fori_loop(0, groups, place, 0, unroll=2)
    total = add_up(lhs, rhs)
    for half in range(2):
        sums[half * WIDE : (half + 1) * WIDE] = total[:, half * LANES : (half + 1) * LANES]
    for copy in copies:
        copy.wait()
    bed = sea_bed[...]
    level = jnp.where(wet_mask[...] == 1, jnp.maximum(sea_level[...], bed), bed)

    def put(field, value):
        fields[field * tile_rows : (field + 1) * tile_rows] = value
        reach = reach_of(field)
        if reach:
            last, first = value[tile_rows - reach :], value[:reach]
            part = slice(ROW_AT[field], ROW_AT[field] + reach)
            odd[part] = jnp.where(first_of_pair, first, last)
            even[part] = jnp.where(first_of_pair, last, first)

    for swap_out in (odd, even):
        swap_out[ROWS_SENT - 8 :] = jnp.zeros((8, LANES), f32)
    for step in range(STEPS):
        halves = [sums[pl.ds(half * WIDE + step, TALL, stride=TALL)] for half in range(2)]
        put(step, jnp.concatenate(halves, axis=0))
    for number, value in enumerate((level, bed, flux_east[...], flux_north[...])):
        put(STEPS + number, value)


def strip_kernel(fields, from_odd, from_even, tall, odd, even):
    upper = lax.axis_index("river") % 2 == 0
    first_of_pair = lax.axis_index("coast") % 2 == 0
    from_before = jnp.where(upper, from_odd[...], from_even[...])
    from_after = jnp.where(upper, from_even[...], from_odd[...])
    tile_rows = fields.shape[0] // FIELDS
    height = tall.shape[0] // FIELDS
    per = LANES // STRIP
    lane = lax.broadcasted_iota(i32, (height, LANES), 1)
    for group in range(FIELDS // per):
        ends = jnp.zeros((height, LANES), f32)
        starts = jnp.zeros((height, LANES), f32)
        for place in range(per):
            field = group * per + place
            parts = [fields[field * tile_rows : (field + 1) * tile_rows]]
            reach, at = reach_of(field), ROW_AT[field]
            if reach:
                parts.append(from_after[at : at + reach])
            if reach < HALO:
                parts.append(jnp.zeros((2 * HALO - 2 * reach, LANES), f32))
            if reach:
                parts.append(from_before[at : at + reach])
            value = jnp.concatenate(parts, axis=0)
            tall[field * height : (field + 1) * height] = value
            here = lane // STRIP == place
            shift = (place + 1) * STRIP % LANES
            moved = value if shift == 0 else pltpu.roll(value, shift, 1)
            ends = jnp.where(here, moved, ends)
            moved = value if place == 0 else pltpu.roll(value, place * STRIP, 1)
            starts = jnp.where(here, moved, starts)
        part = slice(group * height, (group + 1) * height)
        odd[part] = jnp.where(first_of_pair, starts, ends)
        even[part] = jnp.where(first_of_pair, ends, starts)


def ocean_kernel(
    tile_rows, tall, from_odd, from_even, arrived, hot, level_out, replies, sources, history
):
    height = tall.shape[0] // FIELDS
    width = 2 * LANES
    per = LANES // STRIP
    river, coast = lax.axis_index("river"), lax.axis_index("coast")
    rivers, coasts = lax.axis_size("river"), lax.axis_size("coast")
    lane = lax.broadcasted_iota(i32, (height, LANES), 1)
    from_left = jnp.where(coast % 2 == 0, from_odd[...], from_even[...])
    from_right = jnp.where(coast % 2 == 0, from_even[...], from_odd[...])

    def whole(field):
        group, place = field // per, field % per
        rows = slice(group * height, (group + 1) * height)
        shift = (LANES - place * STRIP) % LANES
        after = from_right[rows] if shift == 0 else pltpu.roll(from_right[rows], shift, 1)
        shift = (LANES - (place + 1) * STRIP) % LANES
        before = from_left[rows] if shift == 0 else pltpu.roll(from_left[rows], shift, 1)
        beside = jnp.where(lane < STRIP, after, jnp.where(lane >= LANES - STRIP, before, 0.0))
        return jnp.concatenate([tall[field * height : (field + 1) * height], beside], axis=1)

    for step in range(STEPS):
        sources[step] = whole(step) * (step_seconds / (cell_metres * cell_metres))
    level, bed, east, north = [whole(STEPS + number) for number in range(4)]

    row = lax.broadcasted_iota(i32, (height, width), 0)
    column = lax.broadcasted_iota(i32, (height, width), 1)
    row_in = jnp.where(
        row < tile_rows, 1, jnp.where(row < tile_rows + HALO, (river < rivers - 1).astype(i32), (river > 0).astype(i32))
    )
    column_in = jnp.where(
        column < LANES, 1, jnp.where(column < LANES + LANES // 2, (coast < coasts - 1).astype(i32), (coast > 0).astype(i32))
    )
    inside = row_in * column_in == 1

    def next_row(value):
        return pltpu.roll(value, height - 1, 0)

    def next_column(value):
        return pltpu.roll(value, width - 1, 1)

    bed_east = jnp.maximum(bed, next_row(bed))
    bed_north = jnp.maximum(bed, next_column(bed))
    drive = gravity * step_seconds / cell_metres

    def ocean_turn(step, carry):
        level, east, north = carry
        east = flow_after(east, level, next_row(level), bed_east, drive, ocean_manning)
        north = flow_after(north, level, next_column(level), bed_north, drive, ocean_manning)
        spread = east - pltpu.roll(east, 1, 0) + north - pltpu.roll(north, 1, 1)
        level = level - step_seconds / cell_metres * spread + sources[step]
        level = jnp.where(inside, level, 0.0)
        for half in range(2):
            part = level[half * TALL : (half + 1) * TALL, :LANES]
            history[pl.ds(half * WIDE + step, TALL, stride=TALL)] = part
        return level, east, north

    history[...] = jnp.zeros_like(history)
    level, east, north = lax.fori_loop(0, STEPS, ocean_turn, (level, east, north))
    level_out[...] = level[:tile_rows, :LANES]

    halves = [history[:WIDE], history[WIDE:]]
    table = jnp.concatenate(in_two(jnp.concatenate(halves, axis=1)), axis=1)

    def reply(pair, carry):
        at = [2 * pair, 2 * pair + 1]
        cells = [arrived[pl.ds(s * SENT + STEPS, 1)] for s in at]
        rows, _ = cell_labels(jnp.concatenate(cells, axis=1).astype(i32), LANES)
        found = look_up(table, rows, hot[:, pl.ds(pl.multiple_of(pair * WIDE, WIDE), WIDE)])
        for half, s in enumerate(at):
            replies[pl.ds(s * STEPS, STEPS)] = found[:STEPS, half * LANES : (half + 1) * LANES]
        return carry

    lax.fori_loop(0, replies.shape[0] // STEPS // 2, reply, 0, unroll=2)


def mouth_kernel(returned, address, level_out, table, series, hot):
    rows = address.shape[0]
    groups = LANES // MPB
    for row in range(TALL):
        part = slice(row * TALL, (row + 1) * TALL)
        for half in range(2):
            at = (2 * row + half) * STEPS
            values = returned[at : at + STEPS]
            values = jnp.concatenate([values, jnp.zeros((TALL - STEPS, LANES), f32)], axis=0)
            high, low = in_two(values)
            table[part, half * LANES : (half + 1) * LANES] = high
            table[part, WIDE + half * LANES : WIDE + (half + 1) * LANES] = low
    for i in range(0, rows, 2):
        labels = jnp.concatenate([address[i : i + 1], address[i + 1 : i + 2]], axis=1)
        one_hot_columns(labels % WIDE, hot, slice(None))
        found = look_up(table[...], labels // WIDE, hot[...])
        series[pl.ds(i, TALL, stride=rows)] = found[:, :LANES]
        series[pl.ds(i + 1, TALL, stride=rows)] = found[:, LANES:]
    lane = lax.broadcasted_iota(i32, (rows, LANES), 1)
    for block in range(STEPS // groups):
        for g in range(groups):
            result = jnp.zeros((rows, LANES), f32)
            for place in range(groups):
                step = block * groups + place
                part = series[step * rows : (step + 1) * rows]
                shift = (place - g) * MPB % LANES
                part = part if shift == 0 else pltpu.roll(part, shift, 1)
                result = jnp.where(lane // MPB == place, part, result)
            level_out[g * rows : (g + 1) * rows, block * LANES : (block + 1) * LANES] = result


def shape(*dims, dtype=f32):
    return jax.ShapeDtypeStruct(dims, dtype)


def in_hbm(*arrays):
    return [pltpu.with_memory_space_constraint(whole, pltpu.HBM) for whole in arrays]


def swap(values, tall, devices, capacity):
    per = LANES // capacity
    if per > 1:
        values = values.reshape(devices // per, tall, per, capacity).transpose(0, 2, 1, 3)
    values = values.reshape(devices, 1, tall * capacity)
    values = lax.all_to_all(values, ("river", "coast"), split_axis=0, concat_axis=0, tiled=True)
    if per > 1:
        values = values.reshape(devices // per, per, tall, capacity).transpose(0, 2, 1, 3)
    return values.reshape(devices // per * tall, LANES)


def with_neighbours(odd, even, axis):
    size = lax.axis_size(axis)
    routes = [
        [(i + k, i + 1 - k) for i in range(start, size - 1, 2) for k in range(2)]
        for start in (1, 0)
    ]
    return lax.ppermute(odd, axis, routes[0]), lax.ppermute(even, axis, routes[1])


def per_device(
    reach_depth,
    reach_flow,
    reach_bed,
    reach_width,
    reach_length,
    runoff,
    flows_into,
    mouth_prev,
    mouth_tile,
    mouth_cell,
    sea_level,
    sea_bed,
    wet_mask,
    flux_east,
    flux_north,
):
    devices = lax.axis_size("river") * lax.axis_size("coast")
    blocks = reach_depth.shape[0]
    tile_rows, tile_cols = sea_level.shape
    mouths = blocks * MPB
    capacity = max(2, 2 * mouths // devices)
    groups = devices * capacity // LANES
    rows = mouths // LANES
    height = tile_rows + 2 * HALO

    depth_after, sending, address = pl.pallas_call(
        functools.partial(river_kernel, devices, capacity),
        name="river",
        out_shape=(
            shape(blocks, RB),
            shape(groups * SENT, LANES),
            shape(rows, LANES, dtype=i32),
        ),
        in_specs=[pl.BlockSpec(memory_space=pltpu.HBM)] * 10,
        out_specs=(
            pl.BlockSpec(memory_space=pltpu.HBM),
            pl.BlockSpec(memory_space=pltpu.VMEM),
            pl.BlockSpec(memory_space=pltpu.VMEM),
        ),
        scratch_shapes=[pltpu.VMEM((blocks, RB), f32)] * 6
        + [
            pltpu.VMEM((blocks, RB), i32),
            pltpu.VMEM((MPB, blocks), f32),
            pltpu.VMEM((MPB, blocks), i32),
            pltpu.VMEM((MPB, blocks), i32),
            pltpu.SemaphoreType.DMA((11,)),
            pltpu.VMEM((blocks, RB), f32),
            pltpu.VMEM((reach_offsets, blocks, RB), f32),
            pltpu.VMEM((TALL * rows, LANES), f32),
            pltpu.VMEM((RB, LANES), f32),
            pltpu.VMEM((rows, LANES), i32),
            pltpu.VMEM((rows * devices, LANES), bf16),
            pltpu.VMEM((2 * WIDE, mouths), bf16),
            pltpu.VMEM((WIDE, mouths), bf16),
        ],
        compiler_params=PARAMS,
    )(
        *in_hbm(
            reach_depth,
            reach_flow,
            reach_bed,
            reach_width,
            reach_length,
            runoff,
            flows_into,
            mouth_prev.T,
            mouth_tile[:, :, 0].T,
            mouth_cell.T,
        )
    )
    arrived = swap(sending, SENT, devices, capacity)

    fields, odd, even, hot = pl.pallas_call(
        source_kernel,
        name="sources",
        out_shape=(
            shape(FIELDS * tile_rows, LANES),
            shape(ROWS_SENT, LANES),
            shape(ROWS_SENT, LANES),
            shape(WIDE, groups * LANES, dtype=bf16),
        ),
        in_specs=[pl.BlockSpec(memory_space=pltpu.VMEM)]
        + [pl.BlockSpec(memory_space=pltpu.HBM)] * 5,
        scratch_shapes=[
            pltpu.VMEM((tile_rows, tile_cols), f32),
            pltpu.VMEM((tile_rows, tile_cols), f32),
            pltpu.VMEM((tile_rows, tile_cols), i32),
            pltpu.VMEM((tile_rows, tile_cols), f32),
            pltpu.VMEM((tile_rows, tile_cols), f32),
            pltpu.SemaphoreType.DMA((5,)),
            pltpu.VMEM((2 * WIDE, groups * LANES), bf16),
            pltpu.VMEM((2 * WIDE, LANES), f32),
        ],
        compiler_params=PARAMS,
    )(arrived, *in_hbm(sea_level, sea_bed, wet_mask, flux_east, flux_north))
    from_odd, from_even = with_neighbours(odd, even, "river")

    strips = FIELDS * STRIP // LANES * height
    tall, odd, even = pl.pallas_call(
        strip_kernel,
        name="strips",
        out_shape=(shape(FIELDS * height, LANES), shape(strips, LANES), shape(strips, LANES)),
        compiler_params=PARAMS,
    )(fields, from_odd, from_even)
    from_odd, from_even = with_neighbours(odd, even, "coast")

    level_after, replies = pl.pallas_call(
        functools.partial(ocean_kernel, tile_rows),
        name="ocean",
        out_shape=(shape(tile_rows, tile_cols), shape(groups * STEPS, LANES)),
        scratch_shapes=[
            pltpu.VMEM((STEPS, height, 2 * LANES), f32),
            pltpu.VMEM((2 * WIDE, LANES), f32),
        ],
        compiler_params=PARAMS,
    )(tall, from_odd, from_even, arrived, hot)
    returned = swap(replies, STEPS, devices, capacity)

    mouth_level = pl.pallas_call(
        mouth_kernel,
        name="mouths",
        out_shape=shape(blocks, STEPS * MPB),
        scratch_shapes=[
            pltpu.VMEM((WIDE, 2 * WIDE), bf16),
            pltpu.VMEM((TALL * rows, LANES), f32),
            pltpu.VMEM((WIDE, WIDE), bf16),
        ],
        compiler_params=PARAMS,
    )(returned, address)
    return (depth_after, level_after, mouth_level)


def solution(mesh):
    by_block = P(("river", "coast"), None)
    tiled = P("river", "coast")
    return jax.shard_map(
        per_device,
        mesh=mesh,
        in_specs=(by_block,) * 8
        + (P(("river", "coast"), None, None), by_block)
        + (tiled,) * 5,
        out_specs=(by_block, tiled, by_block),
        check_vma=False,
    )
```

time: 962 us -> 58.7 us (0.06)
  local copies, waits for them, and re-layouts: 681 us -> 0 us
  starting transfers between devices: 204 us -> 6.95 us
  blocking collectives: 0 us -> 28.7 us
  other arithmetic: 26.4 us -> 0 us
  waiting for transfers between devices: 29.8 us -> 4.56 us
  Pallas kernels: 0 us -> 17.2 us
  matrix products: 12.2 us -> 0 us
    gather x26 -> x0, local copies, waits for them, and re-layouts: 626 us -> none  [the longest x12 276 us: ocean_turn(): level_now.reshape(tile_rows * tile_cols)[flat_cells]]
    ppermute x54 -> x4, starting transfers between devices: 178 us -> 6.95 us  [the longest x2 3.82 us: with_neighbours(): lax.ppermute(even, axis, routes[1])]
    all_to_all x0 -> x2, blocking collectives: none -> 28.7 us  [swap(): lax.all_to_all(values, ('river', 'coast'), split_axis=0, concat_axis=0, t...]
    all_to_all x3 -> x0, starting transfers between devices: 25.5 us -> none  [the longest x1 12.5 us: per_device(): lax.all_to_all(replies.reshape(devices, STEPS * capacity), ('river', 'coa...]
    unnamed x46 -> x0, local copies, waits for them, and re-layouts: 18 us -> none
    pallas_call x0 -> x5, Pallas kernels: none -> 17.2 us  [the longest x1 6.37 us: per_device(): pl.pallas_call(functools.partial(river_kernel, devices, capacity), name='...]
    all_to_all x3 -> x0, waiting for transfers between devices: 13.7 us -> none  [the longest x1 8.2 us: per_device(): lax.all_to_all(replies.reshape(devices, STEPS * capacity), ('river', 'coa...]
    dot_general x1 -> x0, matrix products: 12.2 us -> none  [per_device(): jnp.einsum('mr,kmc->krc', row_hits, weighted, precision=lax.Precision.HIG...]
  transfers between devices with their start and end apart: 57 -> 4, of which waited for: 26 -> 2; matrix products, arithmetic and copies ran while one was open for 7% -> 0% of each run, Pallas kernels for 0% -> 0%
where the time goes in v1:
time: 58.7 us; the launch traced here: 58.1 us
  blocking collectives  28.7 us (49%)
  Pallas kernels  17.2 us (29%)
  starting transfers between devices  6.95 us (12%)
  waiting for transfers between devices  4.56 us (8%)
  between operations  0.69 us (1%)
    all_to_all x2, blocking collectives, swap(): lax.all_to_all(values, ('river', 'coast'), split_axis=0, concat_axis=0, t...  28.7 us
    pallas_call x1, Pallas kernels, per_device(): pl.pallas_call(functools.partial(river_kernel, devices, capacity), name='...  6.37 us
    pallas_call x1, Pallas kernels, per_device(): pl.pallas_call(functools.partial(ocean_kernel, tile_rows), name='ocean',...  5.61 us
    ppermute x2, starting transfers between devices, with_neighbours(): lax.ppermute(even, axis, routes[1])  3.82 us
    pallas_call x1, Pallas kernels, per_device(): pl.pallas_call(source_kernel, name='sources', out_shape=(shape(FIELDS * t...  3.41 us
    ppermute x2, starting transfers between devices, with_neighbours(): lax.ppermute(odd, axis, routes[0])  3.13 us
    ppermute x2, waiting for transfers between devices, with_neighbours(): lax.ppermute(odd, axis, routes[0])  2.99 us
    ppermute x2, waiting for transfers between devices, with_neighbours(): lax.ppermute(even, axis, routes[1])  1.57 us
  transfers between devices with their start and end apart: 4, of which 2 were waited for; matrix products, arithmetic and copies ran while one was open for 0% of the time, Pallas kernels for 0%

profile of v1, /device:TPU:1, one launch (start us, length us, event | category | flops | bytes accessed | tf_op | source)
XLA Modules:
  0.0 58.1 jit_solution(16625851707755888772)
XLA Ops:
  0.6 6.4 %river.1 = (f32[64,128]{1,0:T(8,128)}, f32[416,128]{1,0:T(8,128)S(1)}, s32[16,128]{1,0:T(8,128)S(1)}) custom-call(f32[64,128]{1,0:T(8,128)} %refs_0_.2, f32[64,128]{1,0:T(8,128)} %refs_1_.2, f32[64,128]{1,0:T(8,128)} %refs_2_.2, f32[64,128]{1,0:T(8,128)} %refs_3_.2, f32[64,128]{1,0:T(8,128)} %refs_4_.2, f32[64,128]{1,0:T(8,128)} %refs_5_.1, ...), custom_call_target="tpu_custom_call" | custom-call | tf_op jit(solution)/shard_map/river/pallas_call | solution.py:492
  7.0 15.8 %all_to_all.10 = f32[32,1,1664]{2,1,0:T(1,128)S(1)} all-to-all(f32[32,1,1664]{2,1,0:T(1,128)S(1)} %bitcast.12), channel_id=1, replica_groups=mesh['river'=4,'coast'=8] {'river','coast'}, dimensions={0} | all-to-all | bytes 425984 | tf_op jit(solution)/shard_map/all_to_all | solution.py:451
  22.8 3.4 %sources.1 = (f32[512,128]{1,0:T(8,128)S(1)}, f32[120,128]{1,0:T(8,128)S(1)}, f32[120,128]{1,0:T(8,128)S(1)}, bf16[256,4096]{1,0:T(8,128)(2,1)S(1)}) custom-call(f32[416,128]{1,0:T(8,128)S(1)} %bitcast.9, f32[32,128]{1,0:T(8,128)} %refs_0_.3, f32[32,128]{1,0:T(8,128)} %refs_1_.3, s32[32,128]{1,0:T(8,128)} %refs_2_.3, f32[32,128]{1,0:T(8,128)} %refs_3_.3, ...), custom_call_target="tpu_custom_call" | custom-call | tf_op jit(solution)/shard_map/sources/pallas_call | solution.py:539
  26.3 2.5 %collective-permute-start = (f32[120,128]{1,0:T(8,128)S(1)}, f32[120,128]{1,0:T(8,128)S(1)}, u32[]{:S(2)}, u32[]{:S(2)}) collective-permute-start(f32[120,128]{1,0:T(8,128)S(1)} %get-tuple-element.18), channel_id=1, source_target_pairs={{8,16},{16,8},{9,17},{17,9},{10,18},{18,10},{11,19},{19,11},{12,20... | collective-permute-start | bytes 184328 | tf_op jit(solution)/shard_map/ppermute | solution.py:463
  28.7 0.1 collective-permute-start.1
  28.8 3.0 %collective-permute-done.from_odd = f32[120,128]{1,0:T(8,128)S(1)} collective-permute-done((f32[120,128]{1,0:T(8,128)S(1)}, f32[120,128]{1,0:T(8,128)S(1)}, u32[]{:S(2)}, u32[]{:S(2)}) %collective-permute-start) | collective-permute-done | bytes 61472 | tf_op jit(solution)/shard_map/ppermute | solution.py:463
  31.8 0.0 collective-permute-done.1.from_even
  31.8 0.3 strips.1
  32.1 0.7 %collective-permute-start.2 = (f32[112,128]{1,0:T(8,128)S(1)}, f32[112,128]{1,0:T(8,128)S(1)}, u32[]{:S(2)}, u32[]{:S(2)}) collective-permute-start(f32[112,128]{1,0:T(8,128)S(1)} %get-tuple-element.21), channel_id=1, source_target_pairs={{1,2},{2,1},{3,4},{4,3},{5,6},{6,5},{9,10},{10,9},{11,12},{12,11},... | collective-permute-start | bytes 172040 | tf_op jit(solution)/shard_map/ppermute | solution.py:463
  32.7 3.8 %collective-permute-start.3 = (f32[112,128]{1,0:T(8,128)S(1)}, f32[112,128]{1,0:T(8,128)S(1)}, u32[]{:S(2)}, u32[]{:S(2)}) collective-permute-start(f32[112,128]{1,0:T(8,128)S(1)} %get-tuple-element.22), channel_id=1, source_target_pairs={{0,1},{1,0},{2,3},{3,2},{4,5},{5,4},{6,7},{7,6},{8,9},{9,8},{10,11... | collective-permute-start | bytes 172040 | tf_op jit(solution)/shard_map/ppermute | solution.py:463
  36.5 0.0 collective-permute-done.2.from_odd
  36.5 1.6 %collective-permute-done.3.from_even = f32[112,128]{1,0:T(8,128)S(1)} collective-permute-done((f32[112,128]{1,0:T(8,128)S(1)}, f32[112,128]{1,0:T(8,128)S(1)}, u32[]{:S(2)}, u32[]{:S(2)}) %collective-permute-start.3) | collective-permute-done | bytes 57376 | tf_op jit(solution)/shard_map/ppermute | solution.py:463
  38.1 5.6 %ocean.1 = (f32[32,128]{1,0:T(8,128)}, f32[384,128]{1,0:T(8,128)S(1)}) custom-call(f32[896,128]{1,0:T(8,128)S(1)} %get-tuple-element.20.tall, f32[112,128]{1,0:T(8,128)S(1)} %collective-permute-done.2.from_odd, f32[112,128]{1,0:T(8,128)S(1)} %collective-permute-done.3.from_even, f32[416,128]{1,0:T(8,128)S(1)} %bitcast.10, ...), custom_call_target="tpu_custom_call" | custom-call | tf_op jit(solution)/shard_map/ocean/pallas_call | solution.py:573
  43.7 12.9 %all_to_all.11 = f32[32,1,1536]{2,1,0:T(1,128)S(1)} all-to-all(f32[32,1,1536]{2,1,0:T(1,128)S(1)} %bitcast.13), channel_id=1, replica_groups=mesh['river'=4,'coast'=8] {'river','coast'}, dimensions={0} | all-to-all | bytes 393216 | tf_op jit(solution)/shard_map/all_to_all | solution.py:451
  56.6 1.6 %mouths.1 = f32[64,384]{1,0:T(8,128)} custom-call(f32[384,128]{1,0:T(8,128)S(1)} %bitcast.11, s32[16,128]{1,0:T(8,128)S(1)} %get-tuple-element.26.address), custom_call_target="tpu_custom_call" | custom-call | tf_op jit(solution)/shard_map/mouths/pallas_call | solution.py:585
Async XLA Ops:
  26.3 5.5 %collective-permute-start = (f32[120,128]{1,0:T(8,128)S(1)}, f32[120,128]{1,0:T(8,128)S(1)}, u32[]{:S(2)}, u32[]{:S(2)}) collective-permute-start(f32[120,128]{1,0:T(8,128)S(1)} %get-tuple-element.18), channel_id=1, source_target_pairs={{8,16},{16,8},{9,17},{17,9},{10,18},{18,10},{11,19},{19,11},{12,20... | collective-permute-start | bytes 184328 | tf_op jit(solution)/shard_map/ppermute | solution.py:463
  28.7 3.1 %collective-permute-start.1 = (f32[120,128]{1,0:T(8,128)S(1)}, f32[120,128]{1,0:T(8,128)S(1)}, u32[]{:S(2)}, u32[]{:S(2)}) collective-permute-start(f32[120,128]{1,0:T(8,128)S(1)} %get-tuple-element.19), channel_id=1, source_target_pairs={{0,8},{8,0},{16,24},{24,16},{1,9},{9,1},{17,25},{25,17},{2,10},{10... | collective-permute-start | bytes 184328 | tf_op jit(solution)/shard_map/ppermute | solution.py:463
  32.1 4.4 %collective-permute-start.2 = (f32[112,128]{1,0:T(8,128)S(1)}, f32[112,128]{1,0:T(8,128)S(1)}, u32[]{:S(2)}, u32[]{:S(2)}) collective-permute-start(f32[112,128]{1,0:T(8,128)S(1)} %get-tuple-element.21), channel_id=1, source_target_pairs={{1,2},{2,1},{3,4},{4,3},{5,6},{6,5},{9,10},{10,9},{11,12},{12,11},... | collective-permute-start | bytes 172040 | tf_op jit(solution)/shard_map/ppermute | solution.py:463
  32.7 5.3 %collective-permute-start.3 = (f32[112,128]{1,0:T(8,128)S(1)}, f32[112,128]{1,0:T(8,128)S(1)}, u32[]{:S(2)}, u32[]{:S(2)}) collective-permute-start(f32[112,128]{1,0:T(8,128)S(1)} %get-tuple-element.22), channel_id=1, source_target_pairs={{0,1},{1,0},{2,3},{3,2},{4,5},{5,4},{6,7},{7,6},{8,9},{9,8},{10,11... | collective-permute-start | bytes 172040 | tf_op jit(solution)/shard_map/ppermute | solution.py:463

commit v2 on v1

--- a/solution.py
+++ b/solution.py
@@ -24,8 +24,9 @@
 SENT = 13
 TALL = 16
 WIDE = 256
+PARTS = ((0, 8), (8, 4))
+CHUNK = 8
 HALO = 12
-STRIP = 16
 FIELDS = 16
 f32, bf16, i32 = jnp.float32, jnp.bfloat16, jnp.int32
 
@@ -62,32 +63,51 @@
         rhs[part * TALL : (part + 1) * TALL, lanes] = jnp.where(hit, one, none)
 
 
-def lay_out(values, rows, columns, lhs, rhs, lanes):
-    high, low = in_two(values)
+def row_owners(owner, steps):
+    for part in range(0, TALL * steps, TALL):
+        number = part + lax.broadcasted_iota(i32, (TALL, LANES), 0)
+        owner[part : part + TALL] = (number // steps).astype(f32).astype(bf16)
+
+
+def in_turn(series, at, stride, steps, first):
+    parts, row = [], first
+    while row < first + 8:
+        step = row % steps
+        count = min(steps - step, first + 8 - row)
+        parts.append(series[pl.ds(at + step * stride, count, stride=stride)])
+        row += count
+    return parts[0] if len(parts) == 1 else jnp.concatenate(parts, axis=0)
+
+
+def lay_out(series, at, stride, steps, rows, owner, lhs, lanes):
+    turns = math.lcm(steps, 8) // 8
+    cycle = [in_turn(series, at, stride, steps, 8 * turn) for turn in range(turns)]
+    pairs = [(cycle[2 * k % turns], cycle[(2 * k + 1) % turns]) for k in range(turns)]
+    halves = [in_two(jnp.concatenate(pair, axis=0)) for pair in pairs]
     labels = small(rows)
     none = jnp.zeros(labels.shape, bf16)
-    for row in range(TALL):
-        hit = labels == row
-        lhs[row * TALL : (row + 1) * TALL, lanes] = jnp.where(hit, high, none)
-        lhs[WIDE + row * TALL : WIDE + (row + 1) * TALL, lanes] = jnp.where(hit, low, none)
-    one_hot_columns(columns, rhs, lanes)
-
-
-def add_up(lhs, rhs):
-    both = lax.dot_general(
-        lhs[...], rhs[...], (((1,), (1,)), ((), ())), preferred_element_type=f32
-    )
-    return both[:WIDE] + both[WIDE:]
-
-
-def look_up(table, rows, hot):
-    both = jnp.concatenate([hot, hot], axis=0)
-    found = jnp.dot(table, both, preferred_element_type=f32)
-    total = jnp.zeros((TALL, rows.shape[1]), f32)
-    for row in range(TALL):
-        hit = jnp.broadcast_to(rows == row, total.shape)
-        total = total + jnp.where(hit, found[row * TALL : (row + 1) * TALL], 0.0)
-    return total
+    for part in range(steps):
+        at_rows = slice(part * TALL, (part + 1) * TALL)
+        hit = labels == owner[at_rows]
+        for number, half in enumerate(halves[part % turns]):
+            at_rows = slice((number * steps + part) * TALL, (number * steps + part + 1) * TALL)
+            lhs[at_rows, lanes] = jnp.where(hit, half, none)
+
+
+def look_up(table, rows, hot, steps):
+    found = jnp.dot(table, hot, preferred_element_type=f32)
+    per = 2 if steps > 6 else 4
+    several = (per * steps, rows.shape[1])
+    labels = jnp.broadcast_to(rows, several) - lax.broadcasted_iota(i32, several, 0) // steps
+    total = jnp.zeros(several, f32)
+    for row in range(0, TALL, per):
+        high = found[row * steps : (row + per) * steps]
+        low = found[(TALL + row) * steps : (TALL + row + per) * steps]
+        total = total + jnp.where(labels == row, high + low, 0.0)
+    result = total[:steps]
+    for number in range(1, per):
+        result = result + total[number * steps : (number + 1) * steps]
+    return result
 
 
 def cell_labels(cells, tile_cols):
@@ -134,7 +154,10 @@
     turned,
     tiles,
     hots,
-    lhs,
+    owner_first,
+    owner_last,
+    lhs_first,
+    lhs_last,
     rhs,
 ):
     blocks = depth_in.shape[0]
@@ -143,9 +166,10 @@
     inland = RB - MPB
     lane = lax.broadcasted_iota(i32, (blocks, RB), 1)
 
-    turned[...] = jnp.zeros_like(turned)
     for copy in copies[7:]:
         copy.wait()
+
+    turned[...] = jnp.zeros_like(turned)
     turned[0:MPB, 0:blocks] = tile_in[...].astype(f32)
     turned[MPB : 2 * MPB, 0:blocks] = cell_in[...].astype(f32)
     turned[inland:RB, 0:blocks] = prev_in[...]
@@ -163,8 +187,7 @@
         return result
 
     tiles[...] = grouped(mouths, 0).astype(i32)
-    series[STEPS * rows : (STEPS + 1) * rows] = grouped(mouths, MPB)
-    series[(STEPS + 1) * rows :] = jnp.zeros((series.shape[0] - (STEPS + 1) * rows, LANES), f32)
+    series[STEPS * rows :] = grouped(mouths, MPB)
 
     for i in range(rows):
         names = jnp.broadcast_to(tiles[i : i + 1], (devices, LANES))
@@ -196,48 +219,74 @@
     drive = gravity * step_seconds / length_in[...]
     area = step_seconds / (width_in[...] * length_in[...])
     for o in range(1, reach_offsets + 1):
-        hit = jnp.where(offset == o, 1.0, 0.0)
-        enters[o - 1] = pltpu.roll(hit, o, 1)
-
-    def river_turn(substep, carry):
-        depth, flow = carry
+        enters[o - 1] = jnp.where(turn(offset, o) == o, 1.0, 0.0)
+
+    def river_turn(substep, depth, flow):
         surface = bed + depth
         below = jnp.where(at_mouth, prev, jnp.take_along_axis(surface, down, axis=1))
         flow = flow_after(flow, surface, below, bed_top, drive, river_manning)
         discharge = flow * width_in[...]
-        inflow = enters[0] * pltpu.roll(discharge, 1, 1)
-        for o in range(2, reach_offsets + 1):
-            inflow = inflow + enters[o - 1] * pltpu.roll(discharge, o, 1)
-        depth = depth + area * (inflow + runoff_in[...] - discharge)
-        series[pl.ds(pl.multiple_of(substep * rows, rows), rows)] = grouped(discharge, inland)
+        sums = [
+            enters[o] * turn(discharge, o + 1) + enters[o + 1] * turn(discharge, o + 2)
+            for o in range(0, reach_offsets, 2)
+        ]
+        while len(sums) > 1:
+            sums = [one + other for one, other in zip(sums[::2], sums[1::2])]
+        depth = depth + area * (sums[0] + (runoff_in[...] - discharge))
+        series[substep * rows : (substep + 1) * rows] = grouped(discharge, inland)
         return depth, flow
 
-    depth, _ = lax.fori_loop(0, STEPS, river_turn, (depth_in[...], flow_in[...]), unroll=2)
-    depth_end[...] = depth
-    finished = pltpu.make_async_copy(depth_end, depth_out, arrivals.at[len(copies)])
-    finished.start()
-
+    columns = jnp.transpose((address_out[...] % WIDE).astype(f32))
+    place = lax.broadcasted_iota(i32, (LANES, LANES), 1).astype(f32).astype(bf16)
+    one, none = jnp.ones((LANES, LANES), bf16), jnp.zeros((LANES, LANES), bf16)
+    number = lax.broadcasted_iota(i32, (TALL, LANES), 0)
     for i in range(rows):
-        address = address_out[i : i + 1]
-        lay_out(
-            series[pl.ds(i, TALL, stride=rows)],
-            address // WIDE,
-            address % WIDE,
-            lhs,
-            rhs,
-            slice(i * LANES, (i + 1) * LANES),
-        )
-    packed = add_up(lhs, rhs)
-    for row in range(TALL):
-        part = packed[row * TALL : row * TALL + SENT]
+        lanes = slice(i * LANES, (i + 1) * LANES)
+        column = jnp.broadcast_to(columns[:, i : i + 1], (LANES, LANES)).astype(bf16)
         for half in range(2):
-            at = (2 * row + half) * SENT
-            send_out[at : at + SENT] = part[:, half * LANES : (half + 1) * LANES]
+            hit = column - half * LANES == place
+            rhs[lanes, half * LANES : (half + 1) * LANES] = jnp.where(hit, one, none)
+
+    depth, flow = depth_in[...], flow_in[...]
+    for (first, steps), owner, lhs in zip(PARTS, (owner_first, owner_last), (lhs_first, lhs_last)):
+        high_rows = TALL * steps
+        row_owners(owner, steps)
+        for substep in range(first, first + steps):
+            depth, flow = river_turn(substep, depth, flow)
+        if first:
+            depth_end[...] = depth
+            finished = pltpu.make_async_copy(depth_end, depth_out, arrivals.at[len(copies)])
+            finished.start()
+        for i in range(rows):
+            lanes = slice(i * LANES, (i + 1) * LANES)
+            high_label = address_out[i : i + 1] // WIDE
+            lay_out(series, first * rows + i, rows, steps, high_label, owner, lhs, lanes)
+            if not first:
+                cells = series[STEPS * rows + i : STEPS * rows + i + 1]
+                cells = jnp.where(number == high_label, cells, 0.0)
+                for half, part in enumerate(in_two(cells)):
+                    at = 2 * high_rows + half * TALL
+                    lhs[at : at + TALL, lanes] = part
+        both = jnp.dot(lhs[...], rhs[...], preferred_element_type=f32)
+        packed = both[:high_rows] + both[high_rows : 2 * high_rows]
+        for half in range(2):
+            lanes = slice(half * LANES, (half + 1) * LANES)
+            for row in range(TALL):
+                at = (2 * row + half) * SENT + first
+                send_out[at : at + steps] = packed[row * steps : (row + 1) * steps, lanes]
+            if not first:
+                cells = both[2 * high_rows : 2 * high_rows + TALL] + both[2 * high_rows + TALL :]
+                send_out[pl.ds(half * SENT + STEPS, TALL, stride=2 * SENT)] = cells[:, lanes]
     finished.wait()
 
 
 def reach_of(field):
     return STEPS - 1 - field if field < STEPS else HALO
+
+
+def turn(value, lanes):
+    lanes %= value.shape[1]
+    return value if lanes == 0 else pltpu.roll(value, lanes, 1)
 
 
 ROW_AT = [sum(reach_of(f) for f in range(field)) for field in range(FIELDS + 1)]
@@ -247,7 +296,7 @@
 def source_kernel(arrived, *refs):
     inputs, (fields, odd, even, rhs), refs = refs[:5], refs[5:9], refs[9:]
     first_of_pair = lax.axis_index("river") % 2 == 0
-    sea_level, sea_bed, wet_mask, flux_east, flux_north, arrivals, lhs, sums = refs
+    sea_level, sea_bed, wet_mask, flux_east, flux_north, arrivals, owner, lhs, sums = refs
     copies = [
         pltpu.make_async_copy(whole, own, arrivals.at[number])
         for number, (whole, own) in enumerate(zip(inputs, refs[:5]))
@@ -257,18 +306,25 @@
     groups = arrived.shape[0] // SENT
     tile_rows, tile_cols = sea_level.shape
 
-    def place(s, carry):
-        values = arrived[pl.ds(s * SENT, SENT)]
-        values = jnp.concatenate([values, jnp.zeros((TALL - SENT, LANES), f32)], axis=0)
-        cells = values[STEPS : STEPS + 1].astype(i32)
-        rows, columns = cell_labels(cells, tile_cols)
-        lay_out(values, rows, columns, lhs, rhs, pl.ds(pl.multiple_of(s * LANES, LANES), LANES))
-        return carry
-
-    lax.fori_loop(0, groups, place, 0, unroll=2)
-    total = add_up(lhs, rhs)
+    high_rows = TALL * STEPS
+    row_owners(owner, STEPS)
+    both = jnp.zeros((2 * high_rows, WIDE), f32)
+    for chunk in range(0, groups, CHUNK):
+        for s in range(chunk, chunk + CHUNK):
+            at = s * SENT
+            lanes = slice(s * LANES, (s + 1) * LANES)
+            cells = arrived[at + STEPS : at + SENT].astype(i32)
+            rows, columns = cell_labels(cells, tile_cols)
+            lay_out(arrived, at, 1, STEPS, rows, owner, lhs, lanes)
+            one_hot_columns(columns, rhs, lanes)
+        lanes = slice(chunk * LANES, (chunk + CHUNK) * LANES)
+        both = both + lax.dot_general(
+            lhs[:, lanes], rhs[:, lanes], (((1,), (1,)), ((), ())), preferred_element_type=f32
+        )
+    total = both[:high_rows] + both[high_rows:]
     for half in range(2):
-        sums[half * WIDE : (half + 1) * WIDE] = total[:, half * LANES : (half + 1) * LANES]
+        part = slice(half * high_rows, (half + 1) * high_rows)
+        sums[part] = total[:, half * LANES : (half + 1) * LANES]
     for copy in copies:
         copy.wait()
     bed = sea_bed[...]
@@ -286,7 +342,7 @@
     for swap_out in (odd, even):
         swap_out[ROWS_SENT - 8 :] = jnp.zeros((8, LANES), f32)
     for step in range(STEPS):
-        halves = [sums[pl.ds(half * WIDE + step, TALL, stride=TALL)] for half in range(2)]
+        halves = [sums[pl.ds(half * high_rows + step, TALL, stride=STEPS)] for half in range(2)]
         put(step, jnp.concatenate(halves, axis=0))
     for number, value in enumerate((level, bed, flux_east[...], flux_north[...])):
         put(STEPS + number, value)
@@ -299,32 +355,26 @@
     from_after = jnp.where(upper, from_even[...], from_odd[...])
     tile_rows = fields.shape[0] // FIELDS
     height = tall.shape[0] // FIELDS
-    per = LANES // STRIP
     lane = lax.broadcasted_iota(i32, (height, LANES), 1)
-    for group in range(FIELDS // per):
-        ends = jnp.zeros((height, LANES), f32)
-        starts = jnp.zeros((height, LANES), f32)
-        for place in range(per):
-            field = group * per + place
-            parts = [fields[field * tile_rows : (field + 1) * tile_rows]]
-            reach, at = reach_of(field), ROW_AT[field]
-            if reach:
-                parts.append(from_after[at : at + reach])
-            if reach < HALO:
-                parts.append(jnp.zeros((2 * HALO - 2 * reach, LANES), f32))
-            if reach:
-                parts.append(from_before[at : at + reach])
-            value = jnp.concatenate(parts, axis=0)
-            tall[field * height : (field + 1) * height] = value
-            here = lane // STRIP == place
-            shift = (place + 1) * STRIP % LANES
-            moved = value if shift == 0 else pltpu.roll(value, shift, 1)
-            ends = jnp.where(here, moved, ends)
-            moved = value if place == 0 else pltpu.roll(value, place * STRIP, 1)
-            starts = jnp.where(here, moved, starts)
-        part = slice(group * height, (group + 1) * height)
-        odd[part] = jnp.where(first_of_pair, starts, ends)
-        even[part] = jnp.where(first_of_pair, ends, starts)
+    ends = jnp.zeros((height, LANES), f32)
+    starts = jnp.zeros((height, LANES), f32)
+    for field in range(FIELDS):
+        reach, at = reach_of(field), ROW_AT[field]
+        parts = [fields[field * tile_rows : (field + 1) * tile_rows]]
+        if reach:
+            parts.append(from_after[at : at + reach])
+        if reach < HALO:
+            parts.append(jnp.zeros((2 * HALO - 2 * reach, LANES), f32))
+        if reach:
+            parts.append(from_before[at : at + reach])
+        value = jnp.concatenate(parts, axis=0)
+        tall[field * height : (field + 1) * height] = value
+        if reach:
+            here = (lane >= at) & (lane < at + reach)
+            ends = jnp.where(here, turn(value, at + reach - LANES), ends)
+            starts = jnp.where(here, turn(value, at), starts)
+    odd[...] = jnp.where(first_of_pair, starts, ends)
+    even[...] = jnp.where(first_of_pair, ends, starts)
 
 
 def ocean_kernel(
@@ -332,7 +382,6 @@
 ):
     height = tall.shape[0] // FIELDS
     width = 2 * LANES
-    per = LANES // STRIP
     river, coast = lax.axis_index("river"), lax.axis_index("coast")
     rivers, coasts = lax.axis_size("river"), lax.axis_size("coast")
     lane = lax.broadcasted_iota(i32, (height, LANES), 1)
@@ -340,13 +389,11 @@
     from_right = jnp.where(coast % 2 == 0, from_even[...], from_odd[...])
 
     def whole(field):
-        group, place = field // per, field % per
-        rows = slice(group * height, (group + 1) * height)
-        shift = (LANES - place * STRIP) % LANES
-        after = from_right[rows] if shift == 0 else pltpu.roll(from_right[rows], shift, 1)
-        shift = (LANES - (place + 1) * STRIP) % LANES
-        before = from_left[rows] if shift == 0 else pltpu.roll(from_left[rows], shift, 1)
-        beside = jnp.where(lane < STRIP, after, jnp.where(lane >= LANES - STRIP, before, 0.0))
+        reach, at = reach_of(field), ROW_AT[field]
+        beside = jnp.zeros((height, LANES), f32)
+        if reach:
+            beside = jnp.where(lane < reach, turn(from_right, -at), beside)
+            beside = jnp.where(lane >= LANES - reach, turn(from_left, -at - reach), beside)
         return jnp.concatenate([tall[field * height : (field + 1) * height], beside], axis=1)
 
     for step in range(STEPS):
@@ -373,8 +420,7 @@
     bed_north = jnp.maximum(bed, next_column(bed))
     drive = gravity * step_seconds / cell_metres
 
-    def ocean_turn(step, carry):
-        level, east, north = carry
+    def ocean_turn(first, steps, step, level, east, north):
         east = flow_after(east, level, next_row(level), bed_east, drive, ocean_manning)
         north = flow_after(north, level, next_column(level), bed_north, drive, ocean_manning)
         spread = east - pltpu.roll(east, 1, 0) + north - pltpu.roll(north, 1, 1)
@@ -382,57 +428,65 @@
         level = jnp.where(inside, level, 0.0)
         for half in range(2):
             part = level[half * TALL : (half + 1) * TALL, :LANES]
-            history[pl.ds(half * WIDE + step, TALL, stride=TALL)] = part
+            at = TALL * (2 * first + half * steps) + step - first
+            history[pl.ds(at, TALL, stride=steps)] = part
         return level, east, north
 
-    history[...] = jnp.zeros_like(history)
-    level, east, north = lax.fori_loop(0, STEPS, ocean_turn, (level, east, north))
-    level_out[...] = level[:tile_rows, :LANES]
-
-    halves = [history[:WIDE], history[WIDE:]]
-    table = jnp.concatenate(in_two(jnp.concatenate(halves, axis=1)), axis=1)
-
-    def reply(pair, carry):
-        at = [2 * pair, 2 * pair + 1]
-        cells = [arrived[pl.ds(s * SENT + STEPS, 1)] for s in at]
-        rows, _ = cell_labels(jnp.concatenate(cells, axis=1).astype(i32), LANES)
-        found = look_up(table, rows, hot[:, pl.ds(pl.multiple_of(pair * WIDE, WIDE), WIDE)])
-        for half, s in enumerate(at):
-            replies[pl.ds(s * STEPS, STEPS)] = found[:STEPS, half * LANES : (half + 1) * LANES]
-        return carry
-
-    lax.fori_loop(0, replies.shape[0] // STEPS // 2, reply, 0, unroll=2)
-
-
-def mouth_kernel(returned, address, level_out, table, series, hot):
+    for first, steps in PARTS:
+        high_rows = TALL * steps
+        for step in range(first, first + steps):
+            level, east, north = ocean_turn(first, steps, step, level, east, north)
+        if first:
+            level_out[...] = level[:tile_rows, :LANES]
+        at = 2 * TALL * first
+        halves = [history[at + half * high_rows : at + (half + 1) * high_rows] for half in range(2)]
+        table = jnp.concatenate(in_two(jnp.concatenate(halves, axis=1)), axis=0)
+        for s in range(0, replies.shape[0] // STEPS, 2):
+            cells = [arrived[(s + i) * SENT + STEPS : (s + i + 1) * SENT] for i in range(2)]
+            rows, _ = cell_labels(jnp.concatenate(cells, axis=1).astype(i32), LANES)
+            found = look_up(table, rows, hot[:, s * LANES : (s + 2) * LANES], steps)
+            for half in range(2):
+                at = (s + half) * STEPS + first
+                replies[at : at + steps] = found[:, half * LANES : (half + 1) * LANES]
+
+
+def mouth_kernel(returned, address, level_out, whole, series, hot, block, departures):
     rows = address.shape[0]
     groups = LANES // MPB
-    for row in range(TALL):
-        part = slice(row * TALL, (row + 1) * TALL)
-        for half in range(2):
-            at = (2 * row + half) * STEPS
-            values = returned[at : at + STEPS]
-            values = jnp.concatenate([values, jnp.zeros((TALL - STEPS, LANES), f32)], axis=0)
-            high, low = in_two(values)
-            table[part, half * LANES : (half + 1) * LANES] = high
-            table[part, WIDE + half * LANES : WIDE + (half + 1) * LANES] = low
+    labels = []
     for i in range(0, rows, 2):
-        labels = jnp.concatenate([address[i : i + 1], address[i + 1 : i + 2]], axis=1)
-        one_hot_columns(labels % WIDE, hot, slice(None))
-        found = look_up(table[...], labels // WIDE, hot[...])
-        series[pl.ds(i, TALL, stride=rows)] = found[:, :LANES]
-        series[pl.ds(i + 1, TALL, stride=rows)] = found[:, LANES:]
+        pair = jnp.concatenate([address[i : i + 1], address[i + 1 : i + 2]], axis=1)
+        one_hot_columns(pair % WIDE, hot, slice(i * LANES, (i + 2) * LANES))
+        labels.append(pair // WIDE)
     lane = lax.broadcasted_iota(i32, (rows, LANES), 1)
-    for block in range(STEPS // groups):
+    copies = []
+    for first in range(0, STEPS, groups):
+        for row in range(TALL):
+            for half in range(2):
+                at = (2 * row + half) * STEPS + first
+                to = first * TALL + row * groups
+                lanes = slice(half * LANES, (half + 1) * LANES)
+                whole[to : to + groups, lanes] = returned[at : at + groups]
+        own = whole[first * TALL : (first + groups) * TALL]
+        table = jnp.concatenate(in_two(own), axis=0)
+        for i in range(0, rows, 2):
+            lanes = slice(i * LANES, (i + 2) * LANES)
+            found = look_up(table, labels[i // 2], hot[:, lanes], groups)
+            series[pl.ds(first * rows + i, groups, stride=rows)] = found[:, :LANES]
+            series[pl.ds(first * rows + i + 1, groups, stride=rows)] = found[:, LANES:]
+        number = first // groups
         for g in range(groups):
             result = jnp.zeros((rows, LANES), f32)
             for place in range(groups):
-                step = block * groups + place
-                part = series[step * rows : (step + 1) * rows]
-                shift = (place - g) * MPB % LANES
-                part = part if shift == 0 else pltpu.roll(part, shift, 1)
+                at = (first + place) * rows
+                part = turn(series[at : at + rows], (place - g) * MPB)
                 result = jnp.where(lane // MPB == place, part, result)
-            level_out[g * rows : (g + 1) * rows, block * LANES : (block + 1) * LANES] = result
+            block[number, g * rows : (g + 1) * rows] = result
+        to = level_out.at[:, pl.ds(number * LANES, LANES)]
+        copies.append(pltpu.make_async_copy(block.at[number], to, departures.at[number]))
+        copies[-1].start()
+    for copy in copies:
+        copy.wait()
 
 
 def shape(*dims, dtype=f32):
@@ -512,12 +566,14 @@
             pltpu.SemaphoreType.DMA((11,)),
             pltpu.VMEM((blocks, RB), f32),
             pltpu.VMEM((reach_offsets, blocks, RB), f32),
-            pltpu.VMEM((TALL * rows, LANES), f32),
+            pltpu.VMEM((SENT * rows, LANES), f32),
             pltpu.VMEM((RB, LANES), f32),
             pltpu.VMEM((rows, LANES), i32),
             pltpu.VMEM((rows * devices, LANES), bf16),
-            pltpu.VMEM((2 * WIDE, mouths), bf16),
-            pltpu.VMEM((WIDE, mouths), bf16),
+            *[pltpu.VMEM((TALL * steps, LANES), bf16) for _, steps in PARTS],
+            pltpu.VMEM((2 * TALL * (PARTS[0][1] + 1), mouths), bf16),
+            pltpu.VMEM((2 * TALL * PARTS[1][1], mouths), bf16),
+            pltpu.VMEM((mouths, WIDE), bf16),
         ],
         compiler_params=PARAMS,
     )(
@@ -554,18 +610,18 @@
             pltpu.VMEM((tile_rows, tile_cols), f32),
             pltpu.VMEM((tile_rows, tile_cols), f32),
             pltpu.SemaphoreType.DMA((5,)),
-            pltpu.VMEM((2 * WIDE, groups * LANES), bf16),
-            pltpu.VMEM((2 * WIDE, LANES), f32),
+            pltpu.VMEM((TALL * STEPS, LANES), bf16),
+            pltpu.VMEM((2 * TALL * STEPS, groups * LANES), bf16),
+            pltpu.VMEM((2 * TALL * STEPS, LANES), f32),
         ],
         compiler_params=PARAMS,
     )(arrived, *in_hbm(sea_level, sea_bed, wet_mask, flux_east, flux_north))
     from_odd, from_even = with_neighbours(odd, even, "river")
 
-    strips = FIELDS * STRIP // LANES * height
     tall, odd, even = pl.pallas_call(
         strip_kernel,
         name="strips",
-        out_shape=(shape(FIELDS * height, LANES), shape(strips, LANES), shape(strips, LANES)),
+        out_shape=(shape(FIELDS * height, LANES), shape(height, LANES), shape(height, LANES)),
         compiler_params=PARAMS,
     )(fields, from_odd, from_even)
     from_odd, from_even = with_neighbours(odd, even, "coast")
@@ -576,7 +632,7 @@
         out_shape=(shape(tile_rows, tile_cols), shape(groups * STEPS, LANES)),
         scratch_shapes=[
             pltpu.VMEM((STEPS, height, 2 * LANES), f32),
-            pltpu.VMEM((2 * WIDE, LANES), f32),
+            pltpu.VMEM((2 * TALL * STEPS, LANES), f32),
         ],
         compiler_params=PARAMS,
     )(tall, from_odd, from_even, arrived, hot)
@@ -587,10 +643,13 @@
         name="mouths",
         out_shape=shape(blocks, STEPS * MPB),
         scratch_shapes=[
-            pltpu.VMEM((WIDE, 2 * WIDE), bf16),
-            pltpu.VMEM((TALL * rows, LANES), f32),
-            pltpu.VMEM((WIDE, WIDE), bf16),
+            pltpu.VMEM((TALL * STEPS, WIDE), f32),
+            pltpu.VMEM((STEPS * rows, LANES), f32),
+            pltpu.VMEM((WIDE, mouths), bf16),
+            pltpu.VMEM((STEPS * MPB // LANES, blocks, LANES), f32),
+            pltpu.SemaphoreType.DMA((STEPS * MPB // LANES,)),
         ],
+        out_specs=pl.BlockSpec(memory_space=pltpu.HBM),
         compiler_params=PARAMS,
     )(returned, address)
     return (depth_after, level_after, mouth_level)

time: 58.7 us -> 55 us (0.937)
  Pallas kernels: 17.2 us -> 13.8 us
    pallas_call x1, Pallas kernels: 5.61 us -> 3.29 us  [per_device(): pl.pallas_call(functools.partial(ocean_kernel, tile_rows), name='ocean',...]
    pallas_call x1, Pallas kernels: 3.41 us -> 2.59 us  [per_device(): pl.pallas_call(source_kernel, name='sources', out_shape=(shape(FIELDS * t...]
where the time goes in v2:
time: 55 us; the launch traced here: 54.4 us
  blocking collectives  28.7 us (52%)
  Pallas kernels  13.8 us (25%)
  starting transfers between devices  6.96 us (13%)
  waiting for transfers between devices  4.25 us (8%)
  between operations  0.69 us (1%)
    all_to_all x2, blocking collectives, swap(): lax.all_to_all(values, ('river', 'coast'), split_axis=0, concat_axis=0, t...  28.7 us
    pallas_call x1, Pallas kernels, per_device(): pl.pallas_call(functools.partial(river_kernel, devices, capacity), name='...  6.23 us
    ppermute x2, starting transfers between devices, with_neighbours(): lax.ppermute(even, axis, routes[1])  3.83 us
    pallas_call x1, Pallas kernels, per_device(): pl.pallas_call(functools.partial(ocean_kernel, tile_rows), name='ocean',...  3.29 us
    ppermute x2, starting transfers between devices, with_neighbours(): lax.ppermute(odd, axis, routes[0])  3.13 us
    ppermute x2, waiting for transfers between devices, with_neighbours(): lax.ppermute(odd, axis, routes[0])  2.99 us
    pallas_call x1, Pallas kernels, per_device(): pl.pallas_call(source_kernel, name='sources', out_shape=(shape(FIELDS * t...  2.59 us
    pallas_call x1, Pallas kernels, per_device(): pl.pallas_call(mouth_kernel, name='mouths', out_shape=shape(blocks, STEPS...  1.37 us
  transfers between devices with their start and end apart: 4, of which 2 were waited for; matrix products, arithmetic and copies ran while one was open for 0% of the time, Pallas kernels for 0%

profile of v2, /device:TPU:1, one launch (start us, length us, event | category | flops | bytes accessed | tf_op | source)
XLA Modules:
  0.0 54.4 jit_solution(13950809555760254719)
XLA Ops:
  0.6 6.2 %river.1 = (f32[64,128]{1,0:T(8,128)}, f32[416,128]{1,0:T(8,128)S(1)}, s32[16,128]{1,0:T(8,128)S(1)}) custom-call(f32[64,128]{1,0:T(8,128)} %refs_0_.2, f32[64,128]{1,0:T(8,128)} %refs_1_.2, f32[64,128]{1,0:T(8,128)} %refs_2_.2, f32[64,128]{1,0:T(8,128)} %refs_3_.2, f32[64,128]{1,0:T(8,128)} %refs_4_.2, f32[64,128]{1,0:T(8,128)} %refs_5_.1, ...), custom_call_target="tpu_custom_call" | custom-call | tf_op jit(solution)/shard_map/river/pallas_call | solution.py:546
  6.9 15.8 %all_to_all.10 = f32[32,1,1664]{2,1,0:T(1,128)S(1)} all-to-all(f32[32,1,1664]{2,1,0:T(1,128)S(1)} %bitcast.12), channel_id=1, replica_groups=mesh['river'=4,'coast'=8] {'river','coast'}, dimensions={0} | all-to-all | bytes 425984 | tf_op jit(solution)/shard_map/all_to_all | solution.py:505
  22.7 2.6 %sources.1 = (f32[512,128]{1,0:T(8,128)S(1)}, f32[120,128]{1,0:T(8,128)S(1)}, f32[120,128]{1,0:T(8,128)S(1)}, bf16[256,4096]{1,0:T(8,128)(2,1)S(1)}) custom-call(f32[416,128]{1,0:T(8,128)S(1)} %bitcast.9, f32[32,128]{1,0:T(8,128)} %refs_0_.3, f32[32,128]{1,0:T(8,128)} %refs_1_.3, s32[32,128]{1,0:T(8,128)} %refs_2_.3, f32[32,128]{1,0:T(8,128)} %refs_3_.3, ...), custom_call_target="tpu_custom_call" | custom-call | tf_op jit(solution)/shard_map/sources/pallas_call | solution.py:595
  25.3 2.5 %collective-permute-start = (f32[120,128]{1,0:T(8,128)S(1)}, f32[120,128]{1,0:T(8,128)S(1)}, u32[]{:S(2)}, u32[]{:S(2)}) collective-permute-start(f32[120,128]{1,0:T(8,128)S(1)} %get-tuple-element.18), channel_id=1, source_target_pairs={{8,16},{16,8},{9,17},{17,9},{10,18},{18,10},{11,19},{19,11},{12,20... | collective-permute-start | bytes 184328 | tf_op jit(solution)/shard_map/ppermute | solution.py:517
  27.8 0.1 collective-permute-start.1
  27.8 3.0 %collective-permute-done.from_odd = f32[120,128]{1,0:T(8,128)S(1)} collective-permute-done((f32[120,128]{1,0:T(8,128)S(1)}, f32[120,128]{1,0:T(8,128)S(1)}, u32[]{:S(2)}, u32[]{:S(2)}) %collective-permute-start) | collective-permute-done | bytes 61472 | tf_op jit(solution)/shard_map/ppermute | solution.py:517
  30.8 0.0 collective-permute-done.1.from_even
  30.8 0.3 strips.1
  31.1 0.7 %collective-permute-start.2 = (f32[56,128]{1,0:T(8,128)S(1)}, f32[56,128]{1,0:T(8,128)S(1)}, u32[]{:S(2)}, u32[]{:S(2)}) collective-permute-start(f32[56,128]{1,0:T(8,128)S(1)} %get-tuple-element.21), channel_id=1, source_target_pairs={{1,2},{2,1},{3,4},{4,3},{5,6},{6,5},{9,10},{10,9},{11,12},{12,11},... | collective-permute-start | bytes 86024 | tf_op jit(solution)/shard_map/ppermute | solution.py:517
  31.8 3.8 %collective-permute-start.3 = (f32[56,128]{1,0:T(8,128)S(1)}, f32[56,128]{1,0:T(8,128)S(1)}, u32[]{:S(2)}, u32[]{:S(2)}) collective-permute-start(f32[56,128]{1,0:T(8,128)S(1)} %get-tuple-element.22), channel_id=1, source_target_pairs={{0,1},{1,0},{2,3},{3,2},{4,5},{5,4},{6,7},{7,6},{8,9},{9,8},{10,11... | collective-permute-start | bytes 86024 | tf_op jit(solution)/shard_map/ppermute | solution.py:517
  35.5 0.0 collective-permute-done.2.from_odd
  35.5 1.3 %collective-permute-done.3.from_even = f32[56,128]{1,0:T(8,128)S(1)} collective-permute-done((f32[56,128]{1,0:T(8,128)S(1)}, f32[56,128]{1,0:T(8,128)S(1)}, u32[]{:S(2)}, u32[]{:S(2)}) %collective-permute-start.3) | collective-permute-done | bytes 28704 | tf_op jit(solution)/shard_map/ppermute | solution.py:517
  36.8 3.3 %ocean.1 = (f32[32,128]{1,0:T(8,128)}, f32[384,128]{1,0:T(8,128)S(1)}) custom-call(f32[896,128]{1,0:T(8,128)S(1)} %get-tuple-element.20.tall, f32[56,128]{1,0:T(8,128)S(1)} %collective-permute-done.2.from_odd, f32[56,128]{1,0:T(8,128)S(1)} %collective-permute-done.3.from_even, f32[416,128]{1,0:T(8,128)S(1)} %bitcast.10, ...), custom_call_target="tpu_custom_call" | custom-call | tf_op jit(solution)/shard_map/ocean/pallas_call | solution.py:629
  40.1 12.9 %all_to_all.11 = f32[32,1,1536]{2,1,0:T(1,128)S(1)} all-to-all(f32[32,1,1536]{2,1,0:T(1,128)S(1)} %bitcast.13), channel_id=1, replica_groups=mesh['river'=4,'coast'=8] {'river','coast'}, dimensions={0} | all-to-all | bytes 393216 | tf_op jit(solution)/shard_map/all_to_all | solution.py:505
  53.0 1.4 %mouths.1 = f32[64,384]{1,0:T(8,128)} custom-call(f32[384,128]{1,0:T(8,128)S(1)} %bitcast.11, s32[16,128]{1,0:T(8,128)S(1)} %get-tuple-element.26.address), custom_call_target="tpu_custom_call" | custom-call | tf_op jit(solution)/shard_map/mouths/pallas_call | solution.py:641
Async XLA Ops:
  25.3 5.5 %collective-permute-start = (f32[120,128]{1,0:T(8,128)S(1)}, f32[120,128]{1,0:T(8,128)S(1)}, u32[]{:S(2)}, u32[]{:S(2)}) collective-permute-start(f32[120,128]{1,0:T(8,128)S(1)} %get-tuple-element.18), channel_id=1, source_target_pairs={{8,16},{16,8},{9,17},{17,9},{10,18},{18,10},{11,19},{19,11},{12,20... | collective-permute-start | bytes 184328 | tf_op jit(solution)/shard_map/ppermute | solution.py:517
  27.8 3.1 %collective-permute-start.1 = (f32[120,128]{1,0:T(8,128)S(1)}, f32[120,128]{1,0:T(8,128)S(1)}, u32[]{:S(2)}, u32[]{:S(2)}) collective-permute-start(f32[120,128]{1,0:T(8,128)S(1)} %get-tuple-element.19), channel_id=1, source_target_pairs={{0,8},{8,0},{16,24},{24,16},{1,9},{9,1},{17,25},{25,17},{2,10},{10... | collective-permute-start | bytes 184328 | tf_op jit(solution)/shard_map/ppermute | solution.py:517
  31.1 4.4 %collective-permute-start.2 = (f32[56,128]{1,0:T(8,128)S(1)}, f32[56,128]{1,0:T(8,128)S(1)}, u32[]{:S(2)}, u32[]{:S(2)}) collective-permute-start(f32[56,128]{1,0:T(8,128)S(1)} %get-tuple-element.21), channel_id=1, source_target_pairs={{1,2},{2,1},{3,4},{4,3},{5,6},{6,5},{9,10},{10,9},{11,12},{12,11},... | collective-permute-start | bytes 86024 | tf_op jit(solution)/shard_map/ppermute | solution.py:517
  31.8 5.0 %collective-permute-start.3 = (f32[56,128]{1,0:T(8,128)S(1)}, f32[56,128]{1,0:T(8,128)S(1)}, u32[]{:S(2)}, u32[]{:S(2)}) collective-permute-start(f32[56,128]{1,0:T(8,128)S(1)} %get-tuple-element.22), channel_id=1, source_target_pairs={{0,1},{1,0},{2,3},{3,2},{4,5},{5,4},{6,7},{7,6},{8,9},{9,8},{10,11... | collective-permute-start | bytes 86024 | tf_op jit(solution)/shard_map/ppermute | solution.py:517

commit v3 on v2

--- a/solution.py
+++ b/solution.py
@@ -24,7 +24,8 @@
 SENT = 13
 TALL = 16
 WIDE = 256
-PARTS = ((0, 8), (8, 4))
+PARTS = ((0, 8), (8, 2), (10, 2))
+LOOKED_UP = ((0, 8), (8, 4))
 CHUNK = 8
 HALO = 12
 FIELDS = 16
@@ -41,8 +42,7 @@
     friction = (gravity * step_seconds * manning * manning) * jnp.abs(unit_flow) * thin
     divisor = 1.0 + friction
     inverse = pl.reciprocal(divisor, approx=True)
-    inverse = inverse * (2.0 - divisor * inverse)
-    return (unit_flow + driving) * inverse
+    return ((unit_flow + driving) * inverse) * (2.0 - divisor * inverse)
 
 
 def in_two(values):
@@ -51,20 +51,19 @@
 
 
 def small(labels):
-    return jnp.broadcast_to(labels.astype(f32), (TALL, labels.shape[1])).astype(bf16)
-
-
-def one_hot_columns(columns, rhs, lanes):
+    return jnp.broadcast_to(labels, (TALL, labels.shape[1])).astype(bf16)
+
+
+def one_hot_columns(columns, place_of, rhs, lanes):
     labels = small(columns)
-    place = lax.broadcasted_iota(i32, labels.shape, 0).astype(f32).astype(bf16)
     one, none = jnp.ones(labels.shape, bf16), jnp.zeros(labels.shape, bf16)
-    for part in range(WIDE // TALL):
-        hit = labels - part * TALL == place
-        rhs[part * TALL : (part + 1) * TALL, lanes] = jnp.where(hit, one, none)
+    for part in range(0, WIDE, TALL):
+        hit = place_of(labels, part)
+        rhs[part : part + TALL, lanes] = jnp.where(hit, one, none)
 
 
 def row_owners(owner, steps):
-    for part in range(0, TALL * steps, TALL):
+    for part in range(0, owner.shape[0], TALL):
         number = part + lax.broadcasted_iota(i32, (TALL, LANES), 0)
         owner[part : part + TALL] = (number // steps).astype(f32).astype(bf16)
 
@@ -98,7 +97,8 @@
     found = jnp.dot(table, hot, preferred_element_type=f32)
     per = 2 if steps > 6 else 4
     several = (per * steps, rows.shape[1])
-    labels = jnp.broadcast_to(rows, several) - lax.broadcasted_iota(i32, several, 0) // steps
+    number = (lax.broadcasted_iota(i32, several, 0) // steps).astype(f32)
+    labels = jnp.broadcast_to(rows, several) - number
     total = jnp.zeros(several, f32)
     for row in range(0, TALL, per):
         high = found[row * steps : (row + per) * steps]
@@ -110,13 +110,19 @@
     return result
 
 
+def split_label(number, size):
+    return lax.shift_right_logical(number, size.bit_length() - 1), number & (size - 1)
+
+
 def cell_labels(cells, tile_cols):
-    row, column = cells // tile_cols, cells % tile_cols
-    return row % TALL, row // TALL * tile_cols + column
+    row, column = split_label(cells, tile_cols)
+    upper, row = split_label(row, TALL)
+    return row, upper * tile_cols + column
 
 
 def river_kernel(
     devices,
+    coasts,
     capacity,
     *refs,
 ):
@@ -127,11 +133,12 @@
     ]
     for copy in copies[::-1]:
         copy.start()
-    river_steps(devices, capacity, copies, *refs[:10], depth_out, send_out, address_out, *refs[10:])
+    river_steps(devices, coasts, capacity, copies, *refs[:10], depth_out, send_out, address_out, *refs[10:])
 
 
 def river_steps(
     devices,
+    coasts,
     capacity,
     copies,
     depth_in,
@@ -154,19 +161,20 @@
     turned,
     tiles,
     hots,
-    owner_first,
-    owner_last,
-    lhs_first,
-    lhs_last,
+    counted,
+    high_labels,
+    low_labels,
     rhs,
+    *parts,
 ):
+    owners, slots = parts[: len(PARTS)], parts[len(PARTS) :]
     blocks = depth_in.shape[0]
     groups = LANES // MPB
     rows = blocks // groups
     inland = RB - MPB
     lane = lax.broadcasted_iota(i32, (blocks, RB), 1)
 
-    for copy in copies[7:]:
+    for copy in copies:
         copy.wait()
 
     turned[...] = jnp.zeros_like(turned)
@@ -186,87 +194,100 @@
             result = jnp.where(lanes16 // MPB == g, part, result)
         return result
 
-    tiles[...] = grouped(mouths, 0).astype(i32)
+    tile = grouped(mouths, 0).astype(i32)
+    tiles[...] = tile % coasts * (devices // coasts) + tile // coasts
     series[STEPS * rows :] = grouped(mouths, MPB)
 
-    for i in range(rows):
-        names = jnp.broadcast_to(tiles[i : i + 1], (devices, LANES))
-        hit = names == lax.broadcasted_iota(i32, (devices, LANES), 0)
-        hots[i * devices : (i + 1) * devices] = jnp.where(hit, 1.0, 0.0).astype(bf16)
-    shape = (LANES, 2 * LANES)
-    earlier = lax.broadcasted_iota(i32, shape, 0) < lax.broadcasted_iota(i32, shape, 1)
-    counted = jnp.dot(
-        hots[...], jnp.where(earlier, 1.0, 0.0).astype(bf16), preferred_element_type=f32
-    )
-    before = jnp.zeros((devices, LANES), f32)
-    for i in range(rows):
-        part = slice(i * devices, (i + 1) * devices)
-        ranks = (counted[part, :LANES] + before) * hots[part].astype(f32)
-        rank = jnp.sum(ranks, axis=0, keepdims=True).astype(i32)
-        address_out[i : i + 1] = tiles[i : i + 1] * capacity + rank
-        before = before + counted[part, LANES:]
-
-    for copy in copies[:7]:
-        copy.wait()
     into = into_in[...]
     at_mouth = lane >= inland
     down = jnp.where(at_mouth, 0, into)
     offset = jnp.where(at_mouth, 0, into - lane)
     bed = bed_in[...]
     bed_top = jnp.where(
-        at_mouth, bed, jnp.maximum(bed, jnp.take_along_axis(bed, down, axis=1))
+        at_mouth, bed, jnp.maximum(bed, jnp.take_along_axis(bed, down, axis=1, mode="promise_in_bounds"))
     )
     drive = gravity * step_seconds / length_in[...]
-    area = step_seconds / (width_in[...] * length_in[...])
-    for o in range(1, reach_offsets + 1):
-        enters[o - 1] = jnp.where(turn(offset, o) == o, 1.0, 0.0)
+    width = width_in[...]
+    area = step_seconds / (width * length_in[...])
+    gain = area * runoff_in[...]
+    loss = area * width
+    moved = [(turn(offset, 1 + b), turn(width, 1 + b)) for b in range(4)]
+    for o in range(reach_offsets):
+        where_to, its_width = moved[o % 4]
+        weight = its_width * turn(area, -(o - o % 4))
+        enters[o] = jnp.where(where_to == o + 1, weight, 0.0)
 
     def river_turn(substep, depth, flow):
         surface = bed + depth
-        below = jnp.where(at_mouth, prev, jnp.take_along_axis(surface, down, axis=1))
+        below = jnp.where(at_mouth, prev, jnp.take_along_axis(surface, down, axis=1, mode="promise_in_bounds"))
         flow = flow_after(flow, surface, below, bed_top, drive, river_manning)
-        discharge = flow * width_in[...]
-        sums = [
-            enters[o] * turn(discharge, o + 1) + enters[o + 1] * turn(discharge, o + 2)
-            for o in range(0, reach_offsets, 2)
-        ]
-        while len(sums) > 1:
-            sums = [one + other for one, other in zip(sums[::2], sums[1::2])]
-        depth = depth + area * (sums[0] + (runoff_in[...] - discharge))
-        series[substep * rows : (substep + 1) * rows] = grouped(discharge, inland)
+        moved = [turn(flow, 1 + b) for b in range(4)]
+        sums = []
+        for a in range(0, reach_offsets, 4):
+            one, other = [
+                enters[a + b] * moved[b] + enters[a + b + 1] * moved[b + 1] for b in (0, 2)
+            ]
+            sums.append(turn(one + other, a))
+        inflow = (sums[0] + sums[1]) + (sums[2] + sums[3])
+        depth = (depth + gain - loss * flow) + inflow
+        series[substep * rows : (substep + 1) * rows] = grouped(flow * width, inland)
         return depth, flow
 
-    columns = jnp.transpose((address_out[...] % WIDE).astype(f32))
-    place = lax.broadcasted_iota(i32, (LANES, LANES), 1).astype(f32).astype(bf16)
+    def count_mouths():
+        for i in range(rows):
+            names = jnp.broadcast_to(tiles[i : i + 1], (devices, LANES))
+            hit = names == lax.broadcasted_iota(i32, (devices, LANES), 0)
+            hots[i * devices : (i + 1) * devices] = jnp.where(hit, 1.0, 0.0).astype(bf16)
+        shape = (LANES, 2 * LANES)
+        earlier = lax.broadcasted_iota(i32, shape, 0) < lax.broadcasted_iota(i32, shape, 1)
+        counted[...] = jnp.dot(
+            hots[...], jnp.where(earlier, 1.0, 0.0).astype(bf16), preferred_element_type=f32
+        )
+
+    def rank_mouths():
+        before = jnp.zeros((devices, LANES), f32)
+        for i in range(rows):
+            part = slice(i * devices, (i + 1) * devices)
+            ranks = (counted[part, :LANES] + before) * hots[part].astype(f32)
+            rank = jnp.sum(ranks, axis=0, keepdims=True).astype(i32)
+            address_out[i : i + 1] = tiles[i : i + 1] * capacity + rank
+            before = before + counted[part, LANES:]
+
     one, none = jnp.ones((LANES, LANES), bf16), jnp.zeros((LANES, LANES), bf16)
-    number = lax.broadcasted_iota(i32, (TALL, LANES), 0)
-    for i in range(rows):
-        lanes = slice(i * LANES, (i + 1) * LANES)
-        column = jnp.broadcast_to(columns[:, i : i + 1], (LANES, LANES)).astype(bf16)
-        for half in range(2):
-            hit = column - half * LANES == place
-            rhs[lanes, half * LANES : (half + 1) * LANES] = jnp.where(hit, one, none)
-
-    depth, flow = depth_in[...], flow_in[...]
-    for (first, steps), owner, lhs in zip(PARTS, (owner_first, owner_last), (lhs_first, lhs_last)):
+    number = lax.broadcasted_iota(i32, (TALL, LANES), 0).astype(f32)
+
+    def label_mouths():
+        high, low = split_label(address_out[...], WIDE)
+        high_labels[...] = high.astype(f32)
+        low_labels[...] = jnp.transpose(low.astype(f32))
+
+    def slot_columns(group):
+        place = lax.broadcasted_iota(i32, (LANES, LANES), 1).astype(f32).astype(bf16)
+        for i in range(group * rows // 4, (group + 1) * rows // 4):
+            lanes = slice(i * LANES, (i + 1) * LANES)
+            column = jnp.broadcast_to(low_labels[:, i : i + 1], (LANES, LANES)).astype(bf16)
+            for half in range(2):
+                hit = column - half * LANES == place
+                rhs[lanes, half * LANES : (half + 1) * LANES] = jnp.where(hit, one, none)
+
+    def place_series(part, group):
+        first, steps = PARTS[part]
+        owner, lhs = owners[part], slots[part]
+        for i in range(group * rows // 4, (group + 1) * rows // 4):
+            lanes = slice(i * LANES, (i + 1) * LANES)
+            labels = high_labels[i : i + 1]
+            lay_out(series, first * rows + i, rows, steps, labels, owner, lhs, lanes)
+            if part == 0:
+                cells = series[STEPS * rows + i : STEPS * rows + i + 1]
+                cells = jnp.where(number == labels, cells, 0.0)
+                for half, value in enumerate(in_two(cells)):
+                    at = 2 * TALL * steps + half * TALL
+                    lhs[at : at + TALL, lanes] = value
+
+    def pack(part):
+        first, steps = PARTS[part]
         high_rows = TALL * steps
-        row_owners(owner, steps)
-        for substep in range(first, first + steps):
-            depth, flow = river_turn(substep, depth, flow)
-        if first:
-            depth_end[...] = depth
-            finished = pltpu.make_async_copy(depth_end, depth_out, arrivals.at[len(copies)])
-            finished.start()
-        for i in range(rows):
-            lanes = slice(i * LANES, (i + 1) * LANES)
-            high_label = address_out[i : i + 1] // WIDE
-            lay_out(series, first * rows + i, rows, steps, high_label, owner, lhs, lanes)
-            if not first:
-                cells = series[STEPS * rows + i : STEPS * rows + i + 1]
-                cells = jnp.where(number == high_label, cells, 0.0)
-                for half, part in enumerate(in_two(cells)):
-                    at = 2 * high_rows + half * TALL
-                    lhs[at : at + TALL, lanes] = part
+        lhs = slots[part]
         both = jnp.dot(lhs[...], rhs[...], preferred_element_type=f32)
         packed = both[:high_rows] + both[high_rows : 2 * high_rows]
         for half in range(2):
@@ -274,9 +295,30 @@
             for row in range(TALL):
                 at = (2 * row + half) * SENT + first
                 send_out[at : at + steps] = packed[row * steps : (row + 1) * steps, lanes]
-            if not first:
+            if part == 0:
                 cells = both[2 * high_rows : 2 * high_rows + TALL] + both[2 * high_rows + TALL :]
                 send_out[pl.ds(half * SENT + STEPS, TALL, stride=2 * SENT)] = cells[:, lanes]
+
+    beside = {0: [count_mouths], 1: [rank_mouths], 2: [label_mouths]}
+    beside |= {3 + group: [functools.partial(slot_columns, group)] for group in range(4)}
+    beside |= {8: [functools.partial(place_series, 0, group) for group in range(2)]}
+    beside |= {9: [functools.partial(place_series, 0, group) for group in range(2, 4)]}
+    beside |= {10: [functools.partial(pack, 0)]}
+    beside[10] += [functools.partial(place_series, 1, group) for group in range(4)]
+    beside |= {11: [functools.partial(pack, 1)]}
+    for owner, (_, steps) in zip(owners, PARTS):
+        row_owners(owner, steps)
+    depth, flow = depth_in[...], flow_in[...]
+    for substep in range(STEPS):
+        depth, flow = river_turn(substep, depth, flow)
+        for work in beside.get(substep, []):
+            work()
+    depth_end[...] = depth
+    finished = pltpu.make_async_copy(depth_end, depth_out, arrivals.at[len(copies)])
+    finished.start()
+    for group in range(4):
+        place_series(2, group)
+    pack(2)
     finished.wait()
 
 
@@ -294,9 +336,9 @@
 
 
 def source_kernel(arrived, *refs):
-    inputs, (fields, odd, even, rhs), refs = refs[:5], refs[5:9], refs[9:]
+    inputs, (fields, odd, even, rhs, label_out), refs = refs[:5], refs[5:10], refs[10:]
     first_of_pair = lax.axis_index("river") % 2 == 0
-    sea_level, sea_bed, wet_mask, flux_east, flux_north, arrivals, owner, lhs, sums = refs
+    sea_level, sea_bed, wet_mask, flux_east, flux_north, arrivals, owner, places, labels, lhs, sums = refs
     copies = [
         pltpu.make_async_copy(whole, own, arrivals.at[number])
         for number, (whole, own) in enumerate(zip(inputs, refs[:5]))
@@ -308,15 +350,27 @@
 
     high_rows = TALL * STEPS
     row_owners(owner, STEPS)
+    row_owners(places, 1)
+
+    def place_of(label, part):
+        return label == places[part : part + TALL]
+
+    cells = arrived[pl.ds(STEPS, groups, stride=SENT)].astype(i32)
+    for number, label in enumerate(cell_labels(cells, tile_cols)):
+        labels[number * groups : (number + 1) * groups] = label.astype(f32)
+    label_out[...] = labels[:groups]
+
+    def place(chunk):
+        for s in range(chunk, chunk + CHUNK):
+            lanes = slice(s * LANES, (s + 1) * LANES)
+            lay_out(arrived, s * SENT, 1, STEPS, labels[s : s + 1], owner, lhs, lanes)
+            one_hot_columns(labels[groups + s : groups + s + 1], place_of, rhs, lanes)
+
     both = jnp.zeros((2 * high_rows, WIDE), f32)
+    place(0)
     for chunk in range(0, groups, CHUNK):
-        for s in range(chunk, chunk + CHUNK):
-            at = s * SENT
-            lanes = slice(s * LANES, (s + 1) * LANES)
-            cells = arrived[at + STEPS : at + SENT].astype(i32)
-            rows, columns = cell_labels(cells, tile_cols)
-            lay_out(arrived, at, 1, STEPS, rows, owner, lhs, lanes)
-            one_hot_columns(columns, rhs, lanes)
+        if chunk + CHUNK < groups:
+            place(chunk + CHUNK)
         lanes = slice(chunk * LANES, (chunk + CHUNK) * LANES)
         both = both + lax.dot_general(
             lhs[:, lanes], rhs[:, lanes], (((1,), (1,)), ((), ())), preferred_element_type=f32
@@ -378,7 +432,7 @@
 
 
 def ocean_kernel(
-    tile_rows, tall, from_odd, from_even, arrived, hot, level_out, replies, sources, history
+    tile_rows, tall, from_odd, from_even, row_labels, hot, level_out, replies, history
 ):
     height = tall.shape[0] // FIELDS
     width = 2 * LANES
@@ -396,8 +450,6 @@
             beside = jnp.where(lane >= LANES - reach, turn(from_left, -at - reach), beside)
         return jnp.concatenate([tall[field * height : (field + 1) * height], beside], axis=1)
 
-    for step in range(STEPS):
-        sources[step] = whole(step) * (step_seconds / (cell_metres * cell_metres))
     level, bed, east, north = [whole(STEPS + number) for number in range(4)]
 
     row = lax.broadcasted_iota(i32, (height, width), 0)
@@ -421,10 +473,11 @@
     drive = gravity * step_seconds / cell_metres
 
     def ocean_turn(first, steps, step, level, east, north):
+        source = whole(step) * (step_seconds / (cell_metres * cell_metres))
         east = flow_after(east, level, next_row(level), bed_east, drive, ocean_manning)
         north = flow_after(north, level, next_column(level), bed_north, drive, ocean_manning)
         spread = east - pltpu.roll(east, 1, 0) + north - pltpu.roll(north, 1, 1)
-        level = level - step_seconds / cell_metres * spread + sources[step]
+        level = level - step_seconds / cell_metres * spread + source
         level = jnp.where(inside, level, 0.0)
         for half in range(2):
             part = level[half * TALL : (half + 1) * TALL, :LANES]
@@ -432,32 +485,46 @@
             history[pl.ds(at, TALL, stride=steps)] = part
         return level, east, north
 
-    for first, steps in PARTS:
-        high_rows = TALL * steps
-        for step in range(first, first + steps):
-            level, east, north = ocean_turn(first, steps, step, level, east, north)
-        if first:
-            level_out[...] = level[:tile_rows, :LANES]
-        at = 2 * TALL * first
+    def table_of(first, steps):
+        high_rows, at = TALL * steps, 2 * TALL * first
         halves = [history[at + half * high_rows : at + (half + 1) * high_rows] for half in range(2)]
-        table = jnp.concatenate(in_two(jnp.concatenate(halves, axis=1)), axis=0)
-        for s in range(0, replies.shape[0] // STEPS, 2):
-            cells = [arrived[(s + i) * SENT + STEPS : (s + i + 1) * SENT] for i in range(2)]
-            rows, _ = cell_labels(jnp.concatenate(cells, axis=1).astype(i32), LANES)
+        return jnp.concatenate(in_two(jnp.concatenate(halves, axis=1)), axis=0)
+
+    def reply(table, first, steps, group, of):
+        count = replies.shape[0] // STEPS // of
+        for s in range(group * count, (group + 1) * count, 2):
+            rows = jnp.concatenate([row_labels[s : s + 1], row_labels[s + 1 : s + 2]], axis=1)
             found = look_up(table, rows, hot[:, s * LANES : (s + 2) * LANES], steps)
             for half in range(2):
                 at = (s + half) * STEPS + first
                 replies[at : at + steps] = found[:, half * LANES : (half + 1) * LANES]
 
+    waiting = []
+    for part, (first, steps) in enumerate(LOOKED_UP):
+        for step in range(first, first + steps):
+            level, east, north = ocean_turn(first, steps, step, level, east, north)
+            if waiting:
+                reply(*waiting, step - first, steps)
+        if part == len(LOOKED_UP) - 1:
+            level_out[...] = level[:tile_rows, :LANES]
+        waiting = [table_of(first, steps), first, steps]
+    reply(*waiting, 0, 1)
+
 
 def mouth_kernel(returned, address, level_out, whole, series, hot, block, departures):
     rows = address.shape[0]
     groups = LANES // MPB
+    place = lax.broadcasted_iota(i32, (TALL, 2 * LANES), 0).astype(f32).astype(bf16)
+
+    def place_of(label, part):
+        return label - part == place
+
     labels = []
     for i in range(0, rows, 2):
         pair = jnp.concatenate([address[i : i + 1], address[i + 1 : i + 2]], axis=1)
-        one_hot_columns(pair % WIDE, hot, slice(i * LANES, (i + 2) * LANES))
-        labels.append(pair // WIDE)
+        high, low = [label.astype(f32) for label in split_label(pair, WIDE)]
+        one_hot_columns(low, place_of, hot, slice(i * LANES, (i + 2) * LANES))
+        labels.append(high)
     lane = lax.broadcasted_iota(i32, (rows, LANES), 1)
     copies = []
     for first in range(0, STEPS, groups):
@@ -502,7 +569,7 @@
     if per > 1:
         values = values.reshape(devices // per, tall, per, capacity).transpose(0, 2, 1, 3)
     values = values.reshape(devices, 1, tall * capacity)
-    values = lax.all_to_all(values, ("river", "coast"), split_axis=0, concat_axis=0, tiled=True)
+    values = lax.all_to_all(values, ("coast", "river"), split_axis=0, concat_axis=0, tiled=True)
     if per > 1:
         values = values.reshape(devices // per, per, tall, capacity).transpose(0, 2, 1, 3)
     return values.reshape(devices // per * tall, LANES)
@@ -544,7 +611,7 @@
     height = tile_rows + 2 * HALO
 
     depth_after, sending, address = pl.pallas_call(
-        functools.partial(river_kernel, devices, capacity),
+        functools.partial(river_kernel, devices, lax.axis_size("coast"), capacity),
         name="river",
         out_shape=(
             shape(blocks, RB),
@@ -570,10 +637,15 @@
             pltpu.VMEM((RB, LANES), f32),
             pltpu.VMEM((rows, LANES), i32),
             pltpu.VMEM((rows * devices, LANES), bf16),
+            pltpu.VMEM((rows * devices, 2 * LANES), f32),
+            pltpu.VMEM((rows, LANES), f32),
+            pltpu.VMEM((LANES, rows), f32),
+            pltpu.VMEM((mouths, WIDE), bf16),
             *[pltpu.VMEM((TALL * steps, LANES), bf16) for _, steps in PARTS],
-            pltpu.VMEM((2 * TALL * (PARTS[0][1] + 1), mouths), bf16),
-            pltpu.VMEM((2 * TALL * PARTS[1][1], mouths), bf16),
-            pltpu.VMEM((mouths, WIDE), bf16),
+            *[
+                pltpu.VMEM((2 * TALL * (steps + (first == 0)), mouths), bf16)
+                for first, steps in PARTS
+            ],
         ],
         compiler_params=PARAMS,
     )(
@@ -592,7 +664,7 @@
     )
     arrived = swap(sending, SENT, devices, capacity)
 
-    fields, odd, even, hot = pl.pallas_call(
+    fields, odd, even, hot, labels = pl.pallas_call(
         source_kernel,
         name="sources",
         out_shape=(
@@ -600,6 +672,7 @@
             shape(ROWS_SENT, LANES),
             shape(ROWS_SENT, LANES),
             shape(WIDE, groups * LANES, dtype=bf16),
+            shape(groups, LANES),
         ),
         in_specs=[pl.BlockSpec(memory_space=pltpu.VMEM)]
         + [pl.BlockSpec(memory_space=pltpu.HBM)] * 5,
@@ -611,6 +684,8 @@
             pltpu.VMEM((tile_rows, tile_cols), f32),
             pltpu.SemaphoreType.DMA((5,)),
             pltpu.VMEM((TALL * STEPS, LANES), bf16),
+            pltpu.VMEM((WIDE, LANES), bf16),
+            pltpu.VMEM((2 * groups, LANES), f32),
             pltpu.VMEM((2 * TALL * STEPS, groups * LANES), bf16),
             pltpu.VMEM((2 * TALL * STEPS, LANES), f32),
         ],
@@ -631,11 +706,10 @@
         name="ocean",
         out_shape=(shape(tile_rows, tile_cols), shape(groups * STEPS, LANES)),
         scratch_shapes=[
-            pltpu.VMEM((STEPS, height, 2 * LANES), f32),
             pltpu.VMEM((2 * TALL * STEPS, LANES), f32),
         ],
         compiler_params=PARAMS,
-    )(tall, from_odd, from_even, arrived, hot)
+    )(tall, from_odd, from_even, labels, hot)
     returned = swap(replies, STEPS, devices, capacity)
 
     mouth_level = pl.pallas_call(

time: 55 us -> 53.5 us (0.973)
  starting transfers between devices: 6.96 us -> 5.27 us
  blocking collectives: 28.7 us -> 30.3 us
  Pallas kernels: 13.8 us -> 12.4 us
    all_to_all x2, blocking collectives: 28.7 us -> 30.3 us  [swap(): lax.all_to_all(values, ('coast', 'river'), split_axis=0, concat_axis=0, t...]
    ppermute x2, starting transfers between devices: 3.83 us -> 2.39 us  [with_neighbours(): lax.ppermute(even, axis, routes[1])]
    pallas_call x1, Pallas kernels: 6.23 us -> 5.39 us  [per_device(): pl.pallas_call(functools.partial(river_kernel, devices, lax.axis_size('co...]
where the time goes in v3:
time: 53.5 us; the launch traced here: 53.2 us
  blocking collectives  30.3 us (57%)
  Pallas kernels  12.4 us (23%)
  starting transfers between devices  5.27 us (10%)
  waiting for transfers between devices  4.5 us (8%)
  between operations  0.69 us (1%)
    all_to_all x2, blocking collectives, swap(): lax.all_to_all(values, ('coast', 'river'), split_axis=0, concat_axis=0, t...  30.3 us
    pallas_call x1, Pallas kernels, per_device(): pl.pallas_call(functools.partial(river_kernel, devices, lax.axis_size('co...  5.39 us
    ppermute x2, waiting for transfers between devices, with_neighbours(): lax.ppermute(odd, axis, routes[0])  3.24 us
    pallas_call x1, Pallas kernels, per_device(): pl.pallas_call(functools.partial(ocean_kernel, tile_rows), name='ocean',...  3.1 us
    ppermute x2, starting transfers between devices, with_neighbours(): lax.ppermute(odd, axis, routes[0])  2.88 us
    ppermute x2, starting transfers between devices, with_neighbours(): lax.ppermute(even, axis, routes[1])  2.39 us
    pallas_call x1, Pallas kernels, per_device(): pl.pallas_call(source_kernel, name='sources', out_shape=(shape(FIELDS * t...  2.27 us
    pallas_call x1, Pallas kernels, per_device(): pl.pallas_call(mouth_kernel, name='mouths', out_shape=shape(blocks, STEPS...  1.35 us
  transfers between devices with their start and end apart: 4, of which 2 were waited for; matrix products, arithmetic and copies ran while one was open for 0% of the time, Pallas kernels for 0%

profile of v3, /device:TPU:1, one launch (start us, length us, event | category | flops | bytes accessed | tf_op | source)
XLA Modules:
  0.0 53.2 jit_solution(2115593783748533944)
XLA Ops:
  0.6 5.4 %river.1 = (f32[64,128]{1,0:T(8,128)}, f32[416,128]{1,0:T(8,128)S(1)}, s32[16,128]{1,0:T(8,128)S(1)}) custom-call(f32[64,128]{1,0:T(8,128)} %refs_0_.2, f32[64,128]{1,0:T(8,128)} %refs_1_.2, f32[64,128]{1,0:T(8,128)} %refs_2_.2, f32[64,128]{1,0:T(8,128)} %refs_3_.2, f32[64,128]{1,0:T(8,128)} %refs_4_.2, f32[64,128]{1,0:T(8,128)} %refs_5_.1, ...), custom_call_target="tpu_custom_call" | custom-call | tf_op jit(solution)/shard_map/river/pallas_call | solution.py:613
  6.0 16.4 %all_to_all.10 = f32[32,1,1664]{2,1,0:T(1,128)S(1)} all-to-all(f32[32,1,1664]{2,1,0:T(1,128)S(1)} %bitcast.11), channel_id=1, replica_groups=mesh['river'=4,'coast'=8] {'coast','river'}, dimensions={0} | all-to-all | bytes 425984 | tf_op jit(solution)/shard_map/all_to_all | solution.py:572
  22.4 2.3 %sources.1 = (f32[512,128]{1,0:T(8,128)S(1)}, f32[120,128]{1,0:T(8,128)S(1)}, f32[120,128]{1,0:T(8,128)S(1)}, bf16[256,4096]{1,0:T(8,128)(2,1)S(1)}, f32[32,128]{1,0:T(8,128)S(1)}) custom-call(f32[416,128]{1,0:T(8,128)S(1)} %bitcast.9, f32[32,128]{1,0:T(8,128)} %refs_0_.3, f32[32,128]{1,0:T(8,128)} %refs_1_.3, s32[32,128]{1,0:T(8,128)} %refs_2_.3, ...), custom_call_target="tpu_custom_call" | custom-call | tf_op jit(solution)/shard_map/sources/pallas_call | solution.py:667
  24.7 2.2 %collective-permute-start = (f32[120,128]{1,0:T(8,128)S(1)}, f32[120,128]{1,0:T(8,128)S(1)}, u32[]{:S(2)}, u32[]{:S(2)}) collective-permute-start(f32[120,128]{1,0:T(8,128)S(1)} %get-tuple-element.19), channel_id=1, source_target_pairs={{8,16},{16,8},{9,17},{17,9},{10,18},{18,10},{11,19},{19,11},{12,20... | collective-permute-start | bytes 184328 | tf_op jit(solution)/shard_map/ppermute | solution.py:584
  26.9 0.1 collective-permute-start.1
  27.0 3.2 %collective-permute-done.from_odd = f32[120,128]{1,0:T(8,128)S(1)} collective-permute-done((f32[120,128]{1,0:T(8,128)S(1)}, f32[120,128]{1,0:T(8,128)S(1)}, u32[]{:S(2)}, u32[]{:S(2)}) %collective-permute-start) | collective-permute-done | bytes 61472 | tf_op jit(solution)/shard_map/ppermute | solution.py:584
  30.2 0.0 collective-permute-done.1.from_even
  30.2 0.3 strips.1
  30.5 0.7 %collective-permute-start.2 = (f32[56,128]{1,0:T(8,128)S(1)}, f32[56,128]{1,0:T(8,128)S(1)}, u32[]{:S(2)}, u32[]{:S(2)}) collective-permute-start(f32[56,128]{1,0:T(8,128)S(1)} %get-tuple-element.22), channel_id=1, source_target_pairs={{1,2},{2,1},{3,4},{4,3},{5,6},{6,5},{9,10},{10,9},{11,12},{12,11},... | collective-permute-start | bytes 86024 | tf_op jit(solution)/shard_map/ppermute | solution.py:584
  31.2 2.3 %collective-permute-start.3 = (f32[56,128]{1,0:T(8,128)S(1)}, f32[56,128]{1,0:T(8,128)S(1)}, u32[]{:S(2)}, u32[]{:S(2)}) collective-permute-start(f32[56,128]{1,0:T(8,128)S(1)} %get-tuple-element.23), channel_id=1, source_target_pairs={{0,1},{1,0},{2,3},{3,2},{4,5},{5,4},{6,7},{7,6},{8,9},{9,8},{10,11... | collective-permute-start | bytes 86024 | tf_op jit(solution)/shard_map/ppermute | solution.py:584
  33.5 0.0 collective-permute-done.2.from_odd
  33.5 1.3 %collective-permute-done.3.from_even = f32[56,128]{1,0:T(8,128)S(1)} collective-permute-done((f32[56,128]{1,0:T(8,128)S(1)}, f32[56,128]{1,0:T(8,128)S(1)}, u32[]{:S(2)}, u32[]{:S(2)}) %collective-permute-start.3) | collective-permute-done | bytes 28704 | tf_op jit(solution)/shard_map/ppermute | solution.py:584
  34.8 3.1 %ocean.1 = (f32[32,128]{1,0:T(8,128)}, f32[384,128]{1,0:T(8,128)S(1)}) custom-call(f32[896,128]{1,0:T(8,128)S(1)} %get-tuple-element.21.tall, f32[56,128]{1,0:T(8,128)S(1)} %collective-permute-done.2.from_odd, f32[56,128]{1,0:T(8,128)S(1)} %collective-permute-done.3.from_even, f32[32,128]{1,0:T(8,128)S(1)} %get-tuple-element.24.row_labels, ...), custom_call_target="tpu_custom_call" | custom-call | tf_op jit(solution)/shard_map/ocean/pallas_call | solution.py:704
  37.9 13.9 %all_to_all.11 = f32[32,1,1536]{2,1,0:T(1,128)S(1)} all-to-all(f32[32,1,1536]{2,1,0:T(1,128)S(1)} %bitcast.12), channel_id=1, replica_groups=mesh['river'=4,'coast'=8] {'coast','river'}, dimensions={0} | all-to-all | bytes 393216 | tf_op jit(solution)/shard_map/all_to_all | solution.py:572
  51.8 1.3 %mouths.1 = f32[64,384]{1,0:T(8,128)} custom-call(f32[384,128]{1,0:T(8,128)S(1)} %bitcast.10, s32[16,128]{1,0:T(8,128)S(1)} %get-tuple-element.28.address), custom_call_target="tpu_custom_call" | custom-call | tf_op jit(solution)/shard_map/mouths/pallas_call | solution.py:715
Async XLA Ops:
  24.7 5.5 %collective-permute-start = (f32[120,128]{1,0:T(8,128)S(1)}, f32[120,128]{1,0:T(8,128)S(1)}, u32[]{:S(2)}, u32[]{:S(2)}) collective-permute-start(f32[120,128]{1,0:T(8,128)S(1)} %get-tuple-element.19), channel_id=1, source_target_pairs={{8,16},{16,8},{9,17},{17,9},{10,18},{18,10},{11,19},{19,11},{12,20... | collective-permute-start | bytes 184328 | tf_op jit(solution)/shard_map/ppermute | solution.py:584
  26.9 3.3 %collective-permute-start.1 = (f32[120,128]{1,0:T(8,128)S(1)}, f32[120,128]{1,0:T(8,128)S(1)}, u32[]{:S(2)}, u32[]{:S(2)}) collective-permute-start(f32[120,128]{1,0:T(8,128)S(1)} %get-tuple-element.20), channel_id=1, source_target_pairs={{0,8},{8,0},{16,24},{24,16},{1,9},{9,1},{17,25},{25,17},{2,10},{10... | collective-permute-start | bytes 184328 | tf_op jit(solution)/shard_map/ppermute | solution.py:584
  30.5 3.0 %collective-permute-start.2 = (f32[56,128]{1,0:T(8,128)S(1)}, f32[56,128]{1,0:T(8,128)S(1)}, u32[]{:S(2)}, u32[]{:S(2)}) collective-permute-start(f32[56,128]{1,0:T(8,128)S(1)} %get-tuple-element.22), channel_id=1, source_target_pairs={{1,2},{2,1},{3,4},{4,3},{5,6},{6,5},{9,10},{10,9},{11,12},{12,11},... | collective-permute-start | bytes 86024 | tf_op jit(solution)/shard_map/ppermute | solution.py:584
  31.2 3.6 %collective-permute-start.3 = (f32[56,128]{1,0:T(8,128)S(1)}, f32[56,128]{1,0:T(8,128)S(1)}, u32[]{:S(2)}, u32[]{:S(2)}) collective-permute-start(f32[56,128]{1,0:T(8,128)S(1)} %get-tuple-element.23), channel_id=1, source_target_pairs={{0,1},{1,0},{2,3},{3,2},{4,5},{5,4},{6,7},{7,6},{8,9},{9,8},{10,11... | collective-permute-start | bytes 86024 | tf_op jit(solution)/shard_map/ppermute | solution.py:584

commit v4 on v3

--- a/solution.py
+++ b/solution.py
@@ -203,9 +203,14 @@
     down = jnp.where(at_mouth, 0, into)
     offset = jnp.where(at_mouth, 0, into - lane)
     bed = bed_in[...]
-    bed_top = jnp.where(
-        at_mouth, bed, jnp.maximum(bed, jnp.take_along_axis(bed, down, axis=1, mode="promise_in_bounds"))
-    )
+
+    sources = [(down - 4 * a) & (RB - 1) for a in range(reach_offsets // 4)]
+
+    def below_of(value, a=0):
+        return jnp.take_along_axis(value, sources[a], axis=1, mode="promise_in_bounds")
+
+    bed_below = below_of(bed)
+    bed_top = jnp.where(at_mouth, bed, jnp.maximum(bed, bed_below))
     drive = gravity * step_seconds / length_in[...]
     width = width_in[...]
     area = step_seconds / (width * length_in[...])
@@ -217,21 +222,26 @@
         weight = its_width * turn(area, -(o - o % 4))
         enters[o] = jnp.where(where_to == o + 1, weight, 0.0)
 
-    def river_turn(substep, depth, flow):
-        surface = bed + depth
-        below = jnp.where(at_mouth, prev, jnp.take_along_axis(surface, down, axis=1, mode="promise_in_bounds"))
-        flow = flow_after(flow, surface, below, bed_top, drive, river_manning)
+    def river_turn(substep, depth, flow, below):
+        below = jnp.where(at_mouth, prev, below)
+        flow = flow_after(flow, bed + depth, below, bed_top, drive, river_manning)
         moved = [turn(flow, 1 + b) for b in range(4)]
         sums = []
         for a in range(0, reach_offsets, 4):
             one, other = [
                 enters[a + b] * moved[b] + enters[a + b + 1] * moved[b + 1] for b in (0, 2)
             ]
-            sums.append(turn(one + other, a))
-        inflow = (sums[0] + sums[1]) + (sums[2] + sums[3])
-        depth = (depth + gain - loss * flow) + inflow
+            sums.append(one + other)
+        sums[0] = sums[0] + (depth + gain - loss * flow)
+        depth, below = [
+            (places[0] + places[1]) + (places[2] + places[3])
+            for places in (
+                [turn(value, 4 * a) for a, value in enumerate(sums)],
+                [below_of(value, a) for a, value in enumerate(sums)],
+            )
+        ]
         series[substep * rows : (substep + 1) * rows] = grouped(flow * width, inland)
-        return depth, flow
+        return depth, flow, bed_below + below
 
     def count_mouths():
         for i in range(rows):
@@ -309,8 +319,9 @@
     for owner, (_, steps) in zip(owners, PARTS):
         row_owners(owner, steps)
     depth, flow = depth_in[...], flow_in[...]
+    below = bed_below + below_of(depth)
     for substep in range(STEPS):
-        depth, flow = river_turn(substep, depth, flow)
+        depth, flow, below = river_turn(substep, depth, flow, below)
         for work in beside.get(substep, []):
             work()
     depth_end[...] = depth
@@ -432,7 +443,7 @@
 
 
 def ocean_kernel(
-    tile_rows, tall, from_odd, from_even, row_labels, hot, level_out, replies, history
+    tile_rows, tall, from_odd, from_even, row_labels, hot, level_out, replies, history, level_end, departure
 ):
     height = tall.shape[0] // FIELDS
     width = 2 * LANES
@@ -506,9 +517,12 @@
             if waiting:
                 reply(*waiting, step - first, steps)
         if part == len(LOOKED_UP) - 1:
-            level_out[...] = level[:tile_rows, :LANES]
+            level_end[...] = level[:tile_rows, :LANES]
+            finished = pltpu.make_async_copy(level_end, level_out, departure)
+            finished.start()
         waiting = [table_of(first, steps), first, steps]
     reply(*waiting, 0, 1)
+    finished.wait()
 
 
 def mouth_kernel(returned, address, level_out, whole, series, hot, block, departures):
@@ -527,31 +541,31 @@
         labels.append(high)
     lane = lax.broadcasted_iota(i32, (rows, LANES), 1)
     copies = []
-    for first in range(0, STEPS, groups):
+    for first, steps in LOOKED_UP:
         for row in range(TALL):
             for half in range(2):
                 at = (2 * row + half) * STEPS + first
-                to = first * TALL + row * groups
+                to = first * TALL + row * steps
                 lanes = slice(half * LANES, (half + 1) * LANES)
-                whole[to : to + groups, lanes] = returned[at : at + groups]
-        own = whole[first * TALL : (first + groups) * TALL]
+                whole[to : to + steps, lanes] = returned[at : at + steps]
+        own = whole[first * TALL : (first + steps) * TALL]
         table = jnp.concatenate(in_two(own), axis=0)
         for i in range(0, rows, 2):
             lanes = slice(i * LANES, (i + 2) * LANES)
-            found = look_up(table, labels[i // 2], hot[:, lanes], groups)
-            series[pl.ds(first * rows + i, groups, stride=rows)] = found[:, :LANES]
-            series[pl.ds(first * rows + i + 1, groups, stride=rows)] = found[:, LANES:]
-        number = first // groups
-        for g in range(groups):
-            result = jnp.zeros((rows, LANES), f32)
-            for place in range(groups):
-                at = (first + place) * rows
-                part = turn(series[at : at + rows], (place - g) * MPB)
-                result = jnp.where(lane // MPB == place, part, result)
-            block[number, g * rows : (g + 1) * rows] = result
-        to = level_out.at[:, pl.ds(number * LANES, LANES)]
-        copies.append(pltpu.make_async_copy(block.at[number], to, departures.at[number]))
-        copies[-1].start()
+            found = look_up(table, labels[i // 2], hot[:, lanes], steps)
+            series[pl.ds(first * rows + i, steps, stride=rows)] = found[:, :LANES]
+            series[pl.ds(first * rows + i + 1, steps, stride=rows)] = found[:, LANES:]
+        for number in range(first // groups, (first + steps) // groups):
+            for g in range(groups):
+                result = jnp.zeros((rows, LANES), f32)
+                for place in range(groups):
+                    at = (number * groups + place) * rows
+                    part = turn(series[at : at + rows], (place - g) * MPB)
+                    result = jnp.where(lane // MPB == place, part, result)
+                block[number, g * rows : (g + 1) * rows] = result
+            to = level_out.at[:, pl.ds(number * LANES, LANES)]
+            copies.append(pltpu.make_async_copy(block.at[number], to, departures.at[number]))
+            copies[-1].start()
     for copy in copies:
         copy.wait()
 
@@ -707,7 +721,13 @@
         out_shape=(shape(tile_rows, tile_cols), shape(groups * STEPS, LANES)),
         scratch_shapes=[
             pltpu.VMEM((2 * TALL * STEPS, LANES), f32),
+            pltpu.VMEM((tile_rows, tile_cols), f32),
+            pltpu.SemaphoreType.DMA,
         ],
+        out_specs=(
+            pl.BlockSpec(memory_space=pltpu.HBM),
+            pl.BlockSpec(memory_space=pltpu.VMEM),
+        ),
         compiler_params=PARAMS,
     )(tall, from_odd, from_even, labels, hot)
     returned = swap(replies, STEPS, devices, capacity)

time: 53.5 us -> 53.3 us (level)
  no operation moved by 1% of the time
where the time goes in v4:
time: 53.3 us; the launch traced here: 53 us
  blocking collectives  30.3 us (57%)
  Pallas kernels  12.2 us (23%)
  starting transfers between devices  5.27 us (10%)
  waiting for transfers between devices  4.5 us (8%)
  between operations  0.69 us (1%)
    all_to_all x2, blocking collectives, swap(): lax.all_to_all(values, ('coast', 'river'), split_axis=0, concat_axis=0, t...  30.3 us
    pallas_call x1, Pallas kernels, per_device(): pl.pallas_call(functools.partial(river_kernel, devices, lax.axis_size('co...  5.19 us
    ppermute x2, waiting for transfers between devices, with_neighbours(): lax.ppermute(odd, axis, routes[0])  3.24 us
    pallas_call x1, Pallas kernels, per_device(): pl.pallas_call(functools.partial(ocean_kernel, tile_rows), name='ocean',...  3.11 us
    ppermute x2, starting transfers between devices, with_neighbours(): lax.ppermute(odd, axis, routes[0])  2.88 us
    ppermute x2, starting transfers between devices, with_neighbours(): lax.ppermute(even, axis, routes[1])  2.39 us
    pallas_call x1, Pallas kernels, per_device(): pl.pallas_call(source_kernel, name='sources', out_shape=(shape(FIELDS * t...  2.27 us
    pallas_call x1, Pallas kernels, per_device(): pl.pallas_call(mouth_kernel, name='mouths', out_shape=shape(blocks, STEPS...  1.34 us
  transfers between devices with their start and end apart: 4, of which 2 were waited for; matrix products, arithmetic and copies ran while one was open for 0% of the time, Pallas kernels for 0%

profile of v4, /device:TPU:1, one launch (start us, length us, event | category | flops | bytes accessed | tf_op | source)
XLA Modules:
  0.0 53.0 jit_solution(3825847853095460821)
XLA Ops:
  0.6 5.2 %river.1 = (f32[64,128]{1,0:T(8,128)}, f32[416,128]{1,0:T(8,128)S(1)}, s32[16,128]{1,0:T(8,128)S(1)}) custom-call(f32[64,128]{1,0:T(8,128)} %refs_0_.2, f32[64,128]{1,0:T(8,128)} %refs_1_.2, f32[64,128]{1,0:T(8,128)} %refs_2_.2, f32[64,128]{1,0:T(8,128)} %refs_3_.2, f32[64,128]{1,0:T(8,128)} %refs_4_.2, f32[64,128]{1,0:T(8,128)} %refs_5_.1, ...), custom_call_target="tpu_custom_call" | custom-call | tf_op jit(solution)/shard_map/river/pallas_call | solution.py:627
  5.8 16.4 %all_to_all.10 = f32[32,1,1664]{2,1,0:T(1,128)S(1)} all-to-all(f32[32,1,1664]{2,1,0:T(1,128)S(1)} %bitcast.11), channel_id=1, replica_groups=mesh['river'=4,'coast'=8] {'coast','river'}, dimensions={0} | all-to-all | bytes 425984 | tf_op jit(solution)/shard_map/all_to_all | solution.py:586
  22.2 2.3 %sources.1 = (f32[512,128]{1,0:T(8,128)S(1)}, f32[120,128]{1,0:T(8,128)S(1)}, f32[120,128]{1,0:T(8,128)S(1)}, bf16[256,4096]{1,0:T(8,128)(2,1)S(1)}, f32[32,128]{1,0:T(8,128)S(1)}) custom-call(f32[416,128]{1,0:T(8,128)S(1)} %bitcast.9, f32[32,128]{1,0:T(8,128)} %refs_0_.3, f32[32,128]{1,0:T(8,128)} %refs_1_.3, s32[32,128]{1,0:T(8,128)} %refs_2_.3, ...), custom_call_target="tpu_custom_call" | custom-call | tf_op jit(solution)/shard_map/sources/pallas_call | solution.py:681
  24.5 2.2 %collective-permute-start = (f32[120,128]{1,0:T(8,128)S(1)}, f32[120,128]{1,0:T(8,128)S(1)}, u32[]{:S(2)}, u32[]{:S(2)}) collective-permute-start(f32[120,128]{1,0:T(8,128)S(1)} %get-tuple-element.19), channel_id=1, source_target_pairs={{8,16},{16,8},{9,17},{17,9},{10,18},{18,10},{11,19},{19,11},{12,20... | collective-permute-start | bytes 184328 | tf_op jit(solution)/shard_map/ppermute | solution.py:598
  26.7 0.1 collective-permute-start.1
  26.8 3.2 %collective-permute-done.from_odd = f32[120,128]{1,0:T(8,128)S(1)} collective-permute-done((f32[120,128]{1,0:T(8,128)S(1)}, f32[120,128]{1,0:T(8,128)S(1)}, u32[]{:S(2)}, u32[]{:S(2)}) %collective-permute-start) | collective-permute-done | bytes 61472 | tf_op jit(solution)/shard_map/ppermute | solution.py:598
  30.0 0.0 collective-permute-done.1.from_even
  30.0 0.3 strips.1
  30.3 0.7 %collective-permute-start.2 = (f32[56,128]{1,0:T(8,128)S(1)}, f32[56,128]{1,0:T(8,128)S(1)}, u32[]{:S(2)}, u32[]{:S(2)}) collective-permute-start(f32[56,128]{1,0:T(8,128)S(1)} %get-tuple-element.22), channel_id=1, source_target_pairs={{1,2},{2,1},{3,4},{4,3},{5,6},{6,5},{9,10},{10,9},{11,12},{12,11},... | collective-permute-start | bytes 86024 | tf_op jit(solution)/shard_map/ppermute | solution.py:598
  31.0 2.3 %collective-permute-start.3 = (f32[56,128]{1,0:T(8,128)S(1)}, f32[56,128]{1,0:T(8,128)S(1)}, u32[]{:S(2)}, u32[]{:S(2)}) collective-permute-start(f32[56,128]{1,0:T(8,128)S(1)} %get-tuple-element.23), channel_id=1, source_target_pairs={{0,1},{1,0},{2,3},{3,2},{4,5},{5,4},{6,7},{7,6},{8,9},{9,8},{10,11... | collective-permute-start | bytes 86024 | tf_op jit(solution)/shard_map/ppermute | solution.py:598
  33.3 0.0 collective-permute-done.2.from_odd
  33.3 1.3 %collective-permute-done.3.from_even = f32[56,128]{1,0:T(8,128)S(1)} collective-permute-done((f32[56,128]{1,0:T(8,128)S(1)}, f32[56,128]{1,0:T(8,128)S(1)}, u32[]{:S(2)}, u32[]{:S(2)}) %collective-permute-start.3) | collective-permute-done | bytes 28704 | tf_op jit(solution)/shard_map/ppermute | solution.py:598
  34.6 3.1 %ocean.1 = (f32[32,128]{1,0:T(8,128)}, f32[384,128]{1,0:T(8,128)S(1)}) custom-call(f32[896,128]{1,0:T(8,128)S(1)} %get-tuple-element.21.tall, f32[56,128]{1,0:T(8,128)S(1)} %collective-permute-done.2.from_odd, f32[56,128]{1,0:T(8,128)S(1)} %collective-permute-done.3.from_even, f32[32,128]{1,0:T(8,128)S(1)} %get-tuple-element.24.row_labels, ...), custom_call_target="tpu_custom_call" | custom-call | tf_op jit(solution)/shard_map/ocean/pallas_call | solution.py:718
  37.7 13.9 %all_to_all.11 = f32[32,1,1536]{2,1,0:T(1,128)S(1)} all-to-all(f32[32,1,1536]{2,1,0:T(1,128)S(1)} %bitcast.12), channel_id=1, replica_groups=mesh['river'=4,'coast'=8] {'coast','river'}, dimensions={0} | all-to-all | bytes 393216 | tf_op jit(solution)/shard_map/all_to_all | solution.py:586
  51.6 1.3 %mouths.1 = f32[64,384]{1,0:T(8,128)} custom-call(f32[384,128]{1,0:T(8,128)S(1)} %bitcast.10, s32[16,128]{1,0:T(8,128)S(1)} %get-tuple-element.28.address), custom_call_target="tpu_custom_call" | custom-call | tf_op jit(solution)/shard_map/mouths/pallas_call | solution.py:735
Async XLA Ops:
  24.5 5.5 %collective-permute-start = (f32[120,128]{1,0:T(8,128)S(1)}, f32[120,128]{1,0:T(8,128)S(1)}, u32[]{:S(2)}, u32[]{:S(2)}) collective-permute-start(f32[120,128]{1,0:T(8,128)S(1)} %get-tuple-element.19), channel_id=1, source_target_pairs={{8,16},{16,8},{9,17},{17,9},{10,18},{18,10},{11,19},{19,11},{12,20... | collective-permute-start | bytes 184328 | tf_op jit(solution)/shard_map/ppermute | solution.py:598
  26.7 3.3 %collective-permute-start.1 = (f32[120,128]{1,0:T(8,128)S(1)}, f32[120,128]{1,0:T(8,128)S(1)}, u32[]{:S(2)}, u32[]{:S(2)}) collective-permute-start(f32[120,128]{1,0:T(8,128)S(1)} %get-tuple-element.20), channel_id=1, source_target_pairs={{0,8},{8,0},{16,24},{24,16},{1,9},{9,1},{17,25},{25,17},{2,10},{10... | collective-permute-start | bytes 184328 | tf_op jit(solution)/shard_map/ppermute | solution.py:598
  30.3 3.0 %collective-permute-start.2 = (f32[56,128]{1,0:T(8,128)S(1)}, f32[56,128]{1,0:T(8,128)S(1)}, u32[]{:S(2)}, u32[]{:S(2)}) collective-permute-start(f32[56,128]{1,0:T(8,128)S(1)} %get-tuple-element.22), channel_id=1, source_target_pairs={{1,2},{2,1},{3,4},{4,3},{5,6},{6,5},{9,10},{10,9},{11,12},{12,11},... | collective-permute-start | bytes 86024 | tf_op jit(solution)/shard_map/ppermute | solution.py:598
  31.0 3.6 %collective-permute-start.3 = (f32[56,128]{1,0:T(8,128)S(1)}, f32[56,128]{1,0:T(8,128)S(1)}, u32[]{:S(2)}, u32[]{:S(2)}) collective-permute-start(f32[56,128]{1,0:T(8,128)S(1)} %get-tuple-element.23), channel_id=1, source_target_pairs={{0,1},{1,0},{2,3},{3,2},{4,5},{5,4},{6,7},{7,6},{8,9},{9,8},{10,11... | collective-permute-start | bytes 86024 | tf_op jit(solution)/shard_map/ppermute | solution.py:598

commit v5 on v4

--- a/solution.py
+++ b/solution.py
@@ -85,11 +85,11 @@
     halves = [in_two(jnp.concatenate(pair, axis=0)) for pair in pairs]
     labels = small(rows)
     none = jnp.zeros(labels.shape, bf16)
-    for part in range(steps):
-        at_rows = slice(part * TALL, (part + 1) * TALL)
-        hit = labels == owner[at_rows]
-        for number, half in enumerate(halves[part % turns]):
-            at_rows = slice((number * steps + part) * TALL, (number * steps + part + 1) * TALL)
+    high_rows = owner.shape[0]
+    for part in range(0, high_rows, TALL):
+        hit = labels == owner[part : part + TALL]
+        for number, half in enumerate(halves[part // TALL % turns]):
+            at_rows = slice(number * high_rows + part, number * high_rows + part + TALL)
             lhs[at_rows, lanes] = jnp.where(hit, half, none)
 
 
@@ -346,10 +346,38 @@
 ROWS_SENT = -(-ROW_AT[FIELDS] // 8) * 8
 
 
-def source_kernel(arrived, *refs):
-    inputs, (fields, odd, even, rhs, label_out), refs = refs[:5], refs[5:10], refs[10:]
+def add_in_chunks(arrived, row_labels, column_labels, owner, places, lhs, rhs):
+    row_owners(owner, STEPS)
+    row_owners(places, 1)
+    groups = arrived.shape[0] // SENT
+
+    def place_of(label, part):
+        return label == places[part : part + TALL]
+
+    def place(chunk):
+        for s in range(chunk, chunk + CHUNK):
+            lanes = slice(s * LANES, (s + 1) * LANES)
+            lay_out(arrived, s * SENT, 1, STEPS, row_labels[s : s + 1], owner, lhs, lanes)
+            one_hot_columns(column_labels[s : s + 1], place_of, rhs, lanes)
+
+    both = jnp.zeros((lhs.shape[0], WIDE), f32)
+    place(0)
+    for chunk in range(0, groups, CHUNK):
+        if chunk + CHUNK < groups:
+            place(chunk + CHUNK)
+        lanes = slice(chunk * LANES, (chunk + CHUNK) * LANES)
+        both = both + lax.dot_general(
+            lhs[:, lanes], rhs[:, lanes], (((1,), (1,)), ((), ())), preferred_element_type=f32
+        )
+    half = lhs.shape[0] // 2
+    return both[:half] + both[half:]
+
+
+def edge_kernel(arrived, *refs):
+    inputs, (odd, sea), refs = refs[:5], refs[5:7], refs[7:]
+    sea_level, sea_bed, wet_mask, flux_east, flux_north, arrivals = refs[:6]
+    owner, places, row_labels, column_labels, lhs, rhs, sums = refs[6:]
     first_of_pair = lax.axis_index("river") % 2 == 0
-    sea_level, sea_bed, wet_mask, flux_east, flux_north, arrivals, owner, places, labels, lhs, sums = refs
     copies = [
         pltpu.make_async_copy(whole, own, arrivals.at[number])
         for number, (whole, own) in enumerate(zip(inputs, refs[:5]))
@@ -359,41 +387,57 @@
     groups = arrived.shape[0] // SENT
     tile_rows, tile_cols = sea_level.shape
 
-    high_rows = TALL * STEPS
-    row_owners(owner, STEPS)
-    row_owners(places, 1)
-
-    def place_of(label, part):
-        return label == places[part : part + TALL]
-
     cells = arrived[pl.ds(STEPS, groups, stride=SENT)].astype(i32)
-    for number, label in enumerate(cell_labels(cells, tile_cols)):
-        labels[number * groups : (number + 1) * groups] = label.astype(f32)
-    label_out[...] = labels[:groups]
-
-    def place(chunk):
-        for s in range(chunk, chunk + CHUNK):
-            lanes = slice(s * LANES, (s + 1) * LANES)
-            lay_out(arrived, s * SENT, 1, STEPS, labels[s : s + 1], owner, lhs, lanes)
-            one_hot_columns(labels[groups + s : groups + s + 1], place_of, rhs, lanes)
-
-    both = jnp.zeros((2 * high_rows, WIDE), f32)
-    place(0)
-    for chunk in range(0, groups, CHUNK):
-        if chunk + CHUNK < groups:
-            place(chunk + CHUNK)
-        lanes = slice(chunk * LANES, (chunk + CHUNK) * LANES)
-        both = both + lax.dot_general(
-            lhs[:, lanes], rhs[:, lanes], (((1,), (1,)), ((), ())), preferred_element_type=f32
-        )
-    total = both[:high_rows] + both[high_rows:]
+    row, column = split_label(cells, tile_cols)
+    row = row - jnp.where(first_of_pair, 0, tile_rows - HALO)
+    upper = jnp.where(row >= HALO // 2, 1, 0)
+    inside = (row >= 0) & (row < HALO)
+    row_labels[...] = jnp.where(inside, row - upper * (HALO // 2), WIDE - 1).astype(f32)
+    column_labels[...] = (column + upper * tile_cols).astype(f32)
+    total = add_in_chunks(arrived, row_labels, column_labels, owner, places, lhs, rhs)
+    high_rows = total.shape[0]
     for half in range(2):
         part = slice(half * high_rows, (half + 1) * high_rows)
         sums[part] = total[:, half * LANES : (half + 1) * LANES]
+
+    def put(field, start, end):
+        reach = reach_of(field)
+        if reach:
+            last, first = end[end.shape[0] - reach :], start[:reach]
+            part = slice(ROW_AT[field], ROW_AT[field] + reach)
+            odd[part] = jnp.where(first_of_pair, first, last)
+
+    odd[ROWS_SENT - 8 :] = jnp.zeros((8, LANES), f32)
+    for step in range(STEPS):
+        halves = [
+            sums[pl.ds(half * high_rows + step, HALO // 2, stride=STEPS)] for half in range(2)
+        ]
+        rows = jnp.concatenate(halves, axis=0)
+        put(step, rows, rows)
     for copy in copies:
         copy.wait()
     bed = sea_bed[...]
     level = jnp.where(wet_mask[...] == 1, jnp.maximum(sea_level[...], bed), bed)
+    for number, value in enumerate((level, bed, flux_east[...], flux_north[...])):
+        sea[number * tile_rows : (number + 1) * tile_rows] = value
+        put(STEPS + number, value, value)
+
+
+def source_kernel(arrived, sea, fields, even, rhs, label_out, *refs):
+    owner, places, column_labels, lhs, sums = refs
+    first_of_pair = lax.axis_index("river") % 2 == 0
+    groups = arrived.shape[0] // SENT
+    tile_rows, tile_cols = sea.shape[0] // 4, sea.shape[1]
+
+    cells = arrived[pl.ds(STEPS, groups, stride=SENT)].astype(i32)
+    row, column = cell_labels(cells, tile_cols)
+    label_out[...] = row.astype(f32)
+    column_labels[...] = column.astype(f32)
+    total = add_in_chunks(arrived, label_out, column_labels, owner, places, lhs, rhs)
+    high_rows = total.shape[0]
+    for half in range(2):
+        part = slice(half * high_rows, (half + 1) * high_rows)
+        sums[part] = total[:, half * LANES : (half + 1) * LANES]
 
     def put(field, value):
         fields[field * tile_rows : (field + 1) * tile_rows] = value
@@ -401,16 +445,14 @@
         if reach:
             last, first = value[tile_rows - reach :], value[:reach]
             part = slice(ROW_AT[field], ROW_AT[field] + reach)
-            odd[part] = jnp.where(first_of_pair, first, last)
             even[part] = jnp.where(first_of_pair, last, first)
 
-    for swap_out in (odd, even):
-        swap_out[ROWS_SENT - 8 :] = jnp.zeros((8, LANES), f32)
+    even[ROWS_SENT - 8 :] = jnp.zeros((8, LANES), f32)
     for step in range(STEPS):
         halves = [sums[pl.ds(half * high_rows + step, TALL, stride=STEPS)] for half in range(2)]
         put(step, jnp.concatenate(halves, axis=0))
-    for number, value in enumerate((level, bed, flux_east[...], flux_north[...])):
-        put(STEPS + number, value)
+    for number in range(4):
+        put(STEPS + number, sea[number * tile_rows : (number + 1) * tile_rows])
 
 
 def strip_kernel(fields, from_odd, from_even, tall, odd, even):
@@ -574,6 +616,10 @@
     return jax.ShapeDtypeStruct(dims, dtype)
 
 
+def cost(products):
+    return pl.CostEstimate(flops=2 * products, bytes_accessed=8 << 20, transcendentals=0)
+
+
 def in_hbm(*arrays):
     return [pltpu.with_memory_space_constraint(whole, pltpu.HBM) for whole in arrays]
 
@@ -589,13 +635,9 @@
     return values.reshape(devices // per * tall, LANES)
 
 
-def with_neighbours(odd, even, axis):
-    size = lax.axis_size(axis)
-    routes = [
-        [(i + k, i + 1 - k) for i in range(start, size - 1, 2) for k in range(2)]
-        for start in (1, 0)
-    ]
-    return lax.ppermute(odd, axis, routes[0]), lax.ppermute(even, axis, routes[1])
+def with_neighbour(value, axis, start):
+    pairs = range(start, lax.axis_size(axis) - 1, 2)
+    return lax.ppermute(value, axis, [(i + k, i + 1 - k) for i in pairs for k in range(2)])
 
 
 def per_device(
@@ -678,16 +720,11 @@
     )
     arrived = swap(sending, SENT, devices, capacity)
 
-    fields, odd, even, hot, labels = pl.pallas_call(
-        source_kernel,
-        name="sources",
-        out_shape=(
-            shape(FIELDS * tile_rows, LANES),
-            shape(ROWS_SENT, LANES),
-            shape(ROWS_SENT, LANES),
-            shape(WIDE, groups * LANES, dtype=bf16),
-            shape(groups, LANES),
-        ),
+    edge_rows = -(-HALO // 2 * STEPS // TALL) * TALL
+    odd, sea = pl.pallas_call(
+        edge_kernel,
+        name="edges",
+        out_shape=(shape(ROWS_SENT, LANES), shape(4 * tile_rows, tile_cols)),
         in_specs=[pl.BlockSpec(memory_space=pltpu.VMEM)]
         + [pl.BlockSpec(memory_space=pltpu.HBM)] * 5,
         scratch_shapes=[
@@ -697,15 +734,39 @@
             pltpu.VMEM((tile_rows, tile_cols), f32),
             pltpu.VMEM((tile_rows, tile_cols), f32),
             pltpu.SemaphoreType.DMA((5,)),
+            pltpu.VMEM((edge_rows, LANES), bf16),
+            pltpu.VMEM((WIDE, LANES), bf16),
+            pltpu.VMEM((groups, LANES), f32),
+            pltpu.VMEM((groups, LANES), f32),
+            pltpu.VMEM((2 * edge_rows, groups * LANES), bf16),
+            pltpu.VMEM((WIDE, groups * LANES), bf16),
+            pltpu.VMEM((2 * edge_rows, LANES), f32),
+        ],
+        cost_estimate=cost(2 * edge_rows * WIDE * groups * LANES),
+        compiler_params=PARAMS,
+    )(arrived, *in_hbm(sea_level, sea_bed, wet_mask, flux_east, flux_north))
+    from_odd = with_neighbour(odd, "river", 1)
+
+    fields, even, hot, labels = pl.pallas_call(
+        source_kernel,
+        name="sources",
+        out_shape=(
+            shape(FIELDS * tile_rows, LANES),
+            shape(ROWS_SENT, LANES),
+            shape(WIDE, groups * LANES, dtype=bf16),
+            shape(groups, LANES),
+        ),
+        scratch_shapes=[
             pltpu.VMEM((TALL * STEPS, LANES), bf16),
             pltpu.VMEM((WIDE, LANES), bf16),
-            pltpu.VMEM((2 * groups, LANES), f32),
+            pltpu.VMEM((groups, LANES), f32),
             pltpu.VMEM((2 * TALL * STEPS, groups * LANES), bf16),
             pltpu.VMEM((2 * TALL * STEPS, LANES), f32),
         ],
+        cost_estimate=cost(2 * TALL * STEPS * WIDE * groups * LANES),
         compiler_params=PARAMS,
-    )(arrived, *in_hbm(sea_level, sea_bed, wet_mask, flux_east, flux_north))
-    from_odd, from_even = with_neighbours(odd, even, "river")
+    )(arrived, sea)
+    from_even = with_neighbour(even, "river", 0)
 
     tall, odd, even = pl.pallas_call(
         strip_kernel,
@@ -713,7 +774,7 @@
         out_shape=(shape(FIELDS * height, LANES), shape(height, LANES), shape(height, LANES)),
         compiler_params=PARAMS,
     )(fields, from_odd, from_even)
-    from_odd, from_even = with_neighbours(odd, even, "coast")
+    from_odd, from_even = with_neighbour(odd, "coast", 1), with_neighbour(even, "coast", 0)
 
     level_after, replies = pl.pallas_call(
         functools.partial(ocean_kernel, tile_rows),

time: 53.3 us -> 52.2 us (0.979)
  waiting for transfers between devices: 4.5 us -> 2.87 us
  Pallas kernels: 12.2 us -> 12.8 us
    ppermute x4, waiting for transfers between devices: 4.5 us -> 2.87 us  [with_neighbour(): lax.ppermute(value, axis, [(i + k, i + 1 - k) for i in pairs for k in ran...]
    pallas_call x0 -> x1, Pallas kernels: none -> 1.22 us  [per_device(): pl.pallas_call(edge_kernel, name='edges', out_shape=(shape(ROWS_SENT, LAN...]
    pallas_call x1, Pallas kernels: 2.27 us -> 1.62 us  [per_device(): pl.pallas_call(source_kernel, name='sources', out_shape=(shape(FIELDS * t...]
  transfers between devices with their start and end apart: 4 -> 4, of which waited for: 2 -> 2; matrix products, arithmetic and copies ran while one was open for 0% -> 0% of each run, Pallas kernels for 0% -> 3%
where the time goes in v5:
time: 52.2 us; the launch traced here: 51.9 us
  blocking collectives  30.3 us (58%)
  Pallas kernels  12.8 us (25%)
  starting transfers between devices  5.27 us (10%)
  waiting for transfers between devices  2.87 us (5%)
  between operations  0.7 us (1%)
    all_to_all x2, blocking collectives, swap(): lax.all_to_all(values, ('coast', 'river'), split_axis=0, concat_axis=0, t...  30.3 us
    ppermute x4, starting transfers between devices, with_neighbour(): lax.ppermute(value, axis, [(i + k, i + 1 - k) for i in pairs for k in ran...  5.27 us
    pallas_call x1, Pallas kernels, per_device(): pl.pallas_call(functools.partial(river_kernel, devices, lax.axis_size('co...  5.19 us
    pallas_call x1, Pallas kernels, per_device(): pl.pallas_call(functools.partial(ocean_kernel, tile_rows), name='ocean',...  3.11 us
    ppermute x4, waiting for transfers between devices, with_neighbour(): lax.ppermute(value, axis, [(i + k, i + 1 - k) for i in pairs for k in ran...  2.87 us
    pallas_call x1, Pallas kernels, per_device(): pl.pallas_call(source_kernel, name='sources', out_shape=(shape(FIELDS * t...  1.62 us
    pallas_call x1, Pallas kernels, per_device(): pl.pallas_call(mouth_kernel, name='mouths', out_shape=shape(blocks, STEPS...  1.34 us
    pallas_call x1, Pallas kernels, per_device(): pl.pallas_call(edge_kernel, name='edges', out_shape=(shape(ROWS_SENT, LAN...  1.22 us
  transfers between devices with their start and end apart: 4, of which 2 were waited for; matrix products, arithmetic and copies ran while one was open for 0% of the time, Pallas kernels for 3%

profile of v5, /device:TPU:1, one launch (start us, length us, event | category | flops | bytes accessed | tf_op | source)
XLA Modules:
  0.0 51.9 jit_solution(11018538339518255977)
XLA Ops:
  0.6 5.2 %river.1 = (f32[64,128]{1,0:T(8,128)}, f32[416,128]{1,0:T(8,128)S(1)}, s32[16,128]{1,0:T(8,128)S(1)}) custom-call(f32[64,128]{1,0:T(8,128)} %refs_0_.2, f32[64,128]{1,0:T(8,128)} %refs_1_.2, f32[64,128]{1,0:T(8,128)} %refs_2_.2, f32[64,128]{1,0:T(8,128)} %refs_3_.2, f32[64,128]{1,0:T(8,128)} %refs_4_.2, f32[64,128]{1,0:T(8,128)} %refs_5_.1, ...), custom_call_target="tpu_custom_call" | custom-call | tf_op jit(solution)/shard_map/river/pallas_call | solution.py:669
  5.8 16.4 %all_to_all.10 = f32[32,1,1664]{2,1,0:T(1,128)S(1)} all-to-all(f32[32,1,1664]{2,1,0:T(1,128)S(1)} %bitcast.12), channel_id=1, replica_groups=mesh['river'=4,'coast'=8] {'coast','river'}, dimensions={0} | all-to-all | bytes 425984 | tf_op jit(solution)/shard_map/all_to_all | solution.py:632
  22.2 1.2 %edges.1 = (f32[120,128]{1,0:T(8,128)S(1)}, f32[128,128]{1,0:T(8,128)S(1)}) custom-call(f32[416,128]{1,0:T(8,128)S(1)} %bitcast.10, f32[32,128]{1,0:T(8,128)} %refs_0_.3, f32[32,128]{1,0:T(8,128)} %refs_1_.3, s32[32,128]{1,0:T(8,128)} %refs_2_.3, f32[32,128]{1,0:T(8,128)} %refs_3_.3, f32[32,128]{1,0:T(8,128)} %refs_4_.3), custom_call_target="tpu_custom_call" | custom-call | flops 335544320 | bytes 8388608 | tf_op jit(solution)/shard_map/edges/pallas_call | solution.py:724
  23.5 2.2 %collective-permute-start = (f32[120,128]{1,0:T(8,128)S(1)}, f32[120,128]{1,0:T(8,128)S(1)}, u32[]{:S(2)}, u32[]{:S(2)}) collective-permute-start(f32[120,128]{1,0:T(8,128)S(1)} %get-tuple-element.21), channel_id=1, source_target_pairs={{8,16},{16,8},{9,17},{17,9},{10,18},{18,10},{11,19},{19,11},{12,20... | collective-permute-start | bytes 184328 | tf_op jit(solution)/shard_map/ppermute | solution.py:640
  25.7 1.6 %sources.1 = (f32[512,128]{1,0:T(8,128)S(1)}, f32[120,128]{1,0:T(8,128)S(1)}, bf16[256,4096]{1,0:T(8,128)(2,1)S(1)}, f32[32,128]{1,0:T(8,128)S(1)}) custom-call(f32[416,128]{1,0:T(8,128)S(1)} %bitcast.11, f32[128,128]{1,0:T(8,128)S(1)} %get-tuple-element.19.sea), custom_call_target="tpu_custom_call" | custom-call | flops 805306368 | bytes 8388608 | tf_op jit(solution)/shard_map/sources/pallas_call | solution.py:750
  27.3 0.1 collective-permute-start.1
  27.4 1.6 %collective-permute-done.from_odd = f32[120,128]{1,0:T(8,128)S(1)} collective-permute-done((f32[120,128]{1,0:T(8,128)S(1)}, f32[120,128]{1,0:T(8,128)S(1)}, u32[]{:S(2)}, u32[]{:S(2)}) %collective-permute-start) | collective-permute-done | bytes 61472 | tf_op jit(solution)/shard_map/ppermute | solution.py:640
  29.0 0.0 collective-permute-done.1.from_even
  29.0 0.3 strips.1
  29.3 0.7 %collective-permute-start.2 = (f32[56,128]{1,0:T(8,128)S(1)}, f32[56,128]{1,0:T(8,128)S(1)}, u32[]{:S(2)}, u32[]{:S(2)}) collective-permute-start(f32[56,128]{1,0:T(8,128)S(1)} %get-tuple-element.24), channel_id=1, source_target_pairs={{1,2},{2,1},{3,4},{4,3},{5,6},{6,5},{9,10},{10,9},{11,12},{12,11},... | collective-permute-start | bytes 86024 | tf_op jit(solution)/shard_map/ppermute | solution.py:640
  30.0 2.3 %collective-permute-start.3 = (f32[56,128]{1,0:T(8,128)S(1)}, f32[56,128]{1,0:T(8,128)S(1)}, u32[]{:S(2)}, u32[]{:S(2)}) collective-permute-start(f32[56,128]{1,0:T(8,128)S(1)} %get-tuple-element.25), channel_id=1, source_target_pairs={{0,1},{1,0},{2,3},{3,2},{4,5},{5,4},{6,7},{7,6},{8,9},{9,8},{10,11... | collective-permute-start | bytes 86024 | tf_op jit(solution)/shard_map/ppermute | solution.py:640
  32.3 0.0 collective-permute-done.2.from_odd
  32.3 1.3 %collective-permute-done.3.from_even = f32[56,128]{1,0:T(8,128)S(1)} collective-permute-done((f32[56,128]{1,0:T(8,128)S(1)}, f32[56,128]{1,0:T(8,128)S(1)}, u32[]{:S(2)}, u32[]{:S(2)}) %collective-permute-start.3) | collective-permute-done | bytes 28704 | tf_op jit(solution)/shard_map/ppermute | solution.py:640
  33.5 3.1 %ocean.1 = (f32[32,128]{1,0:T(8,128)}, f32[384,128]{1,0:T(8,128)S(1)}) custom-call(f32[896,128]{1,0:T(8,128)S(1)} %get-tuple-element.23.tall, f32[56,128]{1,0:T(8,128)S(1)} %collective-permute-done.2.from_odd, f32[56,128]{1,0:T(8,128)S(1)} %collective-permute-done.3.from_even, f32[32,128]{1,0:T(8,128)S(1)} %get-tuple-element.26.row_labels, ...), custom_call_target="tpu_custom_call" | custom-call | tf_op jit(solution)/shard_map/ocean/pallas_call | solution.py:779
  36.6 13.9 %all_to_all.11 = f32[32,1,1536]{2,1,0:T(1,128)S(1)} all-to-all(f32[32,1,1536]{2,1,0:T(1,128)S(1)} %bitcast.13), channel_id=1, replica_groups=mesh['river'=4,'coast'=8] {'coast','river'}, dimensions={0} | all-to-all | bytes 393216 | tf_op jit(solution)/shard_map/all_to_all | solution.py:632
  50.6 1.3 %mouths.1 = f32[64,384]{1,0:T(8,128)} custom-call(f32[384,128]{1,0:T(8,128)S(1)} %bitcast.9, s32[16,128]{1,0:T(8,128)S(1)} %get-tuple-element.30.address), custom_call_target="tpu_custom_call" | custom-call | tf_op jit(solution)/shard_map/mouths/pallas_call | solution.py:796
Async XLA Ops:
  23.5 5.5 %collective-permute-start = (f32[120,128]{1,0:T(8,128)S(1)}, f32[120,128]{1,0:T(8,128)S(1)}, u32[]{:S(2)}, u32[]{:S(2)}) collective-permute-start(f32[120,128]{1,0:T(8,128)S(1)} %get-tuple-element.21), channel_id=1, source_target_pairs={{8,16},{16,8},{9,17},{17,9},{10,18},{18,10},{11,19},{19,11},{12,20... | collective-permute-start | bytes 184328 | tf_op jit(solution)/shard_map/ppermute | solution.py:640
  27.3 1.7 %collective-permute-start.1 = (f32[120,128]{1,0:T(8,128)S(1)}, f32[120,128]{1,0:T(8,128)S(1)}, u32[]{:S(2)}, u32[]{:S(2)}) collective-permute-start(f32[120,128]{1,0:T(8,128)S(1)} %get-tuple-element.22), channel_id=1, source_target_pairs={{0,8},{8,0},{16,24},{24,16},{1,9},{9,1},{17,25},{25,17},{2,10},{10... | collective-permute-start | bytes 184328 | tf_op jit(solution)/shard_map/ppermute | solution.py:640
  29.3 3.0 %collective-permute-start.2 = (f32[56,128]{1,0:T(8,128)S(1)}, f32[56,128]{1,0:T(8,128)S(1)}, u32[]{:S(2)}, u32[]{:S(2)}) collective-permute-start(f32[56,128]{1,0:T(8,128)S(1)} %get-tuple-element.24), channel_id=1, source_target_pairs={{1,2},{2,1},{3,4},{4,3},{5,6},{6,5},{9,10},{10,9},{11,12},{12,11},... | collective-permute-start | bytes 86024 | tf_op jit(solution)/shard_map/ppermute | solution.py:640
  30.0 3.6 %collective-permute-start.3 = (f32[56,128]{1,0:T(8,128)S(1)}, f32[56,128]{1,0:T(8,128)S(1)}, u32[]{:S(2)}, u32[]{:S(2)}) collective-permute-start(f32[56,128]{1,0:T(8,128)S(1)} %get-tuple-element.25), channel_id=1, source_target_pairs={{0,1},{1,0},{2,3},{3,2},{4,5},{5,4},{6,7},{7,6},{8,9},{9,8},{10,11... | collective-permute-start | bytes 86024 | tf_op jit(solution)/shard_map/ppermute | solution.py:640

commit v6 on v5

--- a/solution.py
+++ b/solution.py
@@ -126,14 +126,29 @@
     capacity,
     *refs,
 ):
-    inputs, (depth_out, send_out, address_out), refs = refs[:10], refs[10:13], refs[13:]
+    inputs, (depth_out, send_out, address_out, sea_out), refs = refs[:15], refs[15:19], refs[19:]
+    arrivals = refs[15]
     copies = [
-        pltpu.make_async_copy(whole, own, refs[10].at[number])
-        for number, (whole, own) in enumerate(zip(inputs, refs[:10]))
+        pltpu.make_async_copy(whole, own, arrivals.at[number])
+        for number, (whole, own) in enumerate(zip(inputs, refs[:15]))
     ]
-    for copy in copies[::-1]:
+    copies, of_sea = copies[:10], copies[10:]
+    for copy in copies[::-1] + of_sea:
         copy.start()
-    river_steps(devices, coasts, capacity, copies, *refs[:10], depth_out, send_out, address_out, *refs[10:])
+    outputs = (depth_out, send_out, address_out)
+    finished = river_steps(
+        devices, coasts, capacity, copies, *refs[:10], *outputs, arrivals, *refs[16:]
+    )
+
+    sea_level, sea_bed, wet_mask, flux_east, flux_north = refs[10:15]
+    tile_rows = sea_level.shape[0]
+    for copy in of_sea:
+        copy.wait()
+    bed = sea_bed[...]
+    level = jnp.where(wet_mask[...] == 1, jnp.maximum(sea_level[...], bed), bed)
+    for number, value in enumerate((level, bed, flux_east[...], flux_north[...])):
+        sea_out[number * tile_rows : (number + 1) * tile_rows] = value
+    finished.wait()
 
 
 def river_steps(
@@ -174,7 +189,7 @@
     inland = RB - MPB
     lane = lax.broadcasted_iota(i32, (blocks, RB), 1)
 
-    for copy in copies:
+    for copy in copies[7:]:
         copy.wait()
 
     turned[...] = jnp.zeros_like(turned)
@@ -197,6 +212,8 @@
     tile = grouped(mouths, 0).astype(i32)
     tiles[...] = tile % coasts * (devices // coasts) + tile // coasts
     series[STEPS * rows :] = grouped(mouths, MPB)
+    for copy in copies[:7]:
+        copy.wait()
 
     into = into_in[...]
     at_mouth = lane >= inland
@@ -325,12 +342,12 @@
         for work in beside.get(substep, []):
             work()
     depth_end[...] = depth
-    finished = pltpu.make_async_copy(depth_end, depth_out, arrivals.at[len(copies)])
+    finished = pltpu.make_async_copy(depth_end, depth_out, arrivals.at[15])
     finished.start()
     for group in range(4):
         place_series(2, group)
     pack(2)
-    finished.wait()
+    return finished
 
 
 def reach_of(field):
@@ -373,19 +390,12 @@
     return both[:half] + both[half:]
 
 
-def edge_kernel(arrived, *refs):
-    inputs, (odd, sea), refs = refs[:5], refs[5:7], refs[7:]
-    sea_level, sea_bed, wet_mask, flux_east, flux_north, arrivals = refs[:6]
-    owner, places, row_labels, column_labels, lhs, rhs, sums = refs[6:]
+def edge_kernel(arrived, sea, odd, sea_out, *refs):
+    owner, places, row_labels, column_labels, lhs, rhs, sums = refs
     first_of_pair = lax.axis_index("river") % 2 == 0
-    copies = [
-        pltpu.make_async_copy(whole, own, arrivals.at[number])
-        for number, (whole, own) in enumerate(zip(inputs, refs[:5]))
-    ]
-    for copy in copies:
-        copy.start()
     groups = arrived.shape[0] // SENT
-    tile_rows, tile_cols = sea_level.shape
+    tile_rows, tile_cols = sea.shape[0] // 4, sea.shape[1]
+    sea_out[...] = sea[...]
 
     cells = arrived[pl.ds(STEPS, groups, stride=SENT)].astype(i32)
     row, column = split_label(cells, tile_cols)
@@ -414,12 +424,8 @@
         ]
         rows = jnp.concatenate(halves, axis=0)
         put(step, rows, rows)
-    for copy in copies:
-        copy.wait()
-    bed = sea_bed[...]
-    level = jnp.where(wet_mask[...] == 1, jnp.maximum(sea_level[...], bed), bed)
-    for number, value in enumerate((level, bed, flux_east[...], flux_north[...])):
-        sea[number * tile_rows : (number + 1) * tile_rows] = value
+    for number in range(4):
+        value = sea[number * tile_rows : (number + 1) * tile_rows]
         put(STEPS + number, value, value)
 
 
@@ -567,20 +573,22 @@
     finished.wait()
 
 
-def mouth_kernel(returned, address, level_out, whole, series, hot, block, departures):
-    rows = address.shape[0]
-    groups = LANES // MPB
+def column_kernel(address, _, hot, labels):
     place = lax.broadcasted_iota(i32, (TALL, 2 * LANES), 0).astype(f32).astype(bf16)
 
     def place_of(label, part):
         return label - part == place
 
-    labels = []
-    for i in range(0, rows, 2):
+    for i in range(0, address.shape[0], 2):
         pair = jnp.concatenate([address[i : i + 1], address[i + 1 : i + 2]], axis=1)
         high, low = [label.astype(f32) for label in split_label(pair, WIDE)]
         one_hot_columns(low, place_of, hot, slice(i * LANES, (i + 2) * LANES))
-        labels.append(high)
+        labels[i // 2 : i // 2 + 1] = high
+
+
+def mouth_kernel(returned, hot, labels, level_out, whole, series, block, departures):
+    rows = hot.shape[1] // LANES
+    groups = LANES // MPB
     lane = lax.broadcasted_iota(i32, (rows, LANES), 1)
     copies = []
     for first, steps in LOOKED_UP:
@@ -594,7 +602,7 @@
         table = jnp.concatenate(in_two(own), axis=0)
         for i in range(0, rows, 2):
             lanes = slice(i * LANES, (i + 2) * LANES)
-            found = look_up(table, labels[i // 2], hot[:, lanes], steps)
+            found = look_up(table, labels[i // 2 : i // 2 + 1], hot[:, lanes], steps)
             series[pl.ds(first * rows + i, steps, stride=rows)] = found[:, :LANES]
             series[pl.ds(first * rows + i + 1, steps, stride=rows)] = found[:, LANES:]
         for number in range(first // groups, (first + steps) // groups):
@@ -666,17 +674,19 @@
     rows = mouths // LANES
     height = tile_rows + 2 * HALO
 
-    depth_after, sending, address = pl.pallas_call(
+    depth_after, sending, address, sea = pl.pallas_call(
         functools.partial(river_kernel, devices, lax.axis_size("coast"), capacity),
         name="river",
         out_shape=(
             shape(blocks, RB),
             shape(groups * SENT, LANES),
             shape(rows, LANES, dtype=i32),
+            shape(4 * tile_rows, tile_cols),
         ),
-        in_specs=[pl.BlockSpec(memory_space=pltpu.HBM)] * 10,
+        in_specs=[pl.BlockSpec(memory_space=pltpu.HBM)] * 15,
         out_specs=(
             pl.BlockSpec(memory_space=pltpu.HBM),
+            pl.BlockSpec(memory_space=pltpu.VMEM),
             pl.BlockSpec(memory_space=pltpu.VMEM),
             pl.BlockSpec(memory_space=pltpu.VMEM),
         ),
@@ -686,7 +696,12 @@
             pltpu.VMEM((MPB, blocks), f32),
             pltpu.VMEM((MPB, blocks), i32),
             pltpu.VMEM((MPB, blocks), i32),
-            pltpu.SemaphoreType.DMA((11,)),
+            pltpu.VMEM((tile_rows, tile_cols), f32),
+            pltpu.VMEM((tile_rows, tile_cols), f32),
+            pltpu.VMEM((tile_rows, tile_cols), i32),
+            pltpu.VMEM((tile_rows, tile_cols), f32),
+            pltpu.VMEM((tile_rows, tile_cols), f32),
+            pltpu.SemaphoreType.DMA((16,)),
             pltpu.VMEM((blocks, RB), f32),
             pltpu.VMEM((reach_offsets, blocks, RB), f32),
             pltpu.VMEM((SENT * rows, LANES), f32),
@@ -716,6 +731,11 @@
             mouth_prev.T,
             mouth_tile[:, :, 0].T,
             mouth_cell.T,
+            sea_level,
+            sea_bed,
+            wet_mask,
+            flux_east,
+            flux_north,
         )
     )
     arrived = swap(sending, SENT, devices, capacity)
@@ -725,15 +745,7 @@
         edge_kernel,
         name="edges",
         out_shape=(shape(ROWS_SENT, LANES), shape(4 * tile_rows, tile_cols)),
-        in_specs=[pl.BlockSpec(memory_space=pltpu.VMEM)]
-        + [pl.BlockSpec(memory_space=pltpu.HBM)] * 5,
         scratch_shapes=[
-            pltpu.VMEM((tile_rows, tile_cols), f32),
-            pltpu.VMEM((tile_rows, tile_cols), f32),
-            pltpu.VMEM((tile_rows, tile_cols), i32),
-            pltpu.VMEM((tile_rows, tile_cols), f32),
-            pltpu.VMEM((tile_rows, tile_cols), f32),
-            pltpu.SemaphoreType.DMA((5,)),
             pltpu.VMEM((edge_rows, LANES), bf16),
             pltpu.VMEM((WIDE, LANES), bf16),
             pltpu.VMEM((groups, LANES), f32),
@@ -744,7 +756,7 @@
         ],
         cost_estimate=cost(2 * edge_rows * WIDE * groups * LANES),
         compiler_params=PARAMS,
-    )(arrived, *in_hbm(sea_level, sea_bed, wet_mask, flux_east, flux_north))
+    )(arrived, sea)
     from_odd = with_neighbour(odd, "river", 1)
 
     fields, even, hot, labels = pl.pallas_call(
@@ -768,6 +780,18 @@
     )(arrived, sea)
     from_even = with_neighbour(even, "river", 0)
 
+    slot_hot, slot_labels = pl.pallas_call(
+        column_kernel,
+        name="columns",
+        out_shape=(shape(WIDE, mouths, dtype=bf16), shape(rows // 2, 2 * LANES)),
+        in_specs=[
+            pl.BlockSpec(memory_space=pltpu.VMEM),
+            pl.BlockSpec(memory_space=pl.ANY),
+        ],
+        cost_estimate=cost(WIDE * mouths * LANES),
+        compiler_params=PARAMS,
+    )(address, labels)
+
     tall, odd, even = pl.pallas_call(
         strip_kernel,
         name="strips",
@@ -800,13 +824,12 @@
         scratch_shapes=[
             pltpu.VMEM((TALL * STEPS, WIDE), f32),
             pltpu.VMEM((STEPS * rows, LANES), f32),
-            pltpu.VMEM((WIDE, mouths), bf16),
             pltpu.VMEM((STEPS * MPB // LANES, blocks, LANES), f32),
             pltpu.SemaphoreType.DMA((STEPS * MPB // LANES,)),
         ],
         out_specs=pl.BlockSpec(memory_space=pltpu.HBM),
         compiler_params=PARAMS,
-    )(returned, address)
+    )(returned, slot_hot, slot_labels)
     return (depth_after, level_after, mouth_level)
 
 

time: 52.2 us -> 53.6 us (1.027)
  blocking collectives: 30.3 us -> 16.4 us
  waiting for transfers between devices: 2.87 us -> 11.9 us
  starting transfers between devices: 5.27 us -> 10.2 us
  Pallas kernels: 12.8 us -> 14.1 us
    all_to_all x2 -> x1, blocking collectives: 30.3 us -> 16.4 us  [swap(): lax.all_to_all(values, ('coast', 'river'), split_axis=0, concat_axis=0, t...]
    all_to_all x0 -> x1, waiting for transfers between devices: none -> 9.05 us  [swap(): lax.all_to_all(values, ('coast', 'river'), split_axis=0, concat_axis=0, t...]
    all_to_all x0 -> x1, starting transfers between devices: none -> 4.92 us  [swap(): lax.all_to_all(values, ('coast', 'river'), split_axis=0, concat_axis=0, t...]
    pallas_call x1, Pallas kernels: 3.11 us -> 3.8 us  [per_device(): pl.pallas_call(functools.partial(ocean_kernel, tile_rows), name='ocean',...]
    pallas_call x1, Pallas kernels: 5.19 us -> 5.77 us  [per_device(): pl.pallas_call(functools.partial(river_kernel, devices, lax.axis_size('co...]
  transfers between devices with their start and end apart: 4 -> 5, of which waited for: 2 -> 3; matrix products, arithmetic and copies ran while one was open for 0% -> 0% of each run, Pallas kernels for 3% -> 3%
where the time goes in v6:
time: 53.6 us; the launch traced here: 53.3 us
  blocking collectives  16.4 us (31%)
  Pallas kernels  14.1 us (26%)
  waiting for transfers between devices  11.9 us (22%)
  starting transfers between devices  10.2 us (19%)
  between operations  0.72 us (1%)
    all_to_all x1, blocking collectives, swap(): lax.all_to_all(values, ('coast', 'river'), split_axis=0, concat_axis=0, t...  16.4 us
    all_to_all x1, waiting for transfers between devices, swap(): lax.all_to_all(values, ('coast', 'river'), split_axis=0, concat_axis=0, t...  9.05 us
    pallas_call x1, Pallas kernels, per_device(): pl.pallas_call(functools.partial(river_kernel, devices, lax.axis_size('co...  5.77 us
    ppermute x4, starting transfers between devices, with_neighbour(): lax.ppermute(value, axis, [(i + k, i + 1 - k) for i in pairs for k in ran...  5.27 us
    all_to_all x1, starting transfers between devices, swap(): lax.all_to_all(values, ('coast', 'river'), split_axis=0, concat_axis=0, t...  4.92 us
    pallas_call x1, Pallas kernels, per_device(): pl.pallas_call(functools.partial(ocean_kernel, tile_rows), name='ocean',...  3.8 us
    ppermute x4, waiting for transfers between devices, with_neighbour(): lax.ppermute(value, axis, [(i + k, i + 1 - k) for i in pairs for k in ran...  2.87 us
    pallas_call x1, Pallas kernels, per_device(): pl.pallas_call(source_kernel, name='sources', out_shape=(shape(FIELDS * t...  1.62 us
  transfers between devices with their start and end apart: 5, of which 3 were waited for; matrix products, arithmetic and copies ran while one was open for 0% of the time, Pallas kernels for 3%

profile of v6, /device:TPU:1, one launch (start us, length us, event | category | flops | bytes accessed | tf_op | source)
XLA Modules:
  0.0 53.3 jit_solution(17980026572641638295)
XLA Ops:
  0.6 5.8 %river.1 = (f32[64,128]{1,0:T(8,128)}, f32[416,128]{1,0:T(8,128)S(1)}, s32[16,128]{1,0:T(8,128)S(1)}, f32[128,128]{1,0:T(8,128)S(1)}) custom-call(f32[64,128]{1,0:T(8,128)} %refs_0_.1, f32[64,128]{1,0:T(8,128)} %refs_1_.1, f32[64,128]{1,0:T(8,128)} %refs_2_.1, f32[64,128]{1,0:T(8,128)} %refs_3_.1, f32[64,128]{1,0:T(8,128)} %refs_4_.1, f32[64,128]{1,0:T(8,128)} %refs_5_.1, ...), custom_call_target="tpu_custom_call" | custom-call | tf_op jit(solution)/shard_map/river/pallas_call | solution.py:677
  6.4 16.4 %all_to_all.10 = f32[32,1,1664]{2,1,0:T(1,128)S(1)} all-to-all(f32[32,1,1664]{2,1,0:T(1,128)S(1)} %bitcast.12), channel_id=1, replica_groups=mesh['river'=4,'coast'=8] {'coast','river'}, dimensions={0} | all-to-all | bytes 425984 | tf_op jit(solution)/shard_map/all_to_all | solution.py:640
  22.8 1.2 %edges.1 = (f32[120,128]{1,0:T(8,128)S(1)}, f32[128,128]{1,0:T(8,128)S(1)}) custom-call(f32[416,128]{1,0:T(8,128)S(1)} %bitcast.10, f32[128,128]{1,0:T(8,128)S(1)} %get-tuple-element.22.sea), custom_call_target="tpu_custom_call" | custom-call | flops 335544320 | bytes 8388608 | tf_op jit(solution)/shard_map/edges/pallas_call | solution.py:744
  24.0 2.2 %collective-permute-start = (f32[120,128]{1,0:T(8,128)S(1)}, f32[120,128]{1,0:T(8,128)S(1)}, u32[]{:S(2)}, u32[]{:S(2)}) collective-permute-start(f32[120,128]{1,0:T(8,128)S(1)} %get-tuple-element.25), channel_id=1, source_target_pairs={{8,16},{16,8},{9,17},{17,9},{10,18},{18,10},{11,19},{19,11},{12,20... | collective-permute-start | bytes 184328 | tf_op jit(solution)/shard_map/ppermute | solution.py:648
  26.2 1.6 %sources.1 = (f32[512,128]{1,0:T(8,128)S(1)}, f32[120,128]{1,0:T(8,128)S(1)}, bf16[256,4096]{1,0:T(8,128)(2,1)S(1)}, f32[32,128]{1,0:T(8,128)S(1)}) custom-call(f32[416,128]{1,0:T(8,128)S(1)} %bitcast.11, f32[128,128]{1,0:T(8,128)S(1)} %get-tuple-element.23.sea), custom_call_target="tpu_custom_call" | custom-call | flops 805306368 | bytes 8388608 | tf_op jit(solution)/shard_map/sources/pallas_call | solution.py:762
  27.8 0.1 collective-permute-start.1
  27.9 1.6 %collective-permute-done.from_odd = f32[120,128]{1,0:T(8,128)S(1)} collective-permute-done((f32[120,128]{1,0:T(8,128)S(1)}, f32[120,128]{1,0:T(8,128)S(1)}, u32[]{:S(2)}, u32[]{:S(2)}) %collective-permute-start) | collective-permute-done | bytes 61472 | tf_op jit(solution)/shard_map/ppermute | solution.py:648
  29.5 0.0 collective-permute-done.1.from_even
  29.5 0.3 strips.1
  29.8 0.7 %collective-permute-start.2 = (f32[56,128]{1,0:T(8,128)S(1)}, f32[56,128]{1,0:T(8,128)S(1)}, u32[]{:S(2)}, u32[]{:S(2)}) collective-permute-start(f32[56,128]{1,0:T(8,128)S(1)} %get-tuple-element.28), channel_id=1, source_target_pairs={{1,2},{2,1},{3,4},{4,3},{5,6},{6,5},{9,10},{10,9},{11,12},{12,11},... | collective-permute-start | bytes 86024 | tf_op jit(solution)/shard_map/ppermute | solution.py:648
  30.5 2.3 %collective-permute-start.3 = (f32[56,128]{1,0:T(8,128)S(1)}, f32[56,128]{1,0:T(8,128)S(1)}, u32[]{:S(2)}, u32[]{:S(2)}) collective-permute-start(f32[56,128]{1,0:T(8,128)S(1)} %get-tuple-element.29), channel_id=1, source_target_pairs={{0,1},{1,0},{2,3},{3,2},{4,5},{5,4},{6,7},{7,6},{8,9},{9,8},{10,11... | collective-permute-start | bytes 86024 | tf_op jit(solution)/shard_map/ppermute | solution.py:648
  32.8 0.0 collective-permute-done.2.from_odd
  32.8 1.3 %collective-permute-done.3.from_even = f32[56,128]{1,0:T(8,128)S(1)} collective-permute-done((f32[56,128]{1,0:T(8,128)S(1)}, f32[56,128]{1,0:T(8,128)S(1)}, u32[]{:S(2)}, u32[]{:S(2)}) %collective-permute-start.3) | collective-permute-done | bytes 28704 | tf_op jit(solution)/shard_map/ppermute | solution.py:648
  34.0 3.8 %ocean.1 = (f32[32,128]{1,0:T(8,128)}, f32[384,128]{1,0:T(8,128)}) custom-call(f32[896,128]{1,0:T(8,128)S(1)} %get-tuple-element.27.tall, f32[56,128]{1,0:T(8,128)S(1)} %collective-permute-done.2.from_odd, f32[56,128]{1,0:T(8,128)S(1)} %collective-permute-done.3.from_even, f32[32,128]{1,0:T(8,128)S(1)} %get-tuple-element.30.row_labels._, ...), custom_call_target="tpu_custom_call" | custom-call | tf_op jit(solution)/shard_map/ocean/pallas_call | solution.py:803
  37.8 4.9 %all-to-all-start.1 = ((f32[32,1,1536]{2,1,0:T(1,128)}), f32[32,1,1536]{2,1,0:T(1,128)S(1)}, u32[]{:S(2)}, u32[]{:S(2)}) async-start(f32[32,1,1536]{2,1,0:T(1,128)} %bitcast.6), calls=%async_computation.1 | async-start | bytes 393216 | tf_op jit(solution)/shard_map/all_to_all | solution.py:640
  42.8 0.2 columns.1
  43.0 9.1 %all-to-all-done.1 = f32[32,1,1536]{2,1,0:T(1,128)S(1)} async-done(((f32[32,1,1536]{2,1,0:T(1,128)}), f32[32,1,1536]{2,1,0:T(1,128)S(1)}, u32[]{:S(2)}, u32[]{:S(2)}) %all-to-all-start.1) | async-done | bytes 196640 | tf_op jit(solution)/shard_map/all_to_all | solution.py:640
  52.0 1.3 %mouths.1 = f32[64,384]{1,0:T(8,128)} custom-call(f32[384,128]{1,0:T(8,128)S(1)} %bitcast.9, bf16[256,2048]{1,0:T(8,128)(2,1)S(1)} %get-tuple-element.35.hot, f32[8,256]{1,0:T(8,128)S(1)} %get-tuple-element.36.labels), custom_call_target="tpu_custom_call" | custom-call | tf_op jit(solution)/shard_map/mouths/pallas_call | solution.py:820
Async XLA Ops:
  24.0 5.5 %collective-permute-start = (f32[120,128]{1,0:T(8,128)S(1)}, f32[120,128]{1,0:T(8,128)S(1)}, u32[]{:S(2)}, u32[]{:S(2)}) collective-permute-start(f32[120,128]{1,0:T(8,128)S(1)} %get-tuple-element.25), channel_id=1, source_target_pairs={{8,16},{16,8},{9,17},{17,9},{10,18},{18,10},{11,19},{19,11},{12,20... | collective-permute-start | bytes 184328 | tf_op jit(solution)/shard_map/ppermute | solution.py:648
  27.8 1.7 %collective-permute-start.1 = (f32[120,128]{1,0:T(8,128)S(1)}, f32[120,128]{1,0:T(8,128)S(1)}, u32[]{:S(2)}, u32[]{:S(2)}) collective-permute-start(f32[120,128]{1,0:T(8,128)S(1)} %get-tuple-element.26), channel_id=1, source_target_pairs={{0,8},{8,0},{16,24},{24,16},{1,9},{9,1},{17,25},{25,17},{2,10},{10... | collective-permute-start | bytes 184328 | tf_op jit(solution)/shard_map/ppermute | solution.py:648
  29.8 3.0 %collective-permute-start.2 = (f32[56,128]{1,0:T(8,128)S(1)}, f32[56,128]{1,0:T(8,128)S(1)}, u32[]{:S(2)}, u32[]{:S(2)}) collective-permute-start(f32[56,128]{1,0:T(8,128)S(1)} %get-tuple-element.28), channel_id=1, source_target_pairs={{1,2},{2,1},{3,4},{4,3},{5,6},{6,5},{9,10},{10,9},{11,12},{12,11},... | collective-permute-start | bytes 86024 | tf_op jit(solution)/shard_map/ppermute | solution.py:648
  30.5 3.6 %collective-permute-start.3 = (f32[56,128]{1,0:T(8,128)S(1)}, f32[56,128]{1,0:T(8,128)S(1)}, u32[]{:S(2)}, u32[]{:S(2)}) collective-permute-start(f32[56,128]{1,0:T(8,128)S(1)} %get-tuple-element.29), channel_id=1, source_target_pairs={{0,1},{1,0},{2,3},{3,2},{4,5},{5,4},{6,7},{7,6},{8,9},{9,8},{10,11... | collective-permute-start | bytes 86024 | tf_op jit(solution)/shard_map/ppermute | solution.py:648
  37.8 14.2 %all-to-all-start.1 = ((f32[32,1,1536]{2,1,0:T(1,128)}), f32[32,1,1536]{2,1,0:T(1,128)S(1)}, u32[]{:S(2)}, u32[]{:S(2)}) async-start(f32[32,1,1536]{2,1,0:T(1,128)} %bitcast.6), calls=%async_computation.1 | async-start | bytes 393216 | tf_op jit(solution)/shard_map/all_to_all | solution.py:640

commit v7 on v6

--- a/solution.py
+++ b/solution.py
@@ -189,7 +189,7 @@
     inland = RB - MPB
     lane = lax.broadcasted_iota(i32, (blocks, RB), 1)
 
-    for copy in copies[7:]:
+    for copy in copies:
         copy.wait()
 
     turned[...] = jnp.zeros_like(turned)
@@ -212,8 +212,6 @@
     tile = grouped(mouths, 0).astype(i32)
     tiles[...] = tile % coasts * (devices // coasts) + tile // coasts
     series[STEPS * rows :] = grouped(mouths, MPB)
-    for copy in copies[:7]:
-        copy.wait()
 
     into = into_in[...]
     at_mouth = lane >= inland
@@ -390,46 +388,7 @@
     return both[:half] + both[half:]
 
 
-def edge_kernel(arrived, sea, odd, sea_out, *refs):
-    owner, places, row_labels, column_labels, lhs, rhs, sums = refs
-    first_of_pair = lax.axis_index("river") % 2 == 0
-    groups = arrived.shape[0] // SENT
-    tile_rows, tile_cols = sea.shape[0] // 4, sea.shape[1]
-    sea_out[...] = sea[...]
-
-    cells = arrived[pl.ds(STEPS, groups, stride=SENT)].astype(i32)
-    row, column = split_label(cells, tile_cols)
-    row = row - jnp.where(first_of_pair, 0, tile_rows - HALO)
-    upper = jnp.where(row >= HALO // 2, 1, 0)
-    inside = (row >= 0) & (row < HALO)
-    row_labels[...] = jnp.where(inside, row - upper * (HALO // 2), WIDE - 1).astype(f32)
-    column_labels[...] = (column + upper * tile_cols).astype(f32)
-    total = add_in_chunks(arrived, row_labels, column_labels, owner, places, lhs, rhs)
-    high_rows = total.shape[0]
-    for half in range(2):
-        part = slice(half * high_rows, (half + 1) * high_rows)
-        sums[part] = total[:, half * LANES : (half + 1) * LANES]
-
-    def put(field, start, end):
-        reach = reach_of(field)
-        if reach:
-            last, first = end[end.shape[0] - reach :], start[:reach]
-            part = slice(ROW_AT[field], ROW_AT[field] + reach)
-            odd[part] = jnp.where(first_of_pair, first, last)
-
-    odd[ROWS_SENT - 8 :] = jnp.zeros((8, LANES), f32)
-    for step in range(STEPS):
-        halves = [
-            sums[pl.ds(half * high_rows + step, HALO // 2, stride=STEPS)] for half in range(2)
-        ]
-        rows = jnp.concatenate(halves, axis=0)
-        put(step, rows, rows)
-    for number in range(4):
-        value = sea[number * tile_rows : (number + 1) * tile_rows]
-        put(STEPS + number, value, value)
-
-
-def source_kernel(arrived, sea, fields, even, rhs, label_out, *refs):
+def source_kernel(arrived, sea, fields, odd, even, rhs, label_out, *refs):
     owner, places, column_labels, lhs, sums = refs
     first_of_pair = lax.axis_index("river") % 2 == 0
     groups = arrived.shape[0] // SENT
@@ -451,9 +410,11 @@
         if reach:
             last, first = value[tile_rows - reach :], value[:reach]
             part = slice(ROW_AT[field], ROW_AT[field] + reach)
+            odd[part] = jnp.where(first_of_pair, first, last)
             even[part] = jnp.where(first_of_pair, last, first)
 
-    even[ROWS_SENT - 8 :] = jnp.zeros((8, LANES), f32)
+    for message in (odd, even):
+        message[ROWS_SENT - 8 :] = jnp.zeros((8, LANES), f32)
     for step in range(STEPS):
         halves = [sums[pl.ds(half * high_rows + step, TALL, stride=STEPS)] for half in range(2)]
         put(step, jnp.concatenate(halves, axis=0))
@@ -573,22 +534,20 @@
     finished.wait()
 
 
-def column_kernel(address, _, hot, labels):
+def mouth_kernel(returned, address, level_out, whole, series, hot, block, departures):
+    rows = address.shape[0]
+    groups = LANES // MPB
     place = lax.broadcasted_iota(i32, (TALL, 2 * LANES), 0).astype(f32).astype(bf16)
 
     def place_of(label, part):
         return label - part == place
 
-    for i in range(0, address.shape[0], 2):
+    labels = []
+    for i in range(0, rows, 2):
         pair = jnp.concatenate([address[i : i + 1], address[i + 1 : i + 2]], axis=1)
         high, low = [label.astype(f32) for label in split_label(pair, WIDE)]
         one_hot_columns(low, place_of, hot, slice(i * LANES, (i + 2) * LANES))
-        labels[i // 2 : i // 2 + 1] = high
-
-
-def mouth_kernel(returned, hot, labels, level_out, whole, series, block, departures):
-    rows = hot.shape[1] // LANES
-    groups = LANES // MPB
+        labels.append(high)
     lane = lax.broadcasted_iota(i32, (rows, LANES), 1)
     copies = []
     for first, steps in LOOKED_UP:
@@ -602,7 +561,7 @@
         table = jnp.concatenate(in_two(own), axis=0)
         for i in range(0, rows, 2):
             lanes = slice(i * LANES, (i + 2) * LANES)
-            found = look_up(table, labels[i // 2 : i // 2 + 1], hot[:, lanes], steps)
+            found = look_up(table, labels[i // 2], hot[:, lanes], steps)
             series[pl.ds(first * rows + i, steps, stride=rows)] = found[:, :LANES]
             series[pl.ds(first * rows + i + 1, steps, stride=rows)] = found[:, LANES:]
         for number in range(first // groups, (first + steps) // groups):
@@ -622,10 +581,6 @@
 
 def shape(*dims, dtype=f32):
     return jax.ShapeDtypeStruct(dims, dtype)
-
-
-def cost(products):
-    return pl.CostEstimate(flops=2 * products, bytes_accessed=8 << 20, transcendentals=0)
 
 
 def in_hbm(*arrays):
@@ -740,30 +695,12 @@
     )
     arrived = swap(sending, SENT, devices, capacity)
 
-    edge_rows = -(-HALO // 2 * STEPS // TALL) * TALL
-    odd, sea = pl.pallas_call(
-        edge_kernel,
-        name="edges",
-        out_shape=(shape(ROWS_SENT, LANES), shape(4 * tile_rows, tile_cols)),
-        scratch_shapes=[
-            pltpu.VMEM((edge_rows, LANES), bf16),
-            pltpu.VMEM((WIDE, LANES), bf16),
-            pltpu.VMEM((groups, LANES), f32),
-            pltpu.VMEM((groups, LANES), f32),
-            pltpu.VMEM((2 * edge_rows, groups * LANES), bf16),
-            pltpu.VMEM((WIDE, groups * LANES), bf16),
-            pltpu.VMEM((2 * edge_rows, LANES), f32),
-        ],
-        cost_estimate=cost(2 * edge_rows * WIDE * groups * LANES),
-        compiler_params=PARAMS,
-    )(arrived, sea)
-    from_odd = with_neighbour(odd, "river", 1)
-
-    fields, even, hot, labels = pl.pallas_call(
+    fields, odd, even, hot, labels = pl.pallas_call(
         source_kernel,
         name="sources",
         out_shape=(
             shape(FIELDS * tile_rows, LANES),
+            shape(ROWS_SENT, LANES),
             shape(ROWS_SENT, LANES),
             shape(WIDE, groups * LANES, dtype=bf16),
             shape(groups, LANES),
@@ -775,22 +712,9 @@
             pltpu.VMEM((2 * TALL * STEPS, groups * LANES), bf16),
             pltpu.VMEM((2 * TALL * STEPS, LANES), f32),
         ],
-        cost_estimate=cost(2 * TALL * STEPS * WIDE * groups * LANES),
         compiler_params=PARAMS,
     )(arrived, sea)
-    from_even = with_neighbour(even, "river", 0)
-
-    slot_hot, slot_labels = pl.pallas_call(
-        column_kernel,
-        name="columns",
-        out_shape=(shape(WIDE, mouths, dtype=bf16), shape(rows // 2, 2 * LANES)),
-        in_specs=[
-            pl.BlockSpec(memory_space=pltpu.VMEM),
-            pl.BlockSpec(memory_space=pl.ANY),
-        ],
-        cost_estimate=cost(WIDE * mouths * LANES),
-        compiler_params=PARAMS,
-    )(address, labels)
+    from_odd, from_even = with_neighbour(odd, "river", 1), with_neighbour(even, "river", 0)
 
     tall, odd, even = pl.pallas_call(
         strip_kernel,
@@ -824,12 +748,13 @@
         scratch_shapes=[
             pltpu.VMEM((TALL * STEPS, WIDE), f32),
             pltpu.VMEM((STEPS * rows, LANES), f32),
+            pltpu.VMEM((WIDE, mouths), bf16),
             pltpu.VMEM((STEPS * MPB // LANES, blocks, LANES), f32),
             pltpu.SemaphoreType.DMA((STEPS * MPB // LANES,)),
         ],
         out_specs=pl.BlockSpec(memory_space=pltpu.HBM),
         compiler_params=PARAMS,
-    )(returned, slot_hot, slot_labels)
+    )(returned, address)
     return (depth_after, level_after, mouth_level)
 
 

time: 53.6 us -> 52.6 us (0.981)
  blocking collectives: 16.4 us -> 30.3 us
  waiting for transfers between devices: 11.9 us -> 4.5 us
  starting transfers between devices: 10.2 us -> 5.26 us
  Pallas kernels: 14.1 us -> 11.6 us
    all_to_all x1 -> x2, blocking collectives: 16.4 us -> 30.3 us  [swap(): lax.all_to_all(values, ('coast', 'river'), split_axis=0, concat_axis=0, t...]
    all_to_all x1 -> x0, waiting for transfers between devices: 9.05 us -> none  [swap(): lax.all_to_all(values, ('coast', 'river'), split_axis=0, concat_axis=0, t...]
    all_to_all x1 -> x0, starting transfers between devices: 4.92 us -> none  [swap(): lax.all_to_all(values, ('coast', 'river'), split_axis=0, concat_axis=0, t...]
    ppermute x4, waiting for transfers between devices: 2.87 us -> 4.5 us  [with_neighbour(): lax.ppermute(value, axis, [(i + k, i + 1 - k) for i in pairs for k in ran...]
    pallas_call x2 -> x0, Pallas kernels: 1.33 us -> none  [the longest x1 1.16 us: per_device(): pl.pallas_call(edge_kernel, name='edges', out_shape=(shape(ROWS_SENT, LAN...]
    pallas_call x1, Pallas kernels: 3.8 us -> 3.11 us  [per_device(): pl.pallas_call(functools.partial(ocean_kernel, tile_rows), name='ocean',...]
  transfers between devices with their start and end apart: 5 -> 4, of which waited for: 3 -> 2; matrix products, arithmetic and copies ran while one was open for 0% -> 0% of each run, Pallas kernels for 3% -> 0%
where the time goes in v7:
time: 52.6 us; the launch traced here: 52.4 us
  blocking collectives  30.3 us (58%)
  Pallas kernels  11.6 us (22%)
  starting transfers between devices  5.26 us (10%)
  waiting for transfers between devices  4.5 us (9%)
  between operations  0.7 us (1%)
    all_to_all x2, blocking collectives, swap(): lax.all_to_all(values, ('coast', 'river'), split_axis=0, concat_axis=0, t...  30.3 us
    ppermute x4, starting transfers between devices, with_neighbour(): lax.ppermute(value, axis, [(i + k, i + 1 - k) for i in pairs for k in ran...  5.26 us
    pallas_call x1, Pallas kernels, per_device(): pl.pallas_call(functools.partial(river_kernel, devices, lax.axis_size('co...  5.24 us
    ppermute x4, waiting for transfers between devices, with_neighbour(): lax.ppermute(value, axis, [(i + k, i + 1 - k) for i in pairs for k in ran...  4.5 us
    pallas_call x1, Pallas kernels, per_device(): pl.pallas_call(functools.partial(ocean_kernel, tile_rows), name='ocean',...  3.11 us
    pallas_call x1, Pallas kernels, per_device(): pl.pallas_call(source_kernel, name='sources', out_shape=(shape(FIELDS * t...  1.62 us
    pallas_call x1, Pallas kernels, per_device(): pl.pallas_call(mouth_kernel, name='mouths', out_shape=shape(blocks, STEPS...  1.34 us
  transfers between devices with their start and end apart: 4, of which 2 were waited for; matrix products, arithmetic and copies ran while one was open for 0% of the time, Pallas kernels for 0%

profile of v7, /device:TPU:1, one launch (start us, length us, event | category | flops | bytes accessed | tf_op | source)
XLA Modules:
  0.0 52.4 jit_solution(5721752112234520168)
XLA Ops:
  0.6 5.2 %river.1 = (f32[64,128]{1,0:T(8,128)}, f32[416,128]{1,0:T(8,128)S(1)}, s32[16,128]{1,0:T(8,128)S(1)}, f32[128,128]{1,0:T(8,128)S(1)}) custom-call(f32[64,128]{1,0:T(8,128)} %refs_0_.1, f32[64,128]{1,0:T(8,128)} %refs_1_.1, f32[64,128]{1,0:T(8,128)} %refs_2_.1, f32[64,128]{1,0:T(8,128)} %refs_3_.1, f32[64,128]{1,0:T(8,128)} %refs_4_.1, f32[64,128]{1,0:T(8,128)} %refs_5_.1, ...), custom_call_target="tpu_custom_call" | custom-call | tf_op jit(solution)/shard_map/river/pallas_call | solution.py:632
  5.9 16.4 %all_to_all.10 = f32[32,1,1664]{2,1,0:T(1,128)S(1)} all-to-all(f32[32,1,1664]{2,1,0:T(1,128)S(1)} %bitcast.11), channel_id=1, replica_groups=mesh['river'=4,'coast'=8] {'coast','river'}, dimensions={0} | all-to-all | bytes 425984 | tf_op jit(solution)/shard_map/all_to_all | solution.py:595
  22.3 1.6 %sources.1 = (f32[512,128]{1,0:T(8,128)S(1)}, f32[120,128]{1,0:T(8,128)S(1)}, f32[120,128]{1,0:T(8,128)S(1)}, bf16[256,4096]{1,0:T(8,128)(2,1)S(1)}, f32[32,128]{1,0:T(8,128)S(1)}) custom-call(f32[416,128]{1,0:T(8,128)S(1)} %bitcast.9, f32[128,128]{1,0:T(8,128)S(1)} %get-tuple-element.19.sea), custom_call_target="tpu_custom_call" | custom-call | tf_op jit(solution)/shard_map/sources/pallas_call | solution.py:698
  23.9 2.2 %collective-permute-start = (f32[120,128]{1,0:T(8,128)S(1)}, f32[120,128]{1,0:T(8,128)S(1)}, u32[]{:S(2)}, u32[]{:S(2)}) collective-permute-start(f32[120,128]{1,0:T(8,128)S(1)} %get-tuple-element.21), channel_id=1, source_target_pairs={{8,16},{16,8},{9,17},{17,9},{10,18},{18,10},{11,19},{19,11},{12,20... | collective-permute-start | bytes 184328 | tf_op jit(solution)/shard_map/ppermute | solution.py:603
  26.1 0.1 collective-permute-start.1
  26.2 3.2 %collective-permute-done.from_odd = f32[120,128]{1,0:T(8,128)S(1)} collective-permute-done((f32[120,128]{1,0:T(8,128)S(1)}, f32[120,128]{1,0:T(8,128)S(1)}, u32[]{:S(2)}, u32[]{:S(2)}) %collective-permute-start) | collective-permute-done | bytes 61472 | tf_op jit(solution)/shard_map/ppermute | solution.py:603
  29.4 0.0 collective-permute-done.1.from_even
  29.4 0.3 strips.1
  29.7 0.7 %collective-permute-start.2 = (f32[56,128]{1,0:T(8,128)S(1)}, f32[56,128]{1,0:T(8,128)S(1)}, u32[]{:S(2)}, u32[]{:S(2)}) collective-permute-start(f32[56,128]{1,0:T(8,128)S(1)} %get-tuple-element.24), channel_id=1, source_target_pairs={{1,2},{2,1},{3,4},{4,3},{5,6},{6,5},{9,10},{10,9},{11,12},{12,11},... | collective-permute-start | bytes 86024 | tf_op jit(solution)/shard_map/ppermute | solution.py:603
  30.4 2.3 %collective-permute-start.3 = (f32[56,128]{1,0:T(8,128)S(1)}, f32[56,128]{1,0:T(8,128)S(1)}, u32[]{:S(2)}, u32[]{:S(2)}) collective-permute-start(f32[56,128]{1,0:T(8,128)S(1)} %get-tuple-element.25), channel_id=1, source_target_pairs={{0,1},{1,0},{2,3},{3,2},{4,5},{5,4},{6,7},{7,6},{8,9},{9,8},{10,11... | collective-permute-start | bytes 86024 | tf_op jit(solution)/shard_map/ppermute | solution.py:603
  32.7 0.0 collective-permute-done.2.from_odd
  32.7 1.3 %collective-permute-done.3.from_even = f32[56,128]{1,0:T(8,128)S(1)} collective-permute-done((f32[56,128]{1,0:T(8,128)S(1)}, f32[56,128]{1,0:T(8,128)S(1)}, u32[]{:S(2)}, u32[]{:S(2)}) %collective-permute-start.3) | collective-permute-done | bytes 28704 | tf_op jit(solution)/shard_map/ppermute | solution.py:603
  34.0 3.1 %ocean.1 = (f32[32,128]{1,0:T(8,128)}, f32[384,128]{1,0:T(8,128)S(1)}) custom-call(f32[896,128]{1,0:T(8,128)S(1)} %get-tuple-element.23.tall, f32[56,128]{1,0:T(8,128)S(1)} %collective-permute-done.2.from_odd, f32[56,128]{1,0:T(8,128)S(1)} %collective-permute-done.3.from_even, f32[32,128]{1,0:T(8,128)S(1)} %get-tuple-element.26.row_labels, ...), custom_call_target="tpu_custom_call" | custom-call | tf_op jit(solution)/shard_map/ocean/pallas_call | solution.py:727
  37.1 13.9 %all_to_all.11 = f32[32,1,1536]{2,1,0:T(1,128)S(1)} all-to-all(f32[32,1,1536]{2,1,0:T(1,128)S(1)} %bitcast.12), channel_id=1, replica_groups=mesh['river'=4,'coast'=8] {'coast','river'}, dimensions={0} | all-to-all | bytes 393216 | tf_op jit(solution)/shard_map/all_to_all | solution.py:595
  51.0 1.3 %mouths.1 = f32[64,384]{1,0:T(8,128)} custom-call(f32[384,128]{1,0:T(8,128)S(1)} %bitcast.10, s32[16,128]{1,0:T(8,128)S(1)} %get-tuple-element.30.address), custom_call_target="tpu_custom_call" | custom-call | tf_op jit(solution)/shard_map/mouths/pallas_call | solution.py:744
Async XLA Ops:
  23.9 5.5 %collective-permute-start = (f32[120,128]{1,0:T(8,128)S(1)}, f32[120,128]{1,0:T(8,128)S(1)}, u32[]{:S(2)}, u32[]{:S(2)}) collective-permute-start(f32[120,128]{1,0:T(8,128)S(1)} %get-tuple-element.21), channel_id=1, source_target_pairs={{8,16},{16,8},{9,17},{17,9},{10,18},{18,10},{11,19},{19,11},{12,20... | collective-permute-start | bytes 184328 | tf_op jit(solution)/shard_map/ppermute | solution.py:603
  26.1 3.3 %collective-permute-start.1 = (f32[120,128]{1,0:T(8,128)S(1)}, f32[120,128]{1,0:T(8,128)S(1)}, u32[]{:S(2)}, u32[]{:S(2)}) collective-permute-start(f32[120,128]{1,0:T(8,128)S(1)} %get-tuple-element.22), channel_id=1, source_target_pairs={{0,8},{8,0},{16,24},{24,16},{1,9},{9,1},{17,25},{25,17},{2,10},{10... | collective-permute-start | bytes 184328 | tf_op jit(solution)/shard_map/ppermute | solution.py:603
  29.7 3.0 %collective-permute-start.2 = (f32[56,128]{1,0:T(8,128)S(1)}, f32[56,128]{1,0:T(8,128)S(1)}, u32[]{:S(2)}, u32[]{:S(2)}) collective-permute-start(f32[56,128]{1,0:T(8,128)S(1)} %get-tuple-element.24), channel_id=1, source_target_pairs={{1,2},{2,1},{3,4},{4,3},{5,6},{6,5},{9,10},{10,9},{11,12},{12,11},... | collective-permute-start | bytes 86024 | tf_op jit(solution)/shard_map/ppermute | solution.py:603
  30.4 3.6 %collective-permute-start.3 = (f32[56,128]{1,0:T(8,128)S(1)}, f32[56,128]{1,0:T(8,128)S(1)}, u32[]{:S(2)}, u32[]{:S(2)}) collective-permute-start(f32[56,128]{1,0:T(8,128)S(1)} %get-tuple-element.25), channel_id=1, source_target_pairs={{0,1},{1,0},{2,3},{3,2},{4,5},{5,4},{6,7},{7,6},{8,9},{9,8},{10,11... | collective-permute-start | bytes 86024 | tf_op jit(solution)/shard_map/ppermute | solution.py:603

commit v8 on v6

--- a/solution.py
+++ b/solution.py
@@ -26,7 +26,7 @@
 WIDE = 256
 PARTS = ((0, 8), (8, 2), (10, 2))
 LOOKED_UP = ((0, 8), (8, 4))
-CHUNK = 8
+CHUNK = 4
 HALO = 12
 FIELDS = 16
 f32, bf16, i32 = jnp.float32, jnp.bfloat16, jnp.int32
@@ -189,7 +189,7 @@
     inland = RB - MPB
     lane = lax.broadcasted_iota(i32, (blocks, RB), 1)
 
-    for copy in copies[7:]:
+    for copy in copies:
         copy.wait()
 
     turned[...] = jnp.zeros_like(turned)
@@ -212,8 +212,6 @@
     tile = grouped(mouths, 0).astype(i32)
     tiles[...] = tile % coasts * (devices // coasts) + tile // coasts
     series[STEPS * rows :] = grouped(mouths, MPB)
-    for copy in copies[:7]:
-        copy.wait()
 
     into = into_in[...]
     at_mouth = lane >= inland
@@ -573,22 +571,20 @@
     finished.wait()
 
 
-def column_kernel(address, _, hot, labels):
+def mouth_kernel(returned, address, level_out, whole, series, hot, block, departures):
+    rows = address.shape[0]
+    groups = LANES // MPB
     place = lax.broadcasted_iota(i32, (TALL, 2 * LANES), 0).astype(f32).astype(bf16)
 
     def place_of(label, part):
         return label - part == place
 
-    for i in range(0, address.shape[0], 2):
+    labels = []
+    for i in range(0, rows, 2):
         pair = jnp.concatenate([address[i : i + 1], address[i + 1 : i + 2]], axis=1)
         high, low = [label.astype(f32) for label in split_label(pair, WIDE)]
         one_hot_columns(low, place_of, hot, slice(i * LANES, (i + 2) * LANES))
-        labels[i // 2 : i // 2 + 1] = high
-
-
-def mouth_kernel(returned, hot, labels, level_out, whole, series, block, departures):
-    rows = hot.shape[1] // LANES
-    groups = LANES // MPB
+        labels.append(high)
     lane = lax.broadcasted_iota(i32, (rows, LANES), 1)
     copies = []
     for first, steps in LOOKED_UP:
@@ -602,7 +598,7 @@
         table = jnp.concatenate(in_two(own), axis=0)
         for i in range(0, rows, 2):
             lanes = slice(i * LANES, (i + 2) * LANES)
-            found = look_up(table, labels[i // 2 : i // 2 + 1], hot[:, lanes], steps)
+            found = look_up(table, labels[i // 2], hot[:, lanes], steps)
             series[pl.ds(first * rows + i, steps, stride=rows)] = found[:, :LANES]
             series[pl.ds(first * rows + i + 1, steps, stride=rows)] = found[:, LANES:]
         for number in range(first // groups, (first + steps) // groups):
@@ -780,18 +776,6 @@
     )(arrived, sea)
     from_even = with_neighbour(even, "river", 0)
 
-    slot_hot, slot_labels = pl.pallas_call(
-        column_kernel,
-        name="columns",
-        out_shape=(shape(WIDE, mouths, dtype=bf16), shape(rows // 2, 2 * LANES)),
-        in_specs=[
-            pl.BlockSpec(memory_space=pltpu.VMEM),
-            pl.BlockSpec(memory_space=pl.ANY),
-        ],
-        cost_estimate=cost(WIDE * mouths * LANES),
-        compiler_params=PARAMS,
-    )(address, labels)
-
     tall, odd, even = pl.pallas_call(
         strip_kernel,
         name="strips",
@@ -824,12 +808,13 @@
         scratch_shapes=[
             pltpu.VMEM((TALL * STEPS, WIDE), f32),
             pltpu.VMEM((STEPS * rows, LANES), f32),
+            pltpu.VMEM((WIDE, mouths), bf16),
             pltpu.VMEM((STEPS * MPB // LANES, blocks, LANES), f32),
             pltpu.SemaphoreType.DMA((STEPS * MPB // LANES,)),
         ],
         out_specs=pl.BlockSpec(memory_space=pltpu.HBM),
         compiler_params=PARAMS,
-    )(returned, slot_hot, slot_labels)
+    )(returned, address)
     return (depth_after, level_after, mouth_level)
 
 

time: 53.6 us -> 52.2 us (0.974)
  blocking collectives: 16.4 us -> 30.4 us
  waiting for transfers between devices: 11.9 us -> 2.8 us
  starting transfers between devices: 10.2 us -> 5.26 us
  Pallas kernels: 14.1 us -> 12.8 us
    all_to_all x1 -> x2, blocking collectives: 16.4 us -> 30.4 us  [swap(): lax.all_to_all(values, ('coast', 'river'), split_axis=0, concat_axis=0, t...]
    all_to_all x1 -> x0, waiting for transfers between devices: 9.05 us -> none  [swap(): lax.all_to_all(values, ('coast', 'river'), split_axis=0, concat_axis=0, t...]
    all_to_all x1 -> x0, starting transfers between devices: 4.92 us -> none  [swap(): lax.all_to_all(values, ('coast', 'river'), split_axis=0, concat_axis=0, t...]
    pallas_call x1, Pallas kernels: 3.8 us -> 3.11 us  [per_device(): pl.pallas_call(functools.partial(ocean_kernel, tile_rows), name='ocean',...]
  transfers between devices with their start and end apart: 5 -> 4, of which waited for: 3 -> 2; matrix products, arithmetic and copies ran while one was open for 0% -> 0% of each run, Pallas kernels for 3% -> 3%
where the time goes in v8:
time: 52.2 us; the launch traced here: 52 us
  blocking collectives  30.4 us (58%)
  Pallas kernels  12.8 us (25%)
  starting transfers between devices  5.26 us (10%)
  waiting for transfers between devices  2.8 us (5%)
  between operations  0.7 us (1%)
    all_to_all x2, blocking collectives, swap(): lax.all_to_all(values, ('coast', 'river'), split_axis=0, concat_axis=0, t...  30.4 us
    ppermute x4, starting transfers between devices, with_neighbour(): lax.ppermute(value, axis, [(i + k, i + 1 - k) for i in pairs for k in ran...  5.26 us
    pallas_call x1, Pallas kernels, per_device(): pl.pallas_call(functools.partial(river_kernel, devices, lax.axis_size('co...  5.24 us
    pallas_call x1, Pallas kernels, per_device(): pl.pallas_call(functools.partial(ocean_kernel, tile_rows), name='ocean',...  3.11 us
    ppermute x4, waiting for transfers between devices, with_neighbour(): lax.ppermute(value, axis, [(i + k, i + 1 - k) for i in pairs for k in ran...  2.8 us
    pallas_call x1, Pallas kernels, per_device(): pl.pallas_call(source_kernel, name='sources', out_shape=(shape(FIELDS * t...  1.69 us
    pallas_call x1, Pallas kernels, per_device(): pl.pallas_call(mouth_kernel, name='mouths', out_shape=shape(blocks, STEPS...  1.34 us
    pallas_call x1, Pallas kernels, per_device(): pl.pallas_call(edge_kernel, name='edges', out_shape=(shape(ROWS_SENT, LAN...  1.19 us
  transfers between devices with their start and end apart: 4, of which 2 were waited for; matrix products, arithmetic and copies ran while one was open for 0% of the time, Pallas kernels for 3%

profile of v8, /device:TPU:1, one launch (start us, length us, event | category | flops | bytes accessed | tf_op | source)
XLA Modules:
  0.0 52.0 jit_solution(5604747637261113979)
XLA Ops:
  0.6 5.2 %river.1 = (f32[64,128]{1,0:T(8,128)}, f32[416,128]{1,0:T(8,128)S(1)}, s32[16,128]{1,0:T(8,128)S(1)}, f32[128,128]{1,0:T(8,128)S(1)}) custom-call(f32[64,128]{1,0:T(8,128)} %refs_0_.1, f32[64,128]{1,0:T(8,128)} %refs_1_.1, f32[64,128]{1,0:T(8,128)} %refs_2_.1, f32[64,128]{1,0:T(8,128)} %refs_3_.1, f32[64,128]{1,0:T(8,128)} %refs_4_.1, f32[64,128]{1,0:T(8,128)} %refs_5_.1, ...), custom_call_target="tpu_custom_call" | custom-call | tf_op jit(solution)/shard_map/river/pallas_call | solution.py:673
  5.9 16.4 %all_to_all.10 = f32[32,1,1664]{2,1,0:T(1,128)S(1)} all-to-all(f32[32,1,1664]{2,1,0:T(1,128)S(1)} %bitcast.12), channel_id=1, replica_groups=mesh['river'=4,'coast'=8] {'coast','river'}, dimensions={0} | all-to-all | bytes 425984 | tf_op jit(solution)/shard_map/all_to_all | solution.py:636
  22.3 1.2 %edges.1 = (f32[120,128]{1,0:T(8,128)S(1)}, f32[128,128]{1,0:T(8,128)S(1)}) custom-call(f32[416,128]{1,0:T(8,128)S(1)} %bitcast.10, f32[128,128]{1,0:T(8,128)S(1)} %get-tuple-element.20.sea), custom_call_target="tpu_custom_call" | custom-call | flops 335544320 | bytes 8388608 | tf_op jit(solution)/shard_map/edges/pallas_call | solution.py:740
  23.5 2.2 %collective-permute-start = (f32[120,128]{1,0:T(8,128)S(1)}, f32[120,128]{1,0:T(8,128)S(1)}, u32[]{:S(2)}, u32[]{:S(2)}) collective-permute-start(f32[120,128]{1,0:T(8,128)S(1)} %get-tuple-element.23), channel_id=1, source_target_pairs={{8,16},{16,8},{9,17},{17,9},{10,18},{18,10},{11,19},{19,11},{12,20... | collective-permute-start | bytes 184328 | tf_op jit(solution)/shard_map/ppermute | solution.py:644
  25.7 1.7 %sources.1 = (f32[512,128]{1,0:T(8,128)S(1)}, f32[120,128]{1,0:T(8,128)S(1)}, bf16[256,4096]{1,0:T(8,128)(2,1)S(1)}, f32[32,128]{1,0:T(8,128)S(1)}) custom-call(f32[416,128]{1,0:T(8,128)S(1)} %bitcast.11, f32[128,128]{1,0:T(8,128)S(1)} %get-tuple-element.21.sea), custom_call_target="tpu_custom_call" | custom-call | flops 805306368 | bytes 8388608 | tf_op jit(solution)/shard_map/sources/pallas_call | solution.py:758
  27.4 0.1 collective-permute-start.1
  27.5 1.5 %collective-permute-done.from_odd = f32[120,128]{1,0:T(8,128)S(1)} collective-permute-done((f32[120,128]{1,0:T(8,128)S(1)}, f32[120,128]{1,0:T(8,128)S(1)}, u32[]{:S(2)}, u32[]{:S(2)}) %collective-permute-start) | collective-permute-done | bytes 61472 | tf_op jit(solution)/shard_map/ppermute | solution.py:644
  29.0 0.0 collective-permute-done.1.from_even
  29.0 0.3 strips.1
  29.3 0.7 %collective-permute-start.2 = (f32[56,128]{1,0:T(8,128)S(1)}, f32[56,128]{1,0:T(8,128)S(1)}, u32[]{:S(2)}, u32[]{:S(2)}) collective-permute-start(f32[56,128]{1,0:T(8,128)S(1)} %get-tuple-element.26), channel_id=1, source_target_pairs={{1,2},{2,1},{3,4},{4,3},{5,6},{6,5},{9,10},{10,9},{11,12},{12,11},... | collective-permute-start | bytes 86024 | tf_op jit(solution)/shard_map/ppermute | solution.py:644
  30.0 2.3 %collective-permute-start.3 = (f32[56,128]{1,0:T(8,128)S(1)}, f32[56,128]{1,0:T(8,128)S(1)}, u32[]{:S(2)}, u32[]{:S(2)}) collective-permute-start(f32[56,128]{1,0:T(8,128)S(1)} %get-tuple-element.27), channel_id=1, source_target_pairs={{0,1},{1,0},{2,3},{3,2},{4,5},{5,4},{6,7},{7,6},{8,9},{9,8},{10,11... | collective-permute-start | bytes 86024 | tf_op jit(solution)/shard_map/ppermute | solution.py:644
  32.3 0.0 collective-permute-done.2.from_odd
  32.3 1.3 %collective-permute-done.3.from_even = f32[56,128]{1,0:T(8,128)S(1)} collective-permute-done((f32[56,128]{1,0:T(8,128)S(1)}, f32[56,128]{1,0:T(8,128)S(1)}, u32[]{:S(2)}, u32[]{:S(2)}) %collective-permute-start.3) | collective-permute-done | bytes 28704 | tf_op jit(solution)/shard_map/ppermute | solution.py:644
  33.5 3.1 %ocean.1 = (f32[32,128]{1,0:T(8,128)}, f32[384,128]{1,0:T(8,128)S(1)}) custom-call(f32[896,128]{1,0:T(8,128)S(1)} %get-tuple-element.25.tall, f32[56,128]{1,0:T(8,128)S(1)} %collective-permute-done.2.from_odd, f32[56,128]{1,0:T(8,128)S(1)} %collective-permute-done.3.from_even, f32[32,128]{1,0:T(8,128)S(1)} %get-tuple-element.28.row_labels, ...), custom_call_target="tpu_custom_call" | custom-call | tf_op jit(solution)/shard_map/ocean/pallas_call | solution.py:787
  36.7 14.0 %all_to_all.11 = f32[32,1,1536]{2,1,0:T(1,128)S(1)} all-to-all(f32[32,1,1536]{2,1,0:T(1,128)S(1)} %bitcast.13), channel_id=1, replica_groups=mesh['river'=4,'coast'=8] {'coast','river'}, dimensions={0} | all-to-all | bytes 393216 | tf_op jit(solution)/shard_map/all_to_all | solution.py:636
  50.6 1.3 %mouths.1 = f32[64,384]{1,0:T(8,128)} custom-call(f32[384,128]{1,0:T(8,128)S(1)} %bitcast.9, s32[16,128]{1,0:T(8,128)S(1)} %get-tuple-element.32.address), custom_call_target="tpu_custom_call" | custom-call | tf_op jit(solution)/shard_map/mouths/pallas_call | solution.py:804
Async XLA Ops:
  23.5 5.5 %collective-permute-start = (f32[120,128]{1,0:T(8,128)S(1)}, f32[120,128]{1,0:T(8,128)S(1)}, u32[]{:S(2)}, u32[]{:S(2)}) collective-permute-start(f32[120,128]{1,0:T(8,128)S(1)} %get-tuple-element.23), channel_id=1, source_target_pairs={{8,16},{16,8},{9,17},{17,9},{10,18},{18,10},{11,19},{19,11},{12,20... | collective-permute-start | bytes 184328 | tf_op jit(solution)/shard_map/ppermute | solution.py:644
  27.4 1.6 %collective-permute-start.1 = (f32[120,128]{1,0:T(8,128)S(1)}, f32[120,128]{1,0:T(8,128)S(1)}, u32[]{:S(2)}, u32[]{:S(2)}) collective-permute-start(f32[120,128]{1,0:T(8,128)S(1)} %get-tuple-element.24), channel_id=1, source_target_pairs={{0,8},{8,0},{16,24},{24,16},{1,9},{9,1},{17,25},{25,17},{2,10},{10... | collective-permute-start | bytes 184328 | tf_op jit(solution)/shard_map/ppermute | solution.py:644
  29.3 3.0 %collective-permute-start.2 = (f32[56,128]{1,0:T(8,128)S(1)}, f32[56,128]{1,0:T(8,128)S(1)}, u32[]{:S(2)}, u32[]{:S(2)}) collective-permute-start(f32[56,128]{1,0:T(8,128)S(1)} %get-tuple-element.26), channel_id=1, source_target_pairs={{1,2},{2,1},{3,4},{4,3},{5,6},{6,5},{9,10},{10,9},{11,12},{12,11},... | collective-permute-start | bytes 86024 | tf_op jit(solution)/shard_map/ppermute | solution.py:644
  30.0 3.6 %collective-permute-start.3 = (f32[56,128]{1,0:T(8,128)S(1)}, f32[56,128]{1,0:T(8,128)S(1)}, u32[]{:S(2)}, u32[]{:S(2)}) collective-permute-start(f32[56,128]{1,0:T(8,128)S(1)} %get-tuple-element.27), channel_id=1, source_target_pairs={{0,1},{1,0},{2,3},{3,2},{4,5},{5,4},{6,7},{7,6},{8,9},{9,8},{10,11... | collective-permute-start | bytes 86024 | tf_op jit(solution)/shard_map/ppermute | solution.py:644

commit v9 on v8

--- a/solution.py
+++ b/solution.py
@@ -26,7 +26,7 @@
 WIDE = 256
 PARTS = ((0, 8), (8, 2), (10, 2))
 LOOKED_UP = ((0, 8), (8, 4))
-CHUNK = 4
+CHUNK = 8
 HALO = 12
 FIELDS = 16
 f32, bf16, i32 = jnp.float32, jnp.bfloat16, jnp.int32

time: 52.2 us -> 52.2 us (level)
  no operation moved by 1% of the time
where the time goes in v9:
time: 52.2 us; the launch traced here: 51.9 us
  blocking collectives  30.3 us (58%)
  Pallas kernels  12.8 us (25%)
  starting transfers between devices  5.27 us (10%)
  waiting for transfers between devices  2.86 us (5%)
  between operations  0.7 us (1%)
    all_to_all x2, blocking collectives, swap(): lax.all_to_all(values, ('coast', 'river'), split_axis=0, concat_axis=0, t...  30.3 us
    ppermute x4, starting transfers between devices, with_neighbour(): lax.ppermute(value, axis, [(i + k, i + 1 - k) for i in pairs for k in ran...  5.27 us
    pallas_call x1, Pallas kernels, per_device(): pl.pallas_call(functools.partial(river_kernel, devices, lax.axis_size('co...  5.24 us
    pallas_call x1, Pallas kernels, per_device(): pl.pallas_call(functools.partial(ocean_kernel, tile_rows), name='ocean',...  3.11 us
    ppermute x4, waiting for transfers between devices, with_neighbour(): lax.ppermute(value, axis, [(i + k, i + 1 - k) for i in pairs for k in ran...  2.86 us
    pallas_call x1, Pallas kernels, per_device(): pl.pallas_call(source_kernel, name='sources', out_shape=(shape(FIELDS * t...  1.63 us
    pallas_call x1, Pallas kernels, per_device(): pl.pallas_call(mouth_kernel, name='mouths', out_shape=shape(blocks, STEPS...  1.36 us
    pallas_call x1, Pallas kernels, per_device(): pl.pallas_call(edge_kernel, name='edges', out_shape=(shape(ROWS_SENT, LAN...  1.16 us
  transfers between devices with their start and end apart: 4, of which 2 were waited for; matrix products, arithmetic and copies ran while one was open for 0% of the time, Pallas kernels for 3%

profile of v9, /device:TPU:1, one launch (start us, length us, event | category | flops | bytes accessed | tf_op | source)
XLA Modules:
  0.0 51.9 jit_solution(163920653476119634)
XLA Ops:
  0.6 5.2 %river.1 = (f32[64,128]{1,0:T(8,128)}, f32[416,128]{1,0:T(8,128)S(1)}, s32[16,128]{1,0:T(8,128)S(1)}, f32[128,128]{1,0:T(8,128)S(1)}) custom-call(f32[64,128]{1,0:T(8,128)} %refs_0_.1, f32[64,128]{1,0:T(8,128)} %refs_1_.1, f32[64,128]{1,0:T(8,128)} %refs_2_.1, f32[64,128]{1,0:T(8,128)} %refs_3_.1, f32[64,128]{1,0:T(8,128)} %refs_4_.1, f32[64,128]{1,0:T(8,128)} %refs_5_.1, ...), custom_call_target="tpu_custom_call" | custom-call | tf_op jit(solution)/shard_map/river/pallas_call | solution.py:673
  5.9 16.4 %all_to_all.10 = f32[32,1,1664]{2,1,0:T(1,128)S(1)} all-to-all(f32[32,1,1664]{2,1,0:T(1,128)S(1)} %bitcast.12), channel_id=1, replica_groups=mesh['river'=4,'coast'=8] {'coast','river'}, dimensions={0} | all-to-all | bytes 425984 | tf_op jit(solution)/shard_map/all_to_all | solution.py:636
  22.3 1.2 %edges.1 = (f32[120,128]{1,0:T(8,128)S(1)}, f32[128,128]{1,0:T(8,128)S(1)}) custom-call(f32[416,128]{1,0:T(8,128)S(1)} %bitcast.10, f32[128,128]{1,0:T(8,128)S(1)} %get-tuple-element.20.sea), custom_call_target="tpu_custom_call" | custom-call | flops 335544320 | bytes 8388608 | tf_op jit(solution)/shard_map/edges/pallas_call | solution.py:740
  23.4 2.2 %collective-permute-start = (f32[120,128]{1,0:T(8,128)S(1)}, f32[120,128]{1,0:T(8,128)S(1)}, u32[]{:S(2)}, u32[]{:S(2)}) collective-permute-start(f32[120,128]{1,0:T(8,128)S(1)} %get-tuple-element.23), channel_id=1, source_target_pairs={{8,16},{16,8},{9,17},{17,9},{10,18},{18,10},{11,19},{19,11},{12,20... | collective-permute-start | bytes 184328 | tf_op jit(solution)/shard_map/ppermute | solution.py:644
  25.7 1.6 %sources.1 = (f32[512,128]{1,0:T(8,128)S(1)}, f32[120,128]{1,0:T(8,128)S(1)}, bf16[256,4096]{1,0:T(8,128)(2,1)S(1)}, f32[32,128]{1,0:T(8,128)S(1)}) custom-call(f32[416,128]{1,0:T(8,128)S(1)} %bitcast.11, f32[128,128]{1,0:T(8,128)S(1)} %get-tuple-element.21.sea), custom_call_target="tpu_custom_call" | custom-call | flops 805306368 | bytes 8388608 | tf_op jit(solution)/shard_map/sources/pallas_call | solution.py:758
  27.3 0.1 collective-permute-start.1
  27.4 1.6 %collective-permute-done.from_odd = f32[120,128]{1,0:T(8,128)S(1)} collective-permute-done((f32[120,128]{1,0:T(8,128)S(1)}, f32[120,128]{1,0:T(8,128)S(1)}, u32[]{:S(2)}, u32[]{:S(2)}) %collective-permute-start) | collective-permute-done | bytes 61472 | tf_op jit(solution)/shard_map/ppermute | solution.py:644
  29.0 0.0 collective-permute-done.1.from_even
  29.0 0.3 strips.1
  29.3 0.7 %collective-permute-start.2 = (f32[56,128]{1,0:T(8,128)S(1)}, f32[56,128]{1,0:T(8,128)S(1)}, u32[]{:S(2)}, u32[]{:S(2)}) collective-permute-start(f32[56,128]{1,0:T(8,128)S(1)} %get-tuple-element.26), channel_id=1, source_target_pairs={{1,2},{2,1},{3,4},{4,3},{5,6},{6,5},{9,10},{10,9},{11,12},{12,11},... | collective-permute-start | bytes 86024 | tf_op jit(solution)/shard_map/ppermute | solution.py:644
  29.9 2.3 %collective-permute-start.3 = (f32[56,128]{1,0:T(8,128)S(1)}, f32[56,128]{1,0:T(8,128)S(1)}, u32[]{:S(2)}, u32[]{:S(2)}) collective-permute-start(f32[56,128]{1,0:T(8,128)S(1)} %get-tuple-element.27), channel_id=1, source_target_pairs={{0,1},{1,0},{2,3},{3,2},{4,5},{5,4},{6,7},{7,6},{8,9},{9,8},{10,11... | collective-permute-start | bytes 86024 | tf_op jit(solution)/shard_map/ppermute | solution.py:644
  32.3 0.0 collective-permute-done.2.from_odd
  32.3 1.3 %collective-permute-done.3.from_even = f32[56,128]{1,0:T(8,128)S(1)} collective-permute-done((f32[56,128]{1,0:T(8,128)S(1)}, f32[56,128]{1,0:T(8,128)S(1)}, u32[]{:S(2)}, u32[]{:S(2)}) %collective-permute-start.3) | collective-permute-done | bytes 28704 | tf_op jit(solution)/shard_map/ppermute | solution.py:644
  33.5 3.1 %ocean.1 = (f32[32,128]{1,0:T(8,128)}, f32[384,128]{1,0:T(8,128)S(1)}) custom-call(f32[896,128]{1,0:T(8,128)S(1)} %get-tuple-element.25.tall, f32[56,128]{1,0:T(8,128)S(1)} %collective-permute-done.2.from_odd, f32[56,128]{1,0:T(8,128)S(1)} %collective-permute-done.3.from_even, f32[32,128]{1,0:T(8,128)S(1)} %get-tuple-element.28.row_labels, ...), custom_call_target="tpu_custom_call" | custom-call | tf_op jit(solution)/shard_map/ocean/pallas_call | solution.py:787
  36.6 13.9 %all_to_all.11 = f32[32,1,1536]{2,1,0:T(1,128)S(1)} all-to-all(f32[32,1,1536]{2,1,0:T(1,128)S(1)} %bitcast.13), channel_id=1, replica_groups=mesh['river'=4,'coast'=8] {'coast','river'}, dimensions={0} | all-to-all | bytes 393216 | tf_op jit(solution)/shard_map/all_to_all | solution.py:636
  50.6 1.4 %mouths.1 = f32[64,384]{1,0:T(8,128)} custom-call(f32[384,128]{1,0:T(8,128)S(1)} %bitcast.9, s32[16,128]{1,0:T(8,128)S(1)} %get-tuple-element.32.address), custom_call_target="tpu_custom_call" | custom-call | tf_op jit(solution)/shard_map/mouths/pallas_call | solution.py:804
Async XLA Ops:
  23.4 5.5 %collective-permute-start = (f32[120,128]{1,0:T(8,128)S(1)}, f32[120,128]{1,0:T(8,128)S(1)}, u32[]{:S(2)}, u32[]{:S(2)}) collective-permute-start(f32[120,128]{1,0:T(8,128)S(1)} %get-tuple-element.23), channel_id=1, source_target_pairs={{8,16},{16,8},{9,17},{17,9},{10,18},{18,10},{11,19},{19,11},{12,20... | collective-permute-start | bytes 184328 | tf_op jit(solution)/shard_map/ppermute | solution.py:644
  27.3 1.7 %collective-permute-start.1 = (f32[120,128]{1,0:T(8,128)S(1)}, f32[120,128]{1,0:T(8,128)S(1)}, u32[]{:S(2)}, u32[]{:S(2)}) collective-permute-start(f32[120,128]{1,0:T(8,128)S(1)} %get-tuple-element.24), channel_id=1, source_target_pairs={{0,8},{8,0},{16,24},{24,16},{1,9},{9,1},{17,25},{25,17},{2,10},{10... | collective-permute-start | bytes 184328 | tf_op jit(solution)/shard_map/ppermute | solution.py:644
  29.3 3.0 %collective-permute-start.2 = (f32[56,128]{1,0:T(8,128)S(1)}, f32[56,128]{1,0:T(8,128)S(1)}, u32[]{:S(2)}, u32[]{:S(2)}) collective-permute-start(f32[56,128]{1,0:T(8,128)S(1)} %get-tuple-element.26), channel_id=1, source_target_pairs={{1,2},{2,1},{3,4},{4,3},{5,6},{6,5},{9,10},{10,9},{11,12},{12,11},... | collective-permute-start | bytes 86024 | tf_op jit(solution)/shard_map/ppermute | solution.py:644
  29.9 3.6 %collective-permute-start.3 = (f32[56,128]{1,0:T(8,128)S(1)}, f32[56,128]{1,0:T(8,128)S(1)}, u32[]{:S(2)}, u32[]{:S(2)}) collective-permute-start(f32[56,128]{1,0:T(8,128)S(1)} %get-tuple-element.27), channel_id=1, source_target_pairs={{0,1},{1,0},{2,3},{3,2},{4,5},{5,4},{6,7},{7,6},{8,9},{9,8},{10,11... | collective-permute-start | bytes 86024 | tf_op jit(solution)/shard_map/ppermute | solution.py:644

commit v10 on v8

--- a/solution.py
+++ b/solution.py
@@ -136,9 +136,7 @@
     for copy in copies[::-1] + of_sea:
         copy.start()
     outputs = (depth_out, send_out, address_out)
-    finished = river_steps(
-        devices, coasts, capacity, copies, *refs[:10], *outputs, arrivals, *refs[16:]
-    )
+    river_steps(devices, coasts, capacity, copies, *refs[:10], *outputs, *refs[16:])
 
     sea_level, sea_bed, wet_mask, flux_east, flux_north = refs[10:15]
     tile_rows = sea_level.shape[0]
@@ -148,7 +146,6 @@
     level = jnp.where(wet_mask[...] == 1, jnp.maximum(sea_level[...], bed), bed)
     for number, value in enumerate((level, bed, flux_east[...], flux_north[...])):
         sea_out[number * tile_rows : (number + 1) * tile_rows] = value
-    finished.wait()
 
 
 def river_steps(
@@ -169,8 +166,6 @@
     depth_out,
     send_out,
     address_out,
-    arrivals,
-    depth_end,
     enters,
     series,
     turned,
@@ -339,13 +334,10 @@
         depth, flow, below = river_turn(substep, depth, flow, below)
         for work in beside.get(substep, []):
             work()
-    depth_end[...] = depth
-    finished = pltpu.make_async_copy(depth_end, depth_out, arrivals.at[15])
-    finished.start()
+    depth_out[...] = depth
     for group in range(4):
         place_series(2, group)
     pack(2)
-    return finished
 
 
 def reach_of(field):
@@ -427,8 +419,10 @@
         put(STEPS + number, value, value)
 
 
-def source_kernel(arrived, sea, fields, even, rhs, label_out, *refs):
-    owner, places, column_labels, lhs, sums = refs
+def source_kernel(arrived, sea, depth, fields, even, rhs, label_out, depth_out, *refs):
+    owner, places, column_labels, lhs, sums, departure = refs
+    finished = pltpu.make_async_copy(depth, depth_out, departure)
+    finished.start()
     first_of_pair = lax.axis_index("river") % 2 == 0
     groups = arrived.shape[0] // SENT
     tile_rows, tile_cols = sea.shape[0] // 4, sea.shape[1]
@@ -457,6 +451,7 @@
         put(step, jnp.concatenate(halves, axis=0))
     for number in range(4):
         put(STEPS + number, sea[number * tile_rows : (number + 1) * tile_rows])
+    finished.wait()
 
 
 def strip_kernel(fields, from_odd, from_even, tall, odd, even):
@@ -670,7 +665,7 @@
     rows = mouths // LANES
     height = tile_rows + 2 * HALO
 
-    depth_after, sending, address, sea = pl.pallas_call(
+    depth, sending, address, sea = pl.pallas_call(
         functools.partial(river_kernel, devices, lax.axis_size("coast"), capacity),
         name="river",
         out_shape=(
@@ -680,12 +675,6 @@
             shape(4 * tile_rows, tile_cols),
         ),
         in_specs=[pl.BlockSpec(memory_space=pltpu.HBM)] * 15,
-        out_specs=(
-            pl.BlockSpec(memory_space=pltpu.HBM),
-            pl.BlockSpec(memory_space=pltpu.VMEM),
-            pl.BlockSpec(memory_space=pltpu.VMEM),
-            pl.BlockSpec(memory_space=pltpu.VMEM),
-        ),
         scratch_shapes=[pltpu.VMEM((blocks, RB), f32)] * 6
         + [
             pltpu.VMEM((blocks, RB), i32),
@@ -697,8 +686,7 @@
             pltpu.VMEM((tile_rows, tile_cols), i32),
             pltpu.VMEM((tile_rows, tile_cols), f32),
             pltpu.VMEM((tile_rows, tile_cols), f32),
-            pltpu.SemaphoreType.DMA((16,)),
-            pltpu.VMEM((blocks, RB), f32),
+            pltpu.SemaphoreType.DMA((15,)),
             pltpu.VMEM((reach_offsets, blocks, RB), f32),
             pltpu.VMEM((SENT * rows, LANES), f32),
             pltpu.VMEM((RB, LANES), f32),
@@ -755,7 +743,7 @@
     )(arrived, sea)
     from_odd = with_neighbour(odd, "river", 1)
 
-    fields, even, hot, labels = pl.pallas_call(
+    fields, even, hot, labels, depth_after = pl.pallas_call(
         source_kernel,
         name="sources",
         out_shape=(
@@ -763,17 +751,21 @@
             shape(ROWS_SENT, LANES),
             shape(WIDE, groups * LANES, dtype=bf16),
             shape(groups, LANES),
+            shape(blocks, RB),
         ),
+        out_specs=(pl.BlockSpec(memory_space=pltpu.VMEM),) * 4
+        + (pl.BlockSpec(memory_space=pltpu.HBM),),
         scratch_shapes=[
             pltpu.VMEM((TALL * STEPS, LANES), bf16),
             pltpu.VMEM((WIDE, LANES), bf16),
             pltpu.VMEM((groups, LANES), f32),
             pltpu.VMEM((2 * TALL * STEPS, groups * LANES), bf16),
             pltpu.VMEM((2 * TALL * STEPS, LANES), f32),
+            pltpu.SemaphoreType.DMA,
         ],
         cost_estimate=cost(2 * TALL * STEPS * WIDE * groups * LANES),
         compiler_params=PARAMS,
-    )(arrived, sea)
+    )(arrived, sea, depth)
     from_even = with_neighbour(even, "river", 0)
 
     tall, odd, even = pl.pallas_call(

time: 52.2 us -> 51.8 us (level)
  no operation moved by 1% of the time
where the time goes in v10:
time: 51.8 us; the launch traced here: 51.5 us
  blocking collectives  30.4 us (59%)
  Pallas kernels  12.4 us (24%)
  starting transfers between devices  5.27 us (10%)
  waiting for transfers between devices  2.78 us (5%)
  between operations  0.7 us (1%)
    all_to_all x2, blocking collectives, swap(): lax.all_to_all(values, ('coast', 'river'), split_axis=0, concat_axis=0, t...  30.4 us
    ppermute x4, starting transfers between devices, with_neighbour(): lax.ppermute(value, axis, [(i + k, i + 1 - k) for i in pairs for k in ran...  5.27 us
    pallas_call x1, Pallas kernels, per_device(): pl.pallas_call(functools.partial(river_kernel, devices, lax.axis_size('co...  4.77 us
    pallas_call x1, Pallas kernels, per_device(): pl.pallas_call(functools.partial(ocean_kernel, tile_rows), name='ocean',...  3.11 us
    ppermute x4, waiting for transfers between devices, with_neighbour(): lax.ppermute(value, axis, [(i + k, i + 1 - k) for i in pairs for k in ran...  2.78 us
    pallas_call x1, Pallas kernels, per_device(): pl.pallas_call(source_kernel, name='sources', out_shape=(shape(FIELDS * t...  1.71 us
    pallas_call x1, Pallas kernels, per_device(): pl.pallas_call(mouth_kernel, name='mouths', out_shape=shape(blocks, STEPS...  1.34 us
    pallas_call x1, Pallas kernels, per_device(): pl.pallas_call(edge_kernel, name='edges', out_shape=(shape(ROWS_SENT, LAN...  1.19 us
  transfers between devices with their start and end apart: 4, of which 2 were waited for; matrix products, arithmetic and copies ran while one was open for 0% of the time, Pallas kernels for 3%

profile of v10, /device:TPU:1, one launch (start us, length us, event | category | flops | bytes accessed | tf_op | source)
XLA Modules:
  0.0 51.5 jit_solution(5792026176946424365)
XLA Ops:
  0.6 4.8 %river.1 = (f32[64,128]{1,0:T(8,128)S(1)}, f32[416,128]{1,0:T(8,128)S(1)}, s32[16,128]{1,0:T(8,128)S(1)}, f32[128,128]{1,0:T(8,128)S(1)}) custom-call(f32[64,128]{1,0:T(8,128)} %refs_0_.1, f32[64,128]{1,0:T(8,128)} %refs_1_.1, f32[64,128]{1,0:T(8,128)} %refs_2_.1, f32[64,128]{1,0:T(8,128)} %refs_3_.1, f32[64,128]{1,0:T(8,128)} %refs_4_.1, ...), custom_call_target="tpu_custom_call" | custom-call | tf_op jit(solution)/shard_map/river/pallas_call | solution.py:668
  5.4 16.4 %all_to_all.10 = f32[32,1,1664]{2,1,0:T(1,128)S(1)} all-to-all(f32[32,1,1664]{2,1,0:T(1,128)S(1)} %bitcast.12), channel_id=1, replica_groups=mesh['river'=4,'coast'=8] {'coast','river'}, dimensions={0} | all-to-all | bytes 425984 | tf_op jit(solution)/shard_map/all_to_all | solution.py:631
  21.8 1.2 %edges.1 = (f32[120,128]{1,0:T(8,128)S(1)}, f32[128,128]{1,0:T(8,128)S(1)}) custom-call(f32[416,128]{1,0:T(8,128)S(1)} %bitcast.10, f32[128,128]{1,0:T(8,128)S(1)} %get-tuple-element.20.sea), custom_call_target="tpu_custom_call" | custom-call | flops 335544320 | bytes 8388608 | tf_op jit(solution)/shard_map/edges/pallas_call | solution.py:728
  23.0 2.2 %collective-permute-start = (f32[120,128]{1,0:T(8,128)S(1)}, f32[120,128]{1,0:T(8,128)S(1)}, u32[]{:S(2)}, u32[]{:S(2)}) collective-permute-start(f32[120,128]{1,0:T(8,128)S(1)} %get-tuple-element.25), channel_id=1, source_target_pairs={{8,16},{16,8},{9,17},{17,9},{10,18},{18,10},{11,19},{19,11},{12,20... | collective-permute-start | bytes 184328 | tf_op jit(solution)/shard_map/ppermute | solution.py:639
  25.2 1.7 %sources.1 = (f32[512,128]{1,0:T(8,128)S(1)}, f32[120,128]{1,0:T(8,128)S(1)}, bf16[256,4096]{1,0:T(8,128)(2,1)S(1)}, f32[32,128]{1,0:T(8,128)S(1)}, f32[64,128]{1,0:T(8,128)}) custom-call(f32[416,128]{1,0:T(8,128)S(1)} %bitcast.11, f32[128,128]{1,0:T(8,128)S(1)} %get-tuple-element.21.sea, f32[64,128]{1,0:T(8,128)S(1)} %get-tuple-element.22.depth), custom_call_target="tpu_custom_call" | custom-call | flops 805306368 | bytes 8388608 | tf_op jit(solution)/shard_map/sources/pallas_call | solution.py:746
  26.9 0.1 collective-permute-start.1
  27.0 1.5 %collective-permute-done.from_odd = f32[120,128]{1,0:T(8,128)S(1)} collective-permute-done((f32[120,128]{1,0:T(8,128)S(1)}, f32[120,128]{1,0:T(8,128)S(1)}, u32[]{:S(2)}, u32[]{:S(2)}) %collective-permute-start) | collective-permute-done | bytes 61472 | tf_op jit(solution)/shard_map/ppermute | solution.py:639
  28.5 0.0 collective-permute-done.1.from_even
  28.5 0.3 strips.1
  28.8 0.7 %collective-permute-start.2 = (f32[56,128]{1,0:T(8,128)S(1)}, f32[56,128]{1,0:T(8,128)S(1)}, u32[]{:S(2)}, u32[]{:S(2)}) collective-permute-start(f32[56,128]{1,0:T(8,128)S(1)} %get-tuple-element.28), channel_id=1, source_target_pairs={{1,2},{2,1},{3,4},{4,3},{5,6},{6,5},{9,10},{10,9},{11,12},{12,11},... | collective-permute-start | bytes 86024 | tf_op jit(solution)/shard_map/ppermute | solution.py:639
  29.5 2.3 %collective-permute-start.3 = (f32[56,128]{1,0:T(8,128)S(1)}, f32[56,128]{1,0:T(8,128)S(1)}, u32[]{:S(2)}, u32[]{:S(2)}) collective-permute-start(f32[56,128]{1,0:T(8,128)S(1)} %get-tuple-element.29), channel_id=1, source_target_pairs={{0,1},{1,0},{2,3},{3,2},{4,5},{5,4},{6,7},{7,6},{8,9},{9,8},{10,11... | collective-permute-start | bytes 86024 | tf_op jit(solution)/shard_map/ppermute | solution.py:639
  31.8 0.0 collective-permute-done.2.from_odd
  31.8 1.3 %collective-permute-done.3.from_even = f32[56,128]{1,0:T(8,128)S(1)} collective-permute-done((f32[56,128]{1,0:T(8,128)S(1)}, f32[56,128]{1,0:T(8,128)S(1)}, u32[]{:S(2)}, u32[]{:S(2)}) %collective-permute-start.3) | collective-permute-done | bytes 28704 | tf_op jit(solution)/shard_map/ppermute | solution.py:639
  33.1 3.1 %ocean.1 = (f32[32,128]{1,0:T(8,128)}, f32[384,128]{1,0:T(8,128)S(1)}) custom-call(f32[896,128]{1,0:T(8,128)S(1)} %get-tuple-element.27.tall, f32[56,128]{1,0:T(8,128)S(1)} %collective-permute-done.2.from_odd, f32[56,128]{1,0:T(8,128)S(1)} %collective-permute-done.3.from_even, f32[32,128]{1,0:T(8,128)S(1)} %get-tuple-element.30.row_labels, ...), custom_call_target="tpu_custom_call" | custom-call | tf_op jit(solution)/shard_map/ocean/pallas_call | solution.py:779
  36.2 14.0 %all_to_all.11 = f32[32,1,1536]{2,1,0:T(1,128)S(1)} all-to-all(f32[32,1,1536]{2,1,0:T(1,128)S(1)} %bitcast.13), channel_id=1, replica_groups=mesh['river'=4,'coast'=8] {'coast','river'}, dimensions={0} | all-to-all | bytes 393216 | tf_op jit(solution)/shard_map/all_to_all | solution.py:631
  50.2 1.3 %mouths.1 = f32[64,384]{1,0:T(8,128)} custom-call(f32[384,128]{1,0:T(8,128)S(1)} %bitcast.9, s32[16,128]{1,0:T(8,128)S(1)} %get-tuple-element.34.address), custom_call_target="tpu_custom_call" | custom-call | tf_op jit(solution)/shard_map/mouths/pallas_call | solution.py:796
Async XLA Ops:
  23.0 5.5 %collective-permute-start = (f32[120,128]{1,0:T(8,128)S(1)}, f32[120,128]{1,0:T(8,128)S(1)}, u32[]{:S(2)}, u32[]{:S(2)}) collective-permute-start(f32[120,128]{1,0:T(8,128)S(1)} %get-tuple-element.25), channel_id=1, source_target_pairs={{8,16},{16,8},{9,17},{17,9},{10,18},{18,10},{11,19},{19,11},{12,20... | collective-permute-start | bytes 184328 | tf_op jit(solution)/shard_map/ppermute | solution.py:639
  26.9 1.6 %collective-permute-start.1 = (f32[120,128]{1,0:T(8,128)S(1)}, f32[120,128]{1,0:T(8,128)S(1)}, u32[]{:S(2)}, u32[]{:S(2)}) collective-permute-start(f32[120,128]{1,0:T(8,128)S(1)} %get-tuple-element.26), channel_id=1, source_target_pairs={{0,8},{8,0},{16,24},{24,16},{1,9},{9,1},{17,25},{25,17},{2,10},{10... | collective-permute-start | bytes 184328 | tf_op jit(solution)/shard_map/ppermute | solution.py:639
  28.8 3.0 %collective-permute-start.2 = (f32[56,128]{1,0:T(8,128)S(1)}, f32[56,128]{1,0:T(8,128)S(1)}, u32[]{:S(2)}, u32[]{:S(2)}) collective-permute-start(f32[56,128]{1,0:T(8,128)S(1)} %get-tuple-element.28), channel_id=1, source_target_pairs={{1,2},{2,1},{3,4},{4,3},{5,6},{6,5},{9,10},{10,9},{11,12},{12,11},... | collective-permute-start | bytes 86024 | tf_op jit(solution)/shard_map/ppermute | solution.py:639
  29.5 3.6 %collective-permute-start.3 = (f32[56,128]{1,0:T(8,128)S(1)}, f32[56,128]{1,0:T(8,128)S(1)}, u32[]{:S(2)}, u32[]{:S(2)}) collective-permute-start(f32[56,128]{1,0:T(8,128)S(1)} %get-tuple-element.29), channel_id=1, source_target_pairs={{0,1},{1,0},{2,3},{3,2},{4,5},{5,4},{6,7},{7,6},{8,9},{9,8},{10,11... | collective-permute-start | bytes 86024 | tf_op jit(solution)/shard_map/ppermute | solution.py:639
